TPU v7x, 32 devices: a whole 2x2x4 slice. The times are simulated.
32 devices in a mesh: wide: 16 (over z, y, x), narrow: 2 (over core).
Axes of the slice: x: 2, y: 2, z: 4, core: 2. Of those that a mesh axis runs over, the one named last changes fastest.
Arguments:
- primal_in: bfloat16 [32, 8192], P('wide', 'narrow'), may hold values from -6 to 6
- tangent_in: bfloat16 [32, 8192], P('wide', 'narrow'), may hold values from -6 to 6
- cotangent: bfloat16 [32, 8192], P('wide', 'narrow'), may hold values from -6 to 6
- gate_weight: bfloat16 [8192, 2048], P('narrow', 'wide'), may hold values from -0.0625 to 0.0625
- up_weight: bfloat16 [8192, 2048], P('narrow', 'wide'), may hold values from -0.0625 to 0.0625
- down_weight: bfloat16 [2048, 8192], P('wide', 'narrow'), may hold values from -0.125 to 0.125
Outputs:
- input_hvp: bfloat16 [32, 8192], P('wide', 'narrow')
- gate_grad_tangent: float32 [8192, 2048], P('narrow', 'wide')
- up_grad_tangent: float32 [8192, 2048], P('narrow', 'wide')
- down_grad_tangent: float32 [2048, 8192], P('wide', 'narrow')
All inputs are finite; a program needn't handle non-finite values.
Results may differ from a plain program's by a relative error of at most 0.0049.
Values may be sent and summed in bfloat16 or wider, within the bound.
No kernel may reach another device: no remote copies, remote signals or barrier semaphores. Data moves between devices by JAX's collectives and lax.ppermute only.
A program may use at most 64 MiB of HBM per device.

v0:
```python
import jax
import jax.numpy as jnp
from jax import lax
from jax.sharding import PartitionSpec as P


def contract_first(left, right):
    return lax.dot_general(
        left, right, (((0,), (0,)), ((), ())), preferred_element_type=jnp.float32
    )


def contract_last(left, right):
    return lax.dot_general(
        left, right, (((1,), (1,)), ((), ())), preferred_element_type=jnp.float32
    )


def factors(gate, up, tgate, tup, dact):
    sig = jax.nn.sigmoid(gate)
    act = gate * sig
    first = sig * (1.0 + gate * (1.0 - sig))
    second = sig * (1.0 - sig) * (2.0 + gate * (1.0 - 2.0 * sig))
    dgate = (dact * up * first).astype(jnp.bfloat16)
    dup = (dact * act).astype(jnp.bfloat16)
    tdgate = (dact * (tup * first + up * second * tgate)).astype(jnp.bfloat16)
    tdup = (dact * first * tgate).astype(jnp.bfloat16)
    tact = (tgate * first * up + act * tup).astype(jnp.bfloat16)
    return (dgate, dup, tdgate, tdup, tact)


def local(primal_in, tangent_in, cotangent, gate_weight, up_weight, down_weight):
    primal, tangent, cotan = (
        lax.all_gather(primal_in, "wide", axis=0, tiled=True),
        lax.all_gather(tangent_in, "wide", axis=0, tiled=True),
        lax.all_gather(cotangent, "wide", axis=0, tiled=True),
    )
    gate_part = jnp.dot(primal, gate_weight, preferred_element_type=jnp.float32)
    up_part = jnp.dot(primal, up_weight, preferred_element_type=jnp.float32)
    tgate_part = jnp.dot(tangent, gate_weight, preferred_element_type=jnp.float32)
    tup_part = jnp.dot(tangent, up_weight, preferred_element_type=jnp.float32)
    dact_part = contract_last(cotan, down_weight)
    gate, up, tgate, tup, dact = lax.psum(
        (gate_part, up_part, tgate_part, tup_part, dact_part), "narrow"
    )
    dgate, dup, tdgate, tdup, tact = factors(gate, up, tgate, tup, dact)
    input_hvp = lax.psum_scatter(
        contract_last(tdgate, gate_weight) + contract_last(tdup, up_weight),
        "wide",
        scatter_dimension=0,
        tiled=True,
    ).astype(jnp.bfloat16)
    gate_grad = contract_first(tangent, dgate) + contract_first(primal, tdgate)
    up_grad = contract_first(tangent, dup) + contract_first(primal, tdup)
    down_grad = contract_first(tact, cotan)
    return (input_hvp, gate_grad, up_grad, down_grad)


def solution(mesh):
    return jax.shard_map(
        local,
        mesh=mesh,
        in_specs=(
            P("wide", "narrow"),
            P("wide", "narrow"),
            P("wide", "narrow"),
            P("narrow", "wide"),
            P("narrow", "wide"),
            P("wide", "narrow"),
        ),
        out_specs=(
            P("wide", "narrow"),
            P("narrow", "wide"),
            P("narrow", "wide"),
            P("wide", "narrow"),
        ),
        check_vma=False,
    )
```

profile of v0, /device:TPU:0, one launch (start us, length us, event | category | flops | bytes accessed | tf_op | source)
XLA Modules:
  0.0 258.1 jit_solution(11240260281633427051)
XLA Ops:
  7.2 0.0 copy-start
  7.2 0.0 all-reduce.5.cloned.1.call-start
  7.2 0.0 copy-start.1
  7.2 44.2 %all-gather.1 = bf16[16,2,4096]{2,1,0:T(2,128)(2,1)S(1)} all-gather(bf16[1,2,4096]{2,1,0:T(2,128)(2,1)} %bitcast.29), channel_id=1, replica_groups=mesh['wide'=16,'narrow'=2] {'wide'}, dimensions={0}, use_global_device_ids=true | all-gather | bytes 278528 | tf_op jit(solution)/shard_map/all_gather | solution.py:35
  51.5 0.1 reshape.11
  51.6 37.2 %all-gather.2 = bf16[16,2,4096]{2,1,0:T(2,128)(2,1)S(1)} all-gather(bf16[1,2,4096]{2,1,0:T(2,128)(2,1)} %bitcast.30), channel_id=1, replica_groups=mesh['wide'=16,'narrow'=2] {'wide'}, dimensions={0}, use_global_device_ids=true | all-gather | bytes 278528 | tf_op jit(solution)/shard_map/all_gather | solution.py:34
  88.8 0.1 reshape.13
  88.9 0.0 copy-done
  88.9 0.9 fusion.24
  89.8 0.0 copy-start.8
  89.8 0.9 fusion.22
  90.7 0.0 copy-done.1
  90.7 0.9 fusion.23
  91.5 0.0 copy-start.9
  91.5 0.9 fusion.21
  92.4 0.0 copy-done.8
  92.4 38.8 %all-gather = bf16[16,2,4096]{2,1,0:T(2,128)(2,1)S(1)} all-gather(bf16[1,2,4096]{2,1,0:T(2,128)(2,1)S(1)} %bitcast.31), channel_id=1, replica_groups=mesh['wide'=16,'narrow'=2] {'wide'}, dimensions={0}, use_global_device_ids=true | all-gather | bytes 278528 | tf_op jit(solution)/shard_map/all_gather | solution.py:36
  131.3 0.1 reshape.9
  131.4 2.3 fusion.20
  133.7 0.0 all-reduce.5.cloned.1.call-update
  133.7 0.0 copy-done.9
  133.7 0.6 dynamic-slice
  135.0 12.9 %all-reduce.5.cloned.1.call-done = (f32[32,128]{1,0:T(8,128)}, f32[32,128]{1,0:T(8,128)}, f32[32,128]{1,0:T(8,128)}, f32[32,128]{1,0:T(8,128)}, f32[32,128]{1,0:T(8,128)}) async-done(((f32[32,128]{1,0:T(8,128)}, f32[32,128]{1,0:T(8,128)}, f32[32,128]{1,0:T(8,128)}, f32[32,128]{1,0:T(8,128)}, f32[32,128]{1,0:T(8,128)}), (f32[32,128]{1,0:T(8,128)}, f32[32,128]{1,0:T(8,128)}, f32[32,128]{1,0:T(8,128)}, ...) | async-done | bytes 81936 | tf_op jit(solution)/shard_map/psum | solution.py:43
  147.9 0.0 copy-start.3
  147.9 0.0 copy-start.4
  147.9 0.0 copy-start.5
  147.9 0.0 copy-start.6
  147.9 0.0 copy-start.7
  148.0 2.6 %fusion.12 = f32[128,4096]{1,0:T(8,128)} fusion(bf16[32,4096]{1,0:T(8,128)(2,1)S(1)} %reshape.11, f32[32,128]{1,0:T(8,128)} %get-tuple-element.12, f32[32,128]{1,0:T(8,128)} %get-tuple-element.15), kind=kOutput, calls=%fused_computation.23 | convolution fusion | flops 33579008 | bytes 2392064 | tf_op jit(solution)/shard_map/dot_general | solution.py:8
  150.6 0.0 copy-done.3
  150.6 0.0 copy-done.4
  150.6 0.0 copy-done.5
  150.6 1.8 fusion.11
  152.4 0.0 copy-done.6
  152.4 0.0 copy-done.7
  152.4 1.8 fusion.13
  154.2 0.4 fusion.25
  154.6 0.5 convolution_add_fusion.2
  155.1 83.6 %all-reduce.6 = bf16[32,4096]{1,0:T(8,128)(2,1)} all-reduce(f32[32,4096]{1,0:T(8,128)S(1)} %convolution_add_fusion.2), channel_id=2, replica_groups=mesh['wide'=16,'narrow'=2] {'wide'}, use_global_device_ids=true, to_apply=%region_5.0.clone | all-reduce | flops 131072 | bytes 786432
  238.7 3.4 %fusion.1 = f32[4096,128]{0,1:T(8,128)} fusion(f32[128,4096]{1,0:T(8,128)} %fusion.11, bf16[32,128]{1,0:T(8,128)(2,1)S(1)} %get-tuple-element.18, bf16[32,4096]{1,0:T(8,128)(2,1)S(1)} %reshape.13), kind=kOutput, calls=%fused_computation.3 | convolution fusion | flops 34078720 | bytes 4464640 | tf_op jit(solution)/shard_map/dot_general | solution.py:8
  242.1 0.0 copy-start.2
  242.1 3.0 %copy.12 = f32[4096,128]{1,0:T(8,128)} copy(f32[4096,128]{0,1:T(8,128)} %fusion.1) | data formatting | bytes 4194304
  245.1 0.0 copy-done.2
  245.1 1.8 fusion
  246.9 2.9 %copy.13 = f32[4096,128]{1,0:T(8,128)} copy(f32[4096,128]{0,1:T(8,128)} %fusion) | data formatting | bytes 4194304
  249.8 1.5 dynamic-slice_convert_fusion
  (1 shorter events, 0.0 us)
Async XLA Ops:
  7.2 81.7 %copy-start = (bf16[4096,128]{1,0:T(8,128)(2,1)S(1)}, bf16[4096,128]{1,0:T(8,128)(2,1)}, u32[]{:S(2)}) copy-start(bf16[4096,128]{1,0:T(8,128)(2,1)} %param.9) | copy-start | bytes 3145732
  7.2 140.8 %all-reduce.5.cloned.1.call-start = ((), (), s32[]{:S(2)}) async-start(), calls=%async_computation | async-start | bytes 163840 | tf_op jit(solution)/shard_map/psum | solution.py:43
  7.2 83.4 %copy-start.1 = (bf16[4096,128]{1,0:T(8,128)(2,1)S(1)}, bf16[4096,128]{1,0:T(8,128)(2,1)}, u32[]{:S(2)}) copy-start(bf16[4096,128]{1,0:T(8,128)(2,1)} %param.10) | copy-start | bytes 3145732
  89.8 2.7 %copy-start.8 = (bf16[2,4096]{1,0:T(2,128)(2,1)S(1)}, bf16[2,4096]{1,0:T(2,128)(2,1)}, u32[]{:S(2)}) copy-start(bf16[2,4096]{1,0:T(2,128)(2,1)} %param.8) | copy-start | bytes 49156
  91.5 42.2 %copy-start.9 = (u32[32]{0:T(128)S(1)}, u32[32]{0:T(128)}, u32[]{:S(2)}) copy-start(u32[32]{0:T(128)} %constant.9) | copy-start | bytes 388
  147.9 2.6 %copy-start.3 = (f32[32,128]{1,0:T(8,128)S(1)}, f32[32,128]{1,0:T(8,128)}, u32[]{:S(2)}) copy-start(f32[32,128]{1,0:T(8,128)} %get-tuple-element.15) | copy-start | bytes 49156
  147.9 2.6 %copy-start.4 = (f32[32,128]{1,0:T(8,128)S(1)}, f32[32,128]{1,0:T(8,128)}, u32[]{:S(2)}) copy-start(f32[32,128]{1,0:T(8,128)} %get-tuple-element.14) | copy-start | bytes 49156
  147.9 2.6 %copy-start.5 = (f32[32,128]{1,0:T(8,128)S(1)}, f32[32,128]{1,0:T(8,128)}, u32[]{:S(2)}) copy-start(f32[32,128]{1,0:T(8,128)} %get-tuple-element.12) | copy-start | bytes 49156
  147.9 4.4 %copy-start.6 = (f32[32,128]{1,0:T(8,128)S(1)}, f32[32,128]{1,0:T(8,128)}, u32[]{:S(2)}) copy-start(f32[32,128]{1,0:T(8,128)} %get-tuple-element.13) | copy-start | bytes 49156
  147.9 4.4 %copy-start.7 = (f32[32,128]{1,0:T(8,128)S(1)}, f32[32,128]{1,0:T(8,128)}, u32[]{:S(2)}) copy-start(f32[32,128]{1,0:T(8,128)} %get-tuple-element.16) | copy-start | bytes 49156
  242.1 3.0 %copy-start.2 = (f32[128,4096]{1,0:T(8,128)S(1)}, f32[128,4096]{1,0:T(8,128)}, u32[]{:S(2)}) copy-start(f32[128,4096]{1,0:T(8,128)} %fusion.12) | copy-start | bytes 6291460
Sparse Core Ops, SparseCore 0:
  133.8 14.0 all-reduce.4
where the time goes:
time: 258 us
  blocking collectives  204 us (79%)
  matrix products  18.1 us (7%)
  between operations  14.7 us (6%)
  waiting for transfers between devices  13 us (5%)
  local copies, waits for them, and re-layouts  8.35 us (3%)
    unnamed x1, blocking collectives  83.6 us
    all_gather x1, blocking collectives, local(): lax.all_gather(tangent_in, 'wide', axis=0, tiled=True)  44.2 us
    all_gather x1, blocking collectives, local(): lax.all_gather(cotangent, 'wide', axis=0, tiled=True)  38.8 us
    all_gather x1, blocking collectives, local(): lax.all_gather(primal_in, 'wide', axis=0, tiled=True)  37.2 us
    psum x1, waiting for transfers between devices, local(): lax.psum((gate_part, up_part, tgate_part, tup_part, dact_part), 'narrow')  12.9 us
    dot_general x5, matrix products, contract_first(): lax.dot_general(left, right, (((0,), (0,)), ((), ())), preferred_element_...  11.4 us
    unnamed x26, local copies, waits for them, and re-layouts  6.89 us
  transfers between devices with their start and end apart: 1, of which 1 were waited for; matrix products, arithmetic and copies ran while one was open for 0% of the time, Pallas kernels for 0%

commit v1 on v0

v1 whole, which is shorter than its diff:
```python
import jax
import jax.numpy as jnp
from jax import lax
from jax.sharding import PartitionSpec as P


def levels_of(size):
    levels, stride = [], 1
    while stride < size:
        rest = size // stride
        radix = next(r for r in (4, 2, 3, 5, 7, rest) if rest % r == 0)
        levels.append((stride, radix))
        stride *= radix
    return levels[::-1]


def partner(index, stride, radix, offset):
    digit = index // stride % radix
    if radix & (radix - 1) == 0:
        other = digit ^ offset
    else:
        other = (digit + offset) % radix
    return index + (other - digit) * stride


def fetch(value, axis, size, stride, radix, offset):
    pairs = [(partner(i, stride, radix, offset), i) for i in range(size)]
    return lax.ppermute(value, axis, pairs)


def deliver(value, axis, size, stride, radix, offset):
    pairs = [(i, partner(i, stride, radix, offset)) for i in range(size)]
    return lax.ppermute(value, axis, pairs)


def gather_rows(rows, axis, size):
    for stride, radix in levels_of(size):
        rows = jnp.concatenate(
            [rows]
            + [fetch(rows, axis, size, stride, radix, o) for o in range(1, radix)]
        )
    return rows


def scatter_sum(rows, axis, size):
    for stride, radix in levels_of(size)[::-1]:
        parts = jnp.split(rows, radix)
        rows = parts[0]
        for o in range(1, radix):
            rows = rows + deliver(parts[o], axis, size, stride, radix, o)
    return rows


def contract_first(left, right):
    return lax.dot_general(
        left, right, (((0,), (0,)), ((), ())), preferred_element_type=jnp.float32
    )


def contract_last(left, right):
    return lax.dot_general(
        left, right, (((1,), (1,)), ((), ())), preferred_element_type=jnp.float32
    )


def factors(gate, up, tgate, tup, dact):
    sig = jax.nn.sigmoid(gate)
    act = gate * sig
    first = sig * (1.0 + gate * (1.0 - sig))
    second = sig * (1.0 - sig) * (2.0 + gate * (1.0 - 2.0 * sig))
    dgate = (dact * up * first).astype(jnp.bfloat16)
    dup = (dact * act).astype(jnp.bfloat16)
    tdgate = (dact * (tup * first + up * second * tgate)).astype(jnp.bfloat16)
    tdup = (dact * first * tgate).astype(jnp.bfloat16)
    tact = (tgate * first * up + act * tup).astype(jnp.bfloat16)
    return (dgate, dup, tdgate, tdup, tact)


def solution(mesh):
    wide, narrow = mesh.shape["wide"], mesh.shape["narrow"]

    def local(primal_in, tangent_in, cotangent, gate_weight, up_weight, down_weight):
        width = primal_in.shape[1]
        rows = gather_rows(
            jnp.concatenate([primal_in, tangent_in, cotangent], axis=1), "wide", wide
        )
        primal, tangent, cotan = (
            rows[:, k * width : (k + 1) * width] for k in range(3)
        )
        parts = jnp.stack(
            [
                jnp.dot(primal, gate_weight, preferred_element_type=jnp.float32),
                jnp.dot(primal, up_weight, preferred_element_type=jnp.float32),
                jnp.dot(tangent, gate_weight, preferred_element_type=jnp.float32),
                jnp.dot(tangent, up_weight, preferred_element_type=jnp.float32),
                contract_last(cotan, down_weight),
            ]
        )
        total = parts
        for shift in range(1, narrow):
            pairs = [(i, (i + shift) % narrow) for i in range(narrow)]
            total = total + lax.ppermute(parts, "narrow", pairs)
        dgate, dup, tdgate, tdup, tact = factors(*total)
        input_hvp = scatter_sum(
            contract_last(tdgate, gate_weight) + contract_last(tdup, up_weight),
            "wide",
            wide,
        ).astype(jnp.bfloat16)
        gate_grad = contract_first(tangent, dgate) + contract_first(primal, tdgate)
        up_grad = contract_first(tangent, dup) + contract_first(primal, tdup)
        down_grad = contract_first(tact, cotan)
        return (input_hvp, gate_grad, up_grad, down_grad)

    return jax.shard_map(
        local,
        mesh=mesh,
        in_specs=(
            P("wide", "narrow"),
            P("wide", "narrow"),
            P("wide", "narrow"),
            P("narrow", "wide"),
            P("narrow", "wide"),
            P("wide", "narrow"),
        ),
        out_specs=(
            P("wide", "narrow"),
            P("narrow", "wide"),
            P("narrow", "wide"),
            P("wide", "narrow"),
        ),
        check_vma=False,
    )
```

time: 258 us -> 50.5 us (0.20)
  blocking collectives: 204 us -> 0 us
  starting transfers between devices: 0.04 us -> 16.4 us
  between operations: 14.7 us -> 0.77 us
  matrix products: 18.1 us -> 8.82 us
  waiting for transfers between devices: 13 us -> 18.9 us
  local copies, waits for them, and re-layouts: 8.35 us -> 4.25 us
    all_gather x3 -> x0, blocking collectives: 120 us -> none  [the longest x1 44.2 us: local(): lax.all_gather(tangent_in, 'wide', axis=0, tiled=True)]
    unnamed x1 -> x0, blocking collectives: 83.6 us -> none
    ppermute x0 -> x13, waiting for transfers between devices: none -> 18.9 us  [the longest x6 11.9 us: fetch(): return lax.ppermute(value, axis, pairs)]
    ppermute x0 -> x13, starting transfers between devices: none -> 16.4 us  [the longest x6 9.31 us: fetch(): return lax.ppermute(value, axis, pairs)]
    psum x1 -> x0, waiting for transfers between devices: 12.9 us -> none  [local(): lax.psum((gate_part, up_part, tgate_part, tup_part, dact_part), 'narrow')]
    dot_general x5, matrix products: 11.4 us -> 6.35 us  [contract_first(): lax.dot_general(left, right, (((0,), (0,)), ((), ())), preferred_element_...]
    unnamed x26 -> x8, local copies, waits for them, and re-layouts: 6.89 us -> 1.99 us
  transfers between devices with their start and end apart: 1 -> 13, of which waited for: 1 -> 10; matrix products, arithmetic and copies ran while one was open for 0% -> 11% of each run, Pallas kernels for 0% -> 0%
where the time goes in v1:
time: 50.5 us; the launch traced here: 50.1 us
  waiting for transfers between devices  18.9 us (37%)
  starting transfers between devices  16.4 us (32%)
  matrix products  8.82 us (17%)
  local copies, waits for them, and re-layouts  4.25 us (8%)
  other arithmetic  0.93 us (2%)
  between operations  0.77 us (2%)
    ppermute x6, waiting for transfers between devices, fetch(): return lax.ppermute(value, axis, pairs)  11.9 us
    ppermute x6, starting transfers between devices, fetch(): return lax.ppermute(value, axis, pairs)  9.31 us
    ppermute x6, starting transfers between devices, deliver(): return lax.ppermute(value, axis, pairs)  7.11 us
    dot_general x5, matrix products, contract_first(): lax.dot_general(left, right, (((0,), (0,)), ((), ())), preferred_element_...  6.35 us
    ppermute x6, waiting for transfers between devices, deliver(): return lax.ppermute(value, axis, pairs)  5.69 us
    unnamed x8, local copies, waits for them, and re-layouts  1.99 us
    concatenate x1, local copies, waits for them, and re-layouts, gather_rows(): jnp.concatenate([rows] + [fetch(rows, axis, size, stride, radix, o) for o...  1.46 us
    dot_general x3, matrix products, contract_last(): lax.dot_general(left, right, (((1,), (1,)), ((), ())), preferred_element_...  1.35 us
  transfers between devices with their start and end apart: 13, of which 10 were waited for; matrix products, arithmetic and copies ran while one was open for 11% of the time, Pallas kernels for 0%

profile of v1, /device:TPU:0, one launch (start us, length us, event | category | flops | bytes accessed | tf_op | source)
XLA Modules:
  0.0 50.1 jit_solution(11907996874041939053)
XLA Ops:
  0.6 0.0 copy-start
  0.6 0.0 copy-start.1
  0.7 0.9 %constant_dynamic-update-slice_fusion.2 = bf16[2,12288]{1,0:T(2,128)(2,1)S(1)} fusion(bf16[2,4096]{1,0:T(2,128)(2,1)} %param.6), kind=kLoop, calls=%fused_computation.38 | loop fusion | bytes 32768
  1.5 0.7 %constant_dynamic-update-slice_fusion.1 = bf16[2,12288]{1,0:T(2,128)(2,1)S(1)} fusion(bf16[2,12288]{1,0:T(2,128)(2,1)S(1)} %constant_dynamic-update-slice_fusion.2, bf16[2,4096]{1,0:T(2,128)(2,1)} %param.7), kind=kLoop, calls=%fused_computation.37 | loop fusion | bytes 32768
  2.3 0.7 %constant_dynamic-update-slice_fusion = bf16[2,12288]{1,0:T(2,128)(2,1)S(1)} fusion(bf16[2,12288]{1,0:T(2,128)(2,1)S(1)} %constant_dynamic-update-slice_fusion.1, bf16[2,4096]{1,0:T(2,128)(2,1)} %param.8), kind=kLoop, calls=%fused_computation.36 | loop fusion | bytes 32768 | tf_op jit(solution)/shard_map/concatenate | solution.py:85
  3.0 5.1 %collective-permute-start.2 = (bf16[2,12288]{1,0:T(2,128)(2,1)S(1)}, bf16[2,12288]{1,0:T(2,128)(2,1)S(1)}, u32[]{:S(2)}, u32[]{:S(2)}) collective-permute-start(bf16[2,12288]{1,0:T(2,128)(2,1)S(1)} %constant_dynamic-update-slice_fusion), channel_id=1, source_target_pairs={{24,0},{26,2},{28,4},{30,6},{16,8},{18,10},{20,12},{22,14},{8,16},... | collective-permute-start | bytes 147464 | tf_op jit(solution)/shard_map/ppermute | solution.py:28
  8.1 0.0 collective-permute-start.1
  8.1 0.6 %collective-permute-start = (bf16[2,12288]{1,0:T(2,128)(2,1)S(1)}, bf16[2,12288]{1,0:T(2,128)(2,1)S(1)}, u32[]{:S(2)}, u32[]{:S(2)}) collective-permute-start(bf16[2,12288]{1,0:T(2,128)(2,1)S(1)} %constant_dynamic-update-slice_fusion), channel_id=1, source_target_pairs={{8,0},{10,2},{12,4},{14,6},{0,8},{2,10},{4,12},{6,14},{24,16},{26,... | collective-permute-start | bytes 147464 | tf_op jit(solution)/shard_map/ppermute | solution.py:28
  8.8 1.6 %collective-permute-done.2 = bf16[2,12288]{1,0:T(2,128)(2,1)S(1)} collective-permute-done((bf16[2,12288]{1,0:T(2,128)(2,1)S(1)}, bf16[2,12288]{1,0:T(2,128)(2,1)S(1)}, u32[]{:S(2)}, u32[]{:S(2)}) %collective-permute-start.2) | collective-permute-done | bytes 49184 | tf_op jit(solution)/shard_map/ppermute | solution.py:28
  10.4 2.8 %collective-permute-done.1 = bf16[2,12288]{1,0:T(2,128)(2,1)S(1)} collective-permute-done((bf16[2,12288]{1,0:T(2,128)(2,1)S(1)}, bf16[2,12288]{1,0:T(2,128)(2,1)S(1)}, u32[]{:S(2)}, u32[]{:S(2)}) %collective-permute-start.1) | collective-permute-done | bytes 49184 | tf_op jit(solution)/shard_map/ppermute | solution.py:28
  13.1 0.0 collective-permute-done
  13.1 0.2 pad_maximum_fusion
  13.4 2.5 %collective-permute-start.5 = (bf16[8,12288]{1,0:T(8,128)(2,1)S(1)}, bf16[8,12288]{1,0:T(8,128)(2,1)S(1)}, u32[]{:S(2)}, u32[]{:S(2)}) collective-permute-start(bf16[8,12288]{1,0:T(8,128)(2,1)S(1)} %pad_maximum_fusion), channel_id=1, source_target_pairs={{6,0},{4,2},{2,4},{0,6},{14,8},{12,10},{10,12},{8,14},{22,16},{20,... | collective-permute-start | bytes 589832 | tf_op jit(solution)/shard_map/ppermute | solution.py:28
  15.9 0.5 %collective-permute-start.4 = (bf16[8,12288]{1,0:T(8,128)(2,1)S(1)}, bf16[8,12288]{1,0:T(8,128)(2,1)S(1)}, u32[]{:S(2)}, u32[]{:S(2)}) collective-permute-start(bf16[8,12288]{1,0:T(8,128)(2,1)S(1)} %pad_maximum_fusion), channel_id=1, source_target_pairs={{4,0},{6,2},{0,4},{2,6},{12,8},{14,10},{8,12},{10,14},{20,16},{22,... | collective-permute-start | bytes 589832 | tf_op jit(solution)/shard_map/ppermute | solution.py:28
  16.4 0.5 %collective-permute-start.3 = (bf16[8,12288]{1,0:T(8,128)(2,1)S(1)}, bf16[8,12288]{1,0:T(8,128)(2,1)}, u32[]{:S(2)}, u32[]{:S(2)}) collective-permute-start(bf16[8,12288]{1,0:T(8,128)(2,1)S(1)} %pad_maximum_fusion), channel_id=1, source_target_pairs={{2,0},{0,2},{6,4},{4,6},{10,8},{8,10},{14,12},{12,14},{18,16},{16,... | collective-permute-start | bytes 589832 | tf_op jit(solution)/shard_map/ppermute | solution.py:28
  16.9 4.9 %collective-permute-done.5 = bf16[8,12288]{1,0:T(8,128)(2,1)S(1)} collective-permute-done((bf16[8,12288]{1,0:T(8,128)(2,1)S(1)}, bf16[8,12288]{1,0:T(8,128)(2,1)S(1)}, u32[]{:S(2)}, u32[]{:S(2)}) %collective-permute-start.5) | collective-permute-done | bytes 196640 | tf_op jit(solution)/shard_map/ppermute | solution.py:28
  21.8 2.5 %collective-permute-done.4 = bf16[8,12288]{1,0:T(8,128)(2,1)S(1)} collective-permute-done((bf16[8,12288]{1,0:T(8,128)(2,1)S(1)}, bf16[8,12288]{1,0:T(8,128)(2,1)S(1)}, u32[]{:S(2)}, u32[]{:S(2)}) %collective-permute-start.4) | collective-permute-done | bytes 196640 | tf_op jit(solution)/shard_map/ppermute | solution.py:28
  24.3 0.2 collective-permute-done.3
  24.5 1.5 %concatenate.12 = bf16[32,12288]{1,0:T(8,128)(2,1)S(1)} concatenate(bf16[2,12288]{1,0:T(2,128)(2,1)S(1)} %constant_dynamic-update-slice_fusion, bf16[2,12288]{1,0:T(2,128)(2,1)S(1)} %collective-permute-done, bf16[2,12288]{1,0:T(2,128)(2,1)S(1)} %collective-permute-done.1, bf16[2,12288]{1,0:T(2,128)(2,1)S(1)} %collective-permute-done.2, bf16[8,12288]{1,0:T(8,128)(2,1)} %collective-permute-done.3, ...), dimensions={0} | concatenate | bytes 1572864 | tf_op jit(solution)/shard_map/concatenate | solution.py:38
  26.0 0.0 copy-done
  26.0 0.3 fusion.4
  26.3 0.0 copy-done.1
  26.3 0.0 copy-start.2
  26.3 0.3 fusion.3
  26.6 0.3 fusion.2
  26.9 0.3 fusion.1
  27.1 0.4 copy-done.2
  27.5 0.4 fusion
  27.9 0.0 collective-permute-start.6
  28.0 1.3 %collective-permute-done.6 = f32[5,32,128]{2,1,0:T(8,128)S(1)} collective-permute-done((f32[5,32,128]{2,1,0:T(8,128)S(1)}, f32[5,32,128]{2,1,0:T(8,128)S(1)}, u32[]{:S(2)}, u32[]{:S(2)}) %collective-permute-start.6) | collective-permute-done | bytes 81952 | tf_op jit(solution)/shard_map/ppermute | solution.py:102
  29.3 0.5 fusion.40
  29.7 0.5 fusion.14
  30.2 0.5 fusion.12
  30.7 0.5 convolution_add_fusion.2
  31.2 1.6 %collective-permute-start.7 = (f32[8,4096]{1,0:T(8,128)S(1)}, f32[8,4096]{1,0:T(8,128)S(1)}, u32[]{:S(2)}, u32[]{:S(2)}) collective-permute-start(f32[8,4096]{1,0:T(8,128)S(1)} %get-tuple-element.4), channel_id=1, source_target_pairs={{0,2},{2,0},{4,6},{6,4},{8,10},{10,8},{12,14},{14,12},{16,18},{18,... | collective-permute-start | bytes 393224 | tf_op jit(solution)/shard_map/ppermute | solution.py:33
  32.8 1.3 %collective-permute-start.9 = (f32[8,4096]{1,0:T(8,128)S(1)}, f32[8,4096]{1,0:T(8,128)S(1)}, u32[]{:S(2)}, u32[]{:S(2)}) collective-permute-start(f32[8,4096]{1,0:T(8,128)S(1)} %get-tuple-element.5), channel_id=1, source_target_pairs={{0,6},{2,4},{4,2},{6,0},{8,14},{10,12},{12,10},{14,8},{16,22},{18,... | collective-permute-start | bytes 393224 | tf_op jit(solution)/shard_map/ppermute | solution.py:33
  34.0 0.7 %collective-permute-start.8 = (f32[8,4096]{1,0:T(8,128)S(1)}, f32[8,4096]{1,0:T(8,128)S(1)}, u32[]{:S(2)}, u32[]{:S(2)}) collective-permute-start(f32[8,4096]{1,0:T(8,128)S(1)} %get-tuple-element.6), channel_id=1, source_target_pairs={{0,4},{2,6},{4,0},{6,2},{8,12},{10,14},{12,8},{14,10},{16,20},{18,... | collective-permute-start | bytes 393224 | tf_op jit(solution)/shard_map/ppermute | solution.py:33
  34.7 1.8 %convolution_add_fusion = f32[4096,128]{1,0:T(8,128)} fusion(f32[4096,128]{1,0:T(8,128)S(1)} %fusion.12, bf16[32,12288]{1,0:T(8,128)(2,1)S(1)} %concatenate.12, f32[5,32,128]{2,1,0:T(8,128)S(1)} %add.45), kind=kOutput, calls=%fused_computation | convolution fusion | flops 34103296 | bytes 4489216 | tf_op jit(solution)/shard_map/dot_general | solution.py:55
  36.5 1.8 %convolution_add_fusion.1 = f32[4096,128]{1,0:T(8,128)} fusion(f32[4096,128]{1,0:T(8,128)S(1)} %fusion.14, bf16[32,12288]{1,0:T(8,128)(2,1)S(1)} %concatenate.12, f32[5,32,128]{2,1,0:T(8,128)S(1)} %add.45), kind=kOutput, calls=%fused_computation.1 | convolution fusion | flops 34119680 | bytes 4505600 | tf_op jit(solution)/shard_map/dot_general | solution.py:55
  38.3 0.0 collective-permute-done.7
  38.3 2.1 %collective-permute-done.9 = f32[8,4096]{1,0:T(8,128)S(1)} collective-permute-done((f32[8,4096]{1,0:T(8,128)S(1)}, f32[8,4096]{1,0:T(8,128)S(1)}, u32[]{:S(2)}, u32[]{:S(2)}) %collective-permute-start.9) | collective-permute-done | bytes 131104 | tf_op jit(solution)/shard_map/ppermute | solution.py:33
  40.5 1.4 %collective-permute-done.8 = f32[8,4096]{1,0:T(8,128)S(1)} collective-permute-done((f32[8,4096]{1,0:T(8,128)S(1)}, f32[8,4096]{1,0:T(8,128)S(1)}, u32[]{:S(2)}, u32[]{:S(2)}) %collective-permute-start.8) | collective-permute-done | bytes 131104 | tf_op jit(solution)/shard_map/ppermute | solution.py:33
  41.9 0.8 %collective-permute-start.10 = (f32[2,4096]{1,0:T(2,128)S(1)}, f32[2,4096]{1,0:T(2,128)S(1)}, u32[]{:S(2)}, u32[]{:S(2)}) collective-permute-start(f32[2,4096]{1,0:T(2,128)S(1)} %get-tuple-element.7), channel_id=1, source_target_pairs={{0,8},{2,10},{4,12},{6,14},{8,0},{10,2},{12,4},{14,6},{16,24},{18,... | collective-permute-start | bytes 98312 | tf_op jit(solution)/shard_map/ppermute | solution.py:33
  42.7 2.0 %collective-permute-start.12 = (f32[2,4096]{1,0:T(2,128)S(1)}, f32[2,4096]{1,0:T(2,128)S(1)}, u32[]{:S(2)}, u32[]{:S(2)}) collective-permute-start(f32[2,4096]{1,0:T(2,128)S(1)} %get-tuple-element.8), channel_id=1, source_target_pairs={{0,24},{2,26},{4,28},{6,30},{8,16},{10,18},{12,20},{14,22},{16,8},... | collective-permute-start | bytes 98312 | tf_op jit(solution)/shard_map/ppermute | solution.py:33
  44.7 0.8 %collective-permute-start.11 = (f32[2,4096]{1,0:T(2,128)S(1)}, f32[2,4096]{1,0:T(2,128)S(1)}, u32[]{:S(2)}, u32[]{:S(2)}) collective-permute-start(f32[2,4096]{1,0:T(2,128)S(1)} %get-tuple-element.9), channel_id=1, source_target_pairs={{0,16},{2,18},{4,20},{6,22},{8,24},{10,26},{12,28},{14,30},{16,0},... | collective-permute-start | bytes 98312 | tf_op jit(solution)/shard_map/ppermute | solution.py:33
  45.5 1.8 %fusion.5 = f32[128,4096]{1,0:T(8,128)} fusion(bf16[32,12288]{1,0:T(8,128)(2,1)S(1)} %concatenate.12, f32[5,32,128]{2,1,0:T(8,128)S(1)} %add.45), kind=kOutput, calls=%fused_computation.13 | convolution fusion | flops 33607680 | bytes 2424832 | tf_op jit(solution)/shard_map/dot_general | solution.py:55
  47.3 0.0 collective-permute-done.10
  47.3 1.1 %collective-permute-done.12 = f32[2,4096]{1,0:T(2,128)S(1)} collective-permute-done((f32[2,4096]{1,0:T(2,128)S(1)}, f32[2,4096]{1,0:T(2,128)S(1)}, u32[]{:S(2)}, u32[]{:S(2)}) %collective-permute-start.12) | collective-permute-done | bytes 32800 | tf_op jit(solution)/shard_map/ppermute | solution.py:33
  48.4 1.1 %collective-permute-done.11 = f32[2,4096]{1,0:T(2,128)S(1)} collective-permute-done((f32[2,4096]{1,0:T(2,128)S(1)}, f32[2,4096]{1,0:T(2,128)S(1)}, u32[]{:S(2)}, u32[]{:S(2)}) %collective-permute-start.11) | collective-permute-done | bytes 32800 | tf_op jit(solution)/shard_map/ppermute | solution.py:33
  49.5 0.6 %fusion.22 = bf16[2,4096]{1,0:T(2,128)(2,1)} fusion(f32[2,4096]{1,0:T(2,128)S(1)} %collective-permute-done.12, f32[2,4096]{1,0:T(2,128)S(1)} %collective-permute-done.11, f32[2,4096]{1,0:T(2,128)S(1)} %collective-permute-done.10, f32[8,4096]{1,0:T(8,128)S(1)} %fusion.19), kind=kLoop, calls=%fused_computation.33 | loop fusion | flops 32768 | bytes 147456 | tf_op jit(solution)/shard_map/convert_element_type | solution.py:108
  (5 shorter events, 0.1 us)
Async XLA Ops:
  0.6 25.3 %copy-start = (bf16[4096,128]{1,0:T(8,128)(2,1)S(1)}, bf16[4096,128]{1,0:T(8,128)(2,1)}, u32[]{:S(2)}) copy-start(bf16[4096,128]{1,0:T(8,128)(2,1)} %param.9) | copy-start | bytes 3145732
  0.6 25.6 %copy-start.1 = (bf16[4096,128]{1,0:T(8,128)(2,1)S(1)}, bf16[4096,128]{1,0:T(8,128)(2,1)}, u32[]{:S(2)}) copy-start(bf16[4096,128]{1,0:T(8,128)(2,1)} %param.10) | copy-start | bytes 3145732
  3.0 7.3 %collective-permute-start.2 = (bf16[2,12288]{1,0:T(2,128)(2,1)S(1)}, bf16[2,12288]{1,0:T(2,128)(2,1)S(1)}, u32[]{:S(2)}, u32[]{:S(2)}) collective-permute-start(bf16[2,12288]{1,0:T(2,128)(2,1)S(1)} %constant_dynamic-update-slice_fusion), channel_id=1, source_target_pairs={{24,0},{26,2},{28,4},{30,6},{16,8},{18,10},{20,12},{22,14},{8,16},... | collective-permute-start | bytes 147464 | tf_op jit(solution)/shard_map/ppermute | solution.py:28
  8.1 5.0 %collective-permute-start.1 = (bf16[2,12288]{1,0:T(2,128)(2,1)S(1)}, bf16[2,12288]{1,0:T(2,128)(2,1)S(1)}, u32[]{:S(2)}, u32[]{:S(2)}) collective-permute-start(bf16[2,12288]{1,0:T(2,128)(2,1)S(1)} %constant_dynamic-update-slice_fusion), channel_id=1, source_target_pairs={{16,0},{18,2},{20,4},{22,6},{24,8},{26,10},{28,12},{30,14},{0,16},... | collective-permute-start | bytes 147464 | tf_op jit(solution)/shard_map/ppermute | solution.py:28
  8.1 5.0 %collective-permute-start = (bf16[2,12288]{1,0:T(2,128)(2,1)S(1)}, bf16[2,12288]{1,0:T(2,128)(2,1)S(1)}, u32[]{:S(2)}, u32[]{:S(2)}) collective-permute-start(bf16[2,12288]{1,0:T(2,128)(2,1)S(1)} %constant_dynamic-update-slice_fusion), channel_id=1, source_target_pairs={{8,0},{10,2},{12,4},{14,6},{0,8},{2,10},{4,12},{6,14},{24,16},{26,... | collective-permute-start | bytes 147464 | tf_op jit(solution)/shard_map/ppermute | solution.py:28
  13.4 8.5 %collective-permute-start.5 = (bf16[8,12288]{1,0:T(8,128)(2,1)S(1)}, bf16[8,12288]{1,0:T(8,128)(2,1)S(1)}, u32[]{:S(2)}, u32[]{:S(2)}) collective-permute-start(bf16[8,12288]{1,0:T(8,128)(2,1)S(1)} %pad_maximum_fusion), channel_id=1, source_target_pairs={{6,0},{4,2},{2,4},{0,6},{14,8},{12,10},{10,12},{8,14},{22,16},{20,... | collective-permute-start | bytes 589832 | tf_op jit(solution)/shard_map/ppermute | solution.py:28
  15.9 8.4 %collective-permute-start.4 = (bf16[8,12288]{1,0:T(8,128)(2,1)S(1)}, bf16[8,12288]{1,0:T(8,128)(2,1)S(1)}, u32[]{:S(2)}, u32[]{:S(2)}) collective-permute-start(bf16[8,12288]{1,0:T(8,128)(2,1)S(1)} %pad_maximum_fusion), channel_id=1, source_target_pairs={{4,0},{6,2},{0,4},{2,6},{12,8},{14,10},{8,12},{10,14},{20,16},{22,... | collective-permute-start | bytes 589832 | tf_op jit(solution)/shard_map/ppermute | solution.py:28
  16.4 8.1 %collective-permute-start.3 = (bf16[8,12288]{1,0:T(8,128)(2,1)S(1)}, bf16[8,12288]{1,0:T(8,128)(2,1)}, u32[]{:S(2)}, u32[]{:S(2)}) collective-permute-start(bf16[8,12288]{1,0:T(8,128)(2,1)S(1)} %pad_maximum_fusion), channel_id=1, source_target_pairs={{2,0},{0,2},{6,4},{4,6},{10,8},{8,10},{14,12},{12,14},{18,16},{16,... | collective-permute-start | bytes 589832 | tf_op jit(solution)/shard_map/ppermute | solution.py:28
  26.3 1.2 %copy-start.2 = (bf16[128,4096]{1,0:T(8,128)(2,1)S(1)}, bf16[128,4096]{1,0:T(8,128)(2,1)}, u32[]{:S(2)}) copy-start(bf16[128,4096]{1,0:T(8,128)(2,1)} %param.11) | copy-start | bytes 3145732
  27.9 1.3 %collective-permute-start.6 = (f32[5,32,128]{2,1,0:T(8,128)S(1)}, f32[5,32,128]{2,1,0:T(8,128)S(1)}, u32[]{:S(2)}, u32[]{:S(2)}) collective-permute-start(f32[5,32,128]{2,1,0:T(8,128)S(1)} %fusion), channel_id=1, source_target_pairs={{0,1},{1,0},{2,3},{3,2},{4,5},{5,4},{6,7},{7,6},{8,9},{9,8},{10,11... | collective-permute-start | bytes 245768 | tf_op jit(solution)/shard_map/ppermute | solution.py:102
  31.2 7.1 %collective-permute-start.7 = (f32[8,4096]{1,0:T(8,128)S(1)}, f32[8,4096]{1,0:T(8,128)S(1)}, u32[]{:S(2)}, u32[]{:S(2)}) collective-permute-start(f32[8,4096]{1,0:T(8,128)S(1)} %get-tuple-element.4), channel_id=1, source_target_pairs={{0,2},{2,0},{4,6},{6,4},{8,10},{10,8},{12,14},{14,12},{16,18},{18,... | collective-permute-start | bytes 393224 | tf_op jit(solution)/shard_map/ppermute | solution.py:33
  32.8 7.7 %collective-permute-start.9 = (f32[8,4096]{1,0:T(8,128)S(1)}, f32[8,4096]{1,0:T(8,128)S(1)}, u32[]{:S(2)}, u32[]{:S(2)}) collective-permute-start(f32[8,4096]{1,0:T(8,128)S(1)} %get-tuple-element.5), channel_id=1, source_target_pairs={{0,6},{2,4},{4,2},{6,0},{8,14},{10,12},{12,10},{14,8},{16,22},{18,... | collective-permute-start | bytes 393224 | tf_op jit(solution)/shard_map/ppermute | solution.py:33
  34.0 7.8 %collective-permute-start.8 = (f32[8,4096]{1,0:T(8,128)S(1)}, f32[8,4096]{1,0:T(8,128)S(1)}, u32[]{:S(2)}, u32[]{:S(2)}) collective-permute-start(f32[8,4096]{1,0:T(8,128)S(1)} %get-tuple-element.6), channel_id=1, source_target_pairs={{0,4},{2,6},{4,0},{6,2},{8,12},{10,14},{12,8},{14,10},{16,20},{18,... | collective-permute-start | bytes 393224 | tf_op jit(solution)/shard_map/ppermute | solution.py:33
  41.9 5.4 %collective-permute-start.10 = (f32[2,4096]{1,0:T(2,128)S(1)}, f32[2,4096]{1,0:T(2,128)S(1)}, u32[]{:S(2)}, u32[]{:S(2)}) collective-permute-start(f32[2,4096]{1,0:T(2,128)S(1)} %get-tuple-element.7), channel_id=1, source_target_pairs={{0,8},{2,10},{4,12},{6,14},{8,0},{10,2},{12,4},{14,6},{16,24},{18,... | collective-permute-start | bytes 98312 | tf_op jit(solution)/shard_map/ppermute | solution.py:33
  42.7 5.7 %collective-permute-start.12 = (f32[2,4096]{1,0:T(2,128)S(1)}, f32[2,4096]{1,0:T(2,128)S(1)}, u32[]{:S(2)}, u32[]{:S(2)}) collective-permute-start(f32[2,4096]{1,0:T(2,128)S(1)} %get-tuple-element.8), channel_id=1, source_target_pairs={{0,24},{2,26},{4,28},{6,30},{8,16},{10,18},{12,20},{14,22},{16,8},... | collective-permute-start | bytes 98312 | tf_op jit(solution)/shard_map/ppermute | solution.py:33
  44.7 4.8 %collective-permute-start.11 = (f32[2,4096]{1,0:T(2,128)S(1)}, f32[2,4096]{1,0:T(2,128)S(1)}, u32[]{:S(2)}, u32[]{:S(2)}) collective-permute-start(f32[2,4096]{1,0:T(2,128)S(1)} %get-tuple-element.9), channel_id=1, source_target_pairs={{0,16},{2,18},{4,20},{6,22},{8,24},{10,26},{12,28},{14,30},{16,0},... | collective-permute-start | bytes 98312 | tf_op jit(solution)/shard_map/ppermute | solution.py:33

commit v2 on v1

--- a/solution.py
+++ b/solution.py
@@ -33,13 +33,17 @@
     return lax.ppermute(value, axis, pairs)
 
 
-def gather_rows(rows, axis, size):
+def gather_blocks(own, axis, size):
+    rest = []
     for stride, radix in levels_of(size):
-        rows = jnp.concatenate(
-            [rows]
-            + [fetch(rows, axis, size, stride, radix, o) for o in range(1, radix)]
-        )
-    return rows
+        held = jnp.concatenate(rest) if rest else None
+        came = []
+        for o in range(1, radix):
+            came.append(fetch(own, axis, size, stride, radix, o))
+            if rest:
+                came.append(fetch(held, axis, size, stride, radix, o))
+        rest = ([held] if rest else []) + came
+    return jnp.concatenate([own] + rest)
 
 
 def scatter_sum(rows, axis, size):
@@ -47,7 +51,10 @@
         parts = jnp.split(rows, radix)
         rows = parts[0]
         for o in range(1, radix):
-            rows = rows + deliver(parts[o], axis, size, stride, radix, o)
+            came = deliver(
+                parts[o].astype(jnp.bfloat16), axis, size, stride, radix, o
+            )
+            rows = rows + came.astype(jnp.float32)
     return rows
 
 
@@ -80,12 +87,10 @@
     wide, narrow = mesh.shape["wide"], mesh.shape["narrow"]
 
     def local(primal_in, tangent_in, cotangent, gate_weight, up_weight, down_weight):
-        width = primal_in.shape[1]
-        rows = gather_rows(
-            jnp.concatenate([primal_in, tangent_in, cotangent], axis=1), "wide", wide
-        )
+        block = jnp.stack([primal_in, tangent_in, cotangent])[None]
+        blocks = gather_blocks(block, "wide", wide)
         primal, tangent, cotan = (
-            rows[:, k * width : (k + 1) * width] for k in range(3)
+            blocks[:, k].reshape(-1, primal_in.shape[1]) for k in range(3)
         )
         parts = jnp.stack(
             [

time: 50.5 us -> 45.4 us (0.90)
  waiting for transfers between devices: 18.9 us -> 9.07 us
  starting transfers between devices: 16.4 us -> 20.8 us
  local copies, waits for them, and re-layouts: 4.25 us -> 1.84 us
  other arithmetic: 0.93 us -> 2.4 us
  matrix products: 8.82 us -> 10 us
    ppermute x6 -> x9, waiting for transfers between devices: 11.9 us -> 6.84 us  [fetch(): return lax.ppermute(value, axis, pairs)]
    ppermute x6, waiting for transfers between devices: 5.69 us -> 0.96 us  [deliver(): return lax.ppermute(value, axis, pairs)]
    ppermute x6 -> x9, starting transfers between devices: 9.31 us -> 12.8 us  [fetch(): return lax.ppermute(value, axis, pairs)]
    concatenate x2, local copies, waits for them, and re-layouts: 2.2 us -> 0.19 us  [the longest x1 0.12 us: gather_blocks(): return jnp.concatenate([own] + rest)]
    unnamed x8 -> x11, local copies, waits for them, and re-layouts: 1.99 us -> 0.53 us
    dot_general x3, matrix products: 1.35 us -> 2.58 us  [contract_last(): lax.dot_general(left, right, (((1,), (1,)), ((), ())), preferred_element_...]
    broadcast_in_dim x0 -> x1, other arithmetic: none -> 0.92 us  [local(): block = jnp.stack([primal_in, tangent_in, cotangent])[None]]
    ppermute x6, starting transfers between devices: 7.11 us -> 8.01 us  [deliver(): return lax.ppermute(value, axis, pairs)]
  transfers between devices with their start and end apart: 13 -> 16, of which waited for: 10 -> 5; matrix products, arithmetic and copies ran while one was open for 11% -> 15% of each run, Pallas kernels for 0% -> 0%
where the time goes in v2:
time: 45.4 us; the launch traced here: 45 us
  starting transfers between devices  20.8 us (46%)
  matrix products  10 us (22%)
  waiting for transfers between devices  9.07 us (20%)
  other arithmetic  2.4 us (5%)
  local copies, waits for them, and re-layouts  1.84 us (4%)
  between operations  0.86 us (2%)
    ppermute x9, starting transfers between devices, fetch(): return lax.ppermute(value, axis, pairs)  12.8 us
    ppermute x6, starting transfers between devices, deliver(): return lax.ppermute(value, axis, pairs)  8.01 us
    ppermute x9, waiting for transfers between devices, fetch(): return lax.ppermute(value, axis, pairs)  6.84 us
    dot_general x5, matrix products, contract_first(): lax.dot_general(left, right, (((0,), (0,)), ((), ())), preferred_element_...  6.33 us
    dot_general x3, matrix products, contract_last(): lax.dot_general(left, right, (((1,), (1,)), ((), ())), preferred_element_...  2.58 us
    ppermute x1, waiting for transfers between devices, local(): total = total + lax.ppermute(parts, 'narrow', pairs)  1.27 us
    ppermute x6, waiting for transfers between devices, deliver(): return lax.ppermute(value, axis, pairs)  0.96 us
    broadcast_in_dim x1, other arithmetic, local(): block = jnp.stack([primal_in, tangent_in, cotangent])[None]  0.92 us
  transfers between devices with their start and end apart: 16, of which 5 were waited for; matrix products, arithmetic and copies ran while one was open for 15% of the time, Pallas kernels for 0%

profile of v2, /device:TPU:0, one launch (start us, length us, event | category | flops | bytes accessed | tf_op | source)
XLA Modules:
  0.0 45.0 jit_solution(5545418636280452812)
XLA Ops:
  0.6 0.0 copy-start
  0.6 0.9 %maximum_bitcast_fusion = bf16[1,3,2,4096]{3,2,1,0:T(2,128)(2,1)S(1)} fusion(bf16[1,2,4096]{2,1,0:T(2,128)(2,1)} %bitcast.112, bf16[1,2,4096]{2,1,0:T(2,128)(2,1)} %bitcast.114, bf16[1,2,4096]{2,1,0:T(2,128)(2,1)} %bitcast.116), kind=kLoop, calls=%fused_computation.16 | loop fusion | flops 49152 | bytes 98304 | tf_op jit(solution)/shard_map/broadcast_in_dim | solution.py:90
  1.6 3.1 %collective-permute-start = (bf16[1,3,2,4096]{3,2,1,0:T(2,128)(2,1)S(1)}, bf16[1,3,2,4096]{3,2,1,0:T(2,128)(2,1)S(1)}, u32[]{:S(2)}, u32[]{:S(2)}) collective-permute-start(bf16[1,3,2,4096]{3,2,1,0:T(2,128)(2,1)S(1)} %maximum_bitcast_fusion), channel_id=1, source_target_pairs={{8,0},{10,2},{12,4},{14,6},{0,8},{2,10},{4,12},{6,14},{24,16},{26,... | collective-permute-start | bytes 147464 | tf_op jit(solution)/shard_map/ppermute | solution.py:28
  4.7 2.6 %collective-permute-start.1 = (bf16[1,3,2,4096]{3,2,1,0:T(2,128)(2,1)S(1)}, bf16[1,3,2,4096]{3,2,1,0:T(2,128)(2,1)S(1)}, u32[]{:S(2)}, u32[]{:S(2)}) collective-permute-start(bf16[1,3,2,4096]{3,2,1,0:T(2,128)(2,1)S(1)} %maximum_bitcast_fusion), channel_id=1, source_target_pairs={{16,0},{18,2},{20,4},{22,6},{24,8},{26,10},{28,12},{30,14},{0,16},... | collective-permute-start | bytes 147464 | tf_op jit(solution)/shard_map/ppermute | solution.py:28
  7.2 0.0 collective-permute-start.2
  7.2 1.7 %collective-permute-start.3 = (bf16[1,3,2,4096]{3,2,1,0:T(2,128)(2,1)S(1)}, bf16[1,3,2,4096]{3,2,1,0:T(2,128)(2,1)S(1)}, u32[]{:S(2)}, u32[]{:S(2)}) collective-permute-start(bf16[1,3,2,4096]{3,2,1,0:T(2,128)(2,1)S(1)} %maximum_bitcast_fusion), channel_id=1, source_target_pairs={{2,0},{0,2},{6,4},{4,6},{10,8},{8,10},{14,12},{12,14},{18,16},{16,... | collective-permute-start | bytes 147464 | tf_op jit(solution)/shard_map/ppermute | solution.py:28
  9.0 1.5 %collective-permute-start.5 = (bf16[1,3,2,4096]{3,2,1,0:T(2,128)(2,1)S(1)}, bf16[1,3,2,4096]{3,2,1,0:T(2,128)(2,1)S(1)}, u32[]{:S(2)}, u32[]{:S(2)}) collective-permute-start(bf16[1,3,2,4096]{3,2,1,0:T(2,128)(2,1)S(1)} %maximum_bitcast_fusion), channel_id=1, source_target_pairs={{4,0},{6,2},{0,4},{2,6},{12,8},{14,10},{8,12},{10,14},{20,16},{22,... | collective-permute-start | bytes 147464 | tf_op jit(solution)/shard_map/ppermute | solution.py:28
  10.5 0.8 %constant_dynamic-update-slice_fusion.12 = bf16[16,3,2,4096]{3,2,1,0:T(2,128)(2,1)S(1)} fusion(bf16[1,2,4096]{2,1,0:T(2,128)(2,1)} %bitcast.113, bf16[1,2,4096]{2,1,0:T(2,128)(2,1)} %bitcast.115, bf16[1,2,4096]{2,1,0:T(2,128)(2,1)} %bitcast.117), kind=kLoop, calls=%fused_computation.29 | loop fusion | flops 147455 | bytes 98304
  11.3 0.0 copy-start.1
  11.3 0.0 collective-permute-done
  11.3 0.3 collective-permute-start.7
  11.6 0.1 constant_dynamic-update-slice_fusion.2
  11.7 0.0 collective-permute-done.1
  11.7 0.1 constant_dynamic-update-slice_fusion.1
  11.8 1.4 %collective-permute-done.2 = bf16[1,3,2,4096]{3,2,1,0:T(2,128)(2,1)S(1)} collective-permute-done((bf16[1,3,2,4096]{3,2,1,0:T(2,128)(2,1)S(1)}, bf16[1,3,2,4096]{3,2,1,0:T(2,128)(2,1)S(1)}, u32[]{:S(2)}, u32[]{:S(2)}) %collective-permute-start.2) | collective-permute-done | bytes 49184 | tf_op jit(solution)/shard_map/ppermute | solution.py:28
  13.1 0.1 constant_dynamic-update-slice_fusion
  13.2 1.6 %collective-permute-start.4 = (bf16[3,3,2,4096]{3,2,1,0:T(2,128)(2,1)S(1)}, bf16[3,3,2,4096]{3,2,1,0:T(2,128)(2,1)S(1)}, u32[]{:S(2)}, u32[]{:S(2)}) collective-permute-start(bf16[3,3,2,4096]{3,2,1,0:T(2,128)(2,1)S(1)} %get-tuple-element.15), channel_id=1, source_target_pairs={{2,0},{0,2},{6,4},{4,6},{10,8},{8,10},{14,12},{12,14},{18,16},{16,... | collective-permute-start | bytes 442376 | tf_op jit(solution)/shard_map/ppermute | solution.py:28
  14.8 1.5 %collective-permute-start.6 = (bf16[3,3,2,4096]{3,2,1,0:T(2,128)(2,1)S(1)}, bf16[3,3,2,4096]{3,2,1,0:T(2,128)(2,1)S(1)}, u32[]{:S(2)}, u32[]{:S(2)}) collective-permute-start(bf16[3,3,2,4096]{3,2,1,0:T(2,128)(2,1)S(1)} %get-tuple-element.15), channel_id=1, source_target_pairs={{4,0},{6,2},{0,4},{2,6},{12,8},{14,10},{8,12},{10,14},{20,16},{22,... | collective-permute-start | bytes 442376 | tf_op jit(solution)/shard_map/ppermute | solution.py:28
  16.3 0.0 collective-permute-done.3
  16.3 0.5 %collective-permute-start.8 = (bf16[3,3,2,4096]{3,2,1,0:T(2,128)(2,1)S(1)}, bf16[3,3,2,4096]{3,2,1,0:T(2,128)(2,1)S(1)}, u32[]{:S(2)}, u32[]{:S(2)}) collective-permute-start(bf16[3,3,2,4096]{3,2,1,0:T(2,128)(2,1)S(1)} %get-tuple-element.15), channel_id=1, source_target_pairs={{6,0},{4,2},{2,4},{0,6},{14,8},{12,10},{10,12},{8,14},{22,16},{20,... | collective-permute-start | bytes 442376 | tf_op jit(solution)/shard_map/ppermute | solution.py:28
  16.8 2.8 %collective-permute-done.4 = bf16[3,3,2,4096]{3,2,1,0:T(2,128)(2,1)S(1)} collective-permute-done((bf16[3,3,2,4096]{3,2,1,0:T(2,128)(2,1)S(1)}, bf16[3,3,2,4096]{3,2,1,0:T(2,128)(2,1)S(1)}, u32[]{:S(2)}, u32[]{:S(2)}) %collective-permute-start.4) | collective-permute-done | bytes 147488 | tf_op jit(solution)/shard_map/ppermute | solution.py:28
  19.7 0.1 constant_dynamic-update-slice_fusion.7
  19.8 0.0 collective-permute-done.5
  19.8 2.6 %collective-permute-done.6 = bf16[3,3,2,4096]{3,2,1,0:T(2,128)(2,1)S(1)} collective-permute-done((bf16[3,3,2,4096]{3,2,1,0:T(2,128)(2,1)S(1)}, bf16[3,3,2,4096]{3,2,1,0:T(2,128)(2,1)S(1)}, u32[]{:S(2)}, u32[]{:S(2)}) %collective-permute-start.6) | collective-permute-done | bytes 147488 | tf_op jit(solution)/shard_map/ppermute | solution.py:28
  22.5 0.1 constant_dynamic-update-slice_fusion.5
  22.6 0.0 collective-permute-done.7
  22.6 0.0 collective-permute-done.8
  22.7 0.1 constant_dynamic-update-slice_fusion.3
  22.8 0.8 %fusion.67 = (bf16[16,1,2,4096]{3,2,1,0:T(2,128)(2,1)S(1)}, bf16[16,1,2,4096]{3,2,1,0:T(2,128)(2,1)S(1)}, bf16[16,1,2,4096]{3,2,1,0:T(2,128)(2,1)S(1)}) fusion(bf16[16,3,2,4096]{3,2,1,0:T(2,128)(2,1)S(1)} %constant_dynamic-update-slice_fusion.3), kind=kLoop, calls=%fused_computation.89 | loop fusion | bytes 1572864 | tf_op jit(solution)/shard_map/slice | solution.py:93
  23.5 0.1 reshape_squeeze.9
  23.7 0.1 reshape_squeeze.10
  23.8 0.0 copy-done.1
  23.8 0.3 fusion.4
  24.1 0.0 copy-done
  24.1 0.3 fusion.3
  24.4 0.3 fusion.2
  24.6 0.3 fusion.1
  24.9 0.1 reshape_squeeze.11
  25.0 1.7 %fusion = f32[5,32,128]{2,1,0:T(8,128)S(1)} fusion(f32[5,32,128]{2,1,0:T(8,128)S(1)} %fusion.1, bf16[32,4096]{1,0:T(8,128)(2,1)S(1)} %reshape_squeeze.11, bf16[128,4096]{1,0:T(8,128)(2,1)} %param.11), kind=kOutput, calls=%fused_computation.4 | convolution fusion | flops 33554432 | bytes 1327104 | tf_op jit(solution)/shard_map/dot_general | solution.py:68
  26.7 0.0 collective-permute-start.9
  26.7 1.3 %collective-permute-done.9 = f32[5,32,128]{2,1,0:T(8,128)S(1)} collective-permute-done((f32[5,32,128]{2,1,0:T(8,128)S(1)}, f32[5,32,128]{2,1,0:T(8,128)S(1)}, u32[]{:S(2)}, u32[]{:S(2)}) %collective-permute-start.9) | collective-permute-done | bytes 81952 | tf_op jit(solution)/shard_map/ppermute | solution.py:107
  28.0 0.4 fusion.43
  28.5 0.5 %fusion.45 = f32[4096,128]{1,0:T(8,128)S(1)} fusion(bf16[32,4096]{1,0:T(8,128)(2,1)S(1)} %reshape_squeeze.9, f32[5,32,128]{2,1,0:T(8,128)S(1)} %add.65), kind=kOutput, calls=%fused_computation.77 | convolution fusion | flops 33632256 | bytes 2441216 | tf_op jit(solution)/shard_map/dot_general | solution.py:62
  29.0 0.5 %fusion.37 = f32[4096,128]{1,0:T(8,128)S(1)} fusion(bf16[32,4096]{1,0:T(8,128)(2,1)S(1)} %reshape_squeeze.9, f32[5,32,128]{2,1,0:T(8,128)S(1)} %add.65), kind=kOutput, calls=%fused_computation.73 | convolution fusion | flops 33595392 | bytes 2408448 | tf_op jit(solution)/shard_map/dot_general | solution.py:62
  29.4 0.5 %fusion.70 = (bf16[32,4096]{1,0:T(8,128)(2,1)S(1)}, f32[32,4096]{1,0:T(8,128)S(1)}) fusion(f32[32,4096]{1,0:T(8,128)S(1)} %fusion.43, bf16[4096,128]{1,0:T(8,128)(2,1)S(1)} %copy-done, f32[5,32,128]{2,1,0:T(8,128)S(1)} %add.65), kind=kOutput, calls=%fused_computation.92 | convolution fusion | flops 33857536 | bytes 2408448 | tf_op jit(solution)/shard_map/dot_general | solution.py:68
  29.9 0.8 %collective-permute-start.12 = (bf16[8,4096]{1,0:T(8,128)(2,1)S(1)}, bf16[8,4096]{1,0:T(8,128)(2,1)S(1)}, u32[]{:S(2)}, u32[]{:S(2)}) collective-permute-start(bf16[8,4096]{1,0:T(8,128)(2,1)S(1)} %get-tuple-element.10), channel_id=1, source_target_pairs={{0,6},{2,4},{4,2},{6,0},{8,14},{10,12},{12,10},{14,8},{16,22},{18,... | collective-permute-start | bytes 196616 | tf_op jit(solution)/shard_map/ppermute | solution.py:33
  30.8 1.2 %collective-permute-start.11 = (bf16[8,4096]{1,0:T(8,128)(2,1)S(1)}, bf16[8,4096]{1,0:T(8,128)(2,1)S(1)}, u32[]{:S(2)}, u32[]{:S(2)}) collective-permute-start(bf16[8,4096]{1,0:T(8,128)(2,1)S(1)} %get-tuple-element.11), channel_id=1, source_target_pairs={{0,4},{2,6},{4,0},{6,2},{8,12},{10,14},{12,8},{14,10},{16,20},{18,... | collective-permute-start | bytes 196616 | tf_op jit(solution)/shard_map/ppermute | solution.py:33
  32.0 1.5 %collective-permute-start.10 = (bf16[8,4096]{1,0:T(8,128)(2,1)S(1)}, bf16[8,4096]{1,0:T(8,128)(2,1)S(1)}, u32[]{:S(2)}, u32[]{:S(2)}) collective-permute-start(bf16[8,4096]{1,0:T(8,128)(2,1)S(1)} %get-tuple-element.9), channel_id=1, source_target_pairs={{0,2},{2,0},{4,6},{6,4},{8,10},{10,8},{12,14},{14,12},{16,18},{18,... | collective-permute-start | bytes 196616 | tf_op jit(solution)/shard_map/ppermute | solution.py:33
  33.5 1.8 %convolution_add_fusion.1 = f32[4096,128]{1,0:T(8,128)} fusion(f32[4096,128]{1,0:T(8,128)S(1)} %fusion.45, bf16[32,4096]{1,0:T(8,128)(2,1)S(1)} %reshape_squeeze.10, f32[5,32,128]{2,1,0:T(8,128)S(1)} %add.65), kind=kOutput, calls=%fused_computation.1 | convolution fusion | flops 34119680 | bytes 4505600 | tf_op jit(solution)/shard_map/dot_general | solution.py:62
  35.3 1.8 %convolution_add_fusion = f32[4096,128]{1,0:T(8,128)} fusion(f32[4096,128]{1,0:T(8,128)S(1)} %fusion.37, bf16[32,4096]{1,0:T(8,128)(2,1)S(1)} %reshape_squeeze.10, f32[5,32,128]{2,1,0:T(8,128)S(1)} %add.65), kind=kOutput, calls=%fused_computation | convolution fusion | flops 34103296 | bytes 4489216 | tf_op jit(solution)/shard_map/dot_general | solution.py:62
  37.1 0.0 collective-permute-done.12
  37.1 0.0 collective-permute-done.11
  37.1 0.0 collective-permute-done.10
  37.2 2.6 %collective-permute-start.15 = (bf16[2,4096]{1,0:T(2,128)(2,1)S(1)}, bf16[2,4096]{1,0:T(2,128)(2,1)S(1)}, u32[]{:S(2)}, u32[]{:S(2)}) collective-permute-start(bf16[2,4096]{1,0:T(2,128)(2,1)S(1)} %get-tuple-element.13), channel_id=1, source_target_pairs={{0,24},{2,26},{4,28},{6,30},{8,16},{10,18},{12,20},{14,22},{16,8},... | collective-permute-start | bytes 49160 | tf_op jit(solution)/shard_map/ppermute | solution.py:33
  39.7 0.0 collective-permute-start.14
  39.7 1.9 %collective-permute-start.13 = (bf16[2,4096]{1,0:T(2,128)(2,1)S(1)}, bf16[2,4096]{1,0:T(2,128)(2,1)S(1)}, u32[]{:S(2)}, u32[]{:S(2)}) collective-permute-start(bf16[2,4096]{1,0:T(2,128)(2,1)S(1)} %get-tuple-element.12), channel_id=1, source_target_pairs={{0,8},{2,10},{4,12},{6,14},{8,0},{10,2},{12,4},{14,6},{16,24},{18,... | collective-permute-start | bytes 49160 | tf_op jit(solution)/shard_map/ppermute | solution.py:33
  41.6 1.8 %fusion.40 = f32[128,4096]{1,0:T(8,128)} fusion(bf16[32,4096]{1,0:T(8,128)(2,1)S(1)} %reshape_squeeze.11, f32[5,32,128]{2,1,0:T(8,128)S(1)} %add.65), kind=kOutput, calls=%fused_computation.75 | convolution fusion | flops 33607680 | bytes 2424832 | tf_op jit(solution)/shard_map/dot_general | solution.py:62
  43.4 0.0 collective-permute-done.15
  43.4 1.0 %collective-permute-done.14 = bf16[2,4096]{1,0:T(2,128)(2,1)S(1)} collective-permute-done((bf16[2,4096]{1,0:T(2,128)(2,1)S(1)}, bf16[2,4096]{1,0:T(2,128)(2,1)S(1)}, u32[]{:S(2)}, u32[]{:S(2)}) %collective-permute-start.14) | collective-permute-done | bytes 16416 | tf_op jit(solution)/shard_map/ppermute | solution.py:33
  44.4 0.0 collective-permute-done.13
  44.4 0.6 %fusion.9 = bf16[2,4096]{1,0:T(2,128)(2,1)} fusion(bf16[2,4096]{1,0:T(2,128)(2,1)S(1)} %collective-permute-done.15, bf16[2,4096]{1,0:T(2,128)(2,1)S(1)} %collective-permute-done.14, bf16[2,4096]{1,0:T(2,128)(2,1)S(1)} %collective-permute-done.13, f32[8,4096]{1,0:T(8,128)S(1)} %get-tuple-element.5), kind=kLoop, calls=%fused_computation.33 | loop fusion | flops 57344 | bytes 98304 | tf_op jit(solution)/shard_map/convert_element_type | solution.py:113
  (7 shorter events, 0.2 us)
Async XLA Ops:
  0.6 23.4 %copy-start = (bf16[4096,128]{1,0:T(8,128)(2,1)S(1)}, bf16[4096,128]{1,0:T(8,128)(2,1)}, u32[]{:S(2)}) copy-start(bf16[4096,128]{1,0:T(8,128)(2,1)} %param.10) | copy-start | bytes 3145732
  1.6 9.7 %collective-permute-start = (bf16[1,3,2,4096]{3,2,1,0:T(2,128)(2,1)S(1)}, bf16[1,3,2,4096]{3,2,1,0:T(2,128)(2,1)S(1)}, u32[]{:S(2)}, u32[]{:S(2)}) collective-permute-start(bf16[1,3,2,4096]{3,2,1,0:T(2,128)(2,1)S(1)} %maximum_bitcast_fusion), channel_id=1, source_target_pairs={{8,0},{10,2},{12,4},{14,6},{0,8},{2,10},{4,12},{6,14},{24,16},{26,... | collective-permute-start | bytes 147464 | tf_op jit(solution)/shard_map/ppermute | solution.py:28
  4.7 7.0 %collective-permute-start.1 = (bf16[1,3,2,4096]{3,2,1,0:T(2,128)(2,1)S(1)}, bf16[1,3,2,4096]{3,2,1,0:T(2,128)(2,1)S(1)}, u32[]{:S(2)}, u32[]{:S(2)}) collective-permute-start(bf16[1,3,2,4096]{3,2,1,0:T(2,128)(2,1)S(1)} %maximum_bitcast_fusion), channel_id=1, source_target_pairs={{16,0},{18,2},{20,4},{22,6},{24,8},{26,10},{28,12},{30,14},{0,16},... | collective-permute-start | bytes 147464 | tf_op jit(solution)/shard_map/ppermute | solution.py:28
  7.2 5.9 %collective-permute-start.2 = (bf16[1,3,2,4096]{3,2,1,0:T(2,128)(2,1)S(1)}, bf16[1,3,2,4096]{3,2,1,0:T(2,128)(2,1)S(1)}, u32[]{:S(2)}, u32[]{:S(2)}) collective-permute-start(bf16[1,3,2,4096]{3,2,1,0:T(2,128)(2,1)S(1)} %maximum_bitcast_fusion), channel_id=1, source_target_pairs={{24,0},{26,2},{28,4},{30,6},{16,8},{18,10},{20,12},{22,14},{8,16},... | collective-permute-start | bytes 147464 | tf_op jit(solution)/shard_map/ppermute | solution.py:28
  7.2 9.0 %collective-permute-start.3 = (bf16[1,3,2,4096]{3,2,1,0:T(2,128)(2,1)S(1)}, bf16[1,3,2,4096]{3,2,1,0:T(2,128)(2,1)S(1)}, u32[]{:S(2)}, u32[]{:S(2)}) collective-permute-start(bf16[1,3,2,4096]{3,2,1,0:T(2,128)(2,1)S(1)} %maximum_bitcast_fusion), channel_id=1, source_target_pairs={{2,0},{0,2},{6,4},{4,6},{10,8},{8,10},{14,12},{12,14},{18,16},{16,... | collective-permute-start | bytes 147464 | tf_op jit(solution)/shard_map/ppermute | solution.py:28
  9.0 10.8 %collective-permute-start.5 = (bf16[1,3,2,4096]{3,2,1,0:T(2,128)(2,1)S(1)}, bf16[1,3,2,4096]{3,2,1,0:T(2,128)(2,1)S(1)}, u32[]{:S(2)}, u32[]{:S(2)}) collective-permute-start(bf16[1,3,2,4096]{3,2,1,0:T(2,128)(2,1)S(1)} %maximum_bitcast_fusion), channel_id=1, source_target_pairs={{4,0},{6,2},{0,4},{2,6},{12,8},{14,10},{8,12},{10,14},{20,16},{22,... | collective-permute-start | bytes 147464 | tf_op jit(solution)/shard_map/ppermute | solution.py:28
  11.3 12.5 %copy-start.1 = (bf16[4096,128]{1,0:T(8,128)(2,1)S(1)}, bf16[4096,128]{1,0:T(8,128)(2,1)}, u32[]{:S(2)}) copy-start(bf16[4096,128]{1,0:T(8,128)(2,1)} %param.9) | copy-start | bytes 3145732
  11.3 11.3 %collective-permute-start.7 = (bf16[1,3,2,4096]{3,2,1,0:T(2,128)(2,1)S(1)}, bf16[1,3,2,4096]{3,2,1,0:T(2,128)(2,1)S(1)}, u32[]{:S(2)}, u32[]{:S(2)}) collective-permute-start(bf16[1,3,2,4096]{3,2,1,0:T(2,128)(2,1)S(1)} %maximum_bitcast_fusion), channel_id=1, source_target_pairs={{6,0},{4,2},{2,4},{0,6},{14,8},{12,10},{10,12},{8,14},{22,16},{20,... | collective-permute-start | bytes 147464 | tf_op jit(solution)/shard_map/ppermute | solution.py:28
  13.2 6.4 %collective-permute-start.4 = (bf16[3,3,2,4096]{3,2,1,0:T(2,128)(2,1)S(1)}, bf16[3,3,2,4096]{3,2,1,0:T(2,128)(2,1)S(1)}, u32[]{:S(2)}, u32[]{:S(2)}) collective-permute-start(bf16[3,3,2,4096]{3,2,1,0:T(2,128)(2,1)S(1)} %get-tuple-element.15), channel_id=1, source_target_pairs={{2,0},{0,2},{6,4},{4,6},{10,8},{8,10},{14,12},{12,14},{18,16},{16,... | collective-permute-start | bytes 442376 | tf_op jit(solution)/shard_map/ppermute | solution.py:28
  14.8 7.7 %collective-permute-start.6 = (bf16[3,3,2,4096]{3,2,1,0:T(2,128)(2,1)S(1)}, bf16[3,3,2,4096]{3,2,1,0:T(2,128)(2,1)S(1)}, u32[]{:S(2)}, u32[]{:S(2)}) collective-permute-start(bf16[3,3,2,4096]{3,2,1,0:T(2,128)(2,1)S(1)} %get-tuple-element.15), channel_id=1, source_target_pairs={{4,0},{6,2},{0,4},{2,6},{12,8},{14,10},{8,12},{10,14},{20,16},{22,... | collective-permute-start | bytes 442376 | tf_op jit(solution)/shard_map/ppermute | solution.py:28
  16.3 6.4 %collective-permute-start.8 = (bf16[3,3,2,4096]{3,2,1,0:T(2,128)(2,1)S(1)}, bf16[3,3,2,4096]{3,2,1,0:T(2,128)(2,1)S(1)}, u32[]{:S(2)}, u32[]{:S(2)}) collective-permute-start(bf16[3,3,2,4096]{3,2,1,0:T(2,128)(2,1)S(1)} %get-tuple-element.15), channel_id=1, source_target_pairs={{6,0},{4,2},{2,4},{0,6},{14,8},{12,10},{10,12},{8,14},{22,16},{20,... | collective-permute-start | bytes 442376 | tf_op jit(solution)/shard_map/ppermute | solution.py:28
  26.7 1.3 %collective-permute-start.9 = (f32[5,32,128]{2,1,0:T(8,128)S(1)}, f32[5,32,128]{2,1,0:T(8,128)S(1)}, u32[]{:S(2)}, u32[]{:S(2)}) collective-permute-start(f32[5,32,128]{2,1,0:T(8,128)S(1)} %fusion), channel_id=1, source_target_pairs={{0,1},{1,0},{2,3},{3,2},{4,5},{5,4},{6,7},{7,6},{8,9},{9,8},{10,11... | collective-permute-start | bytes 245768 | tf_op jit(solution)/shard_map/ppermute | solution.py:107
  29.9 7.1 %collective-permute-start.12 = (bf16[8,4096]{1,0:T(8,128)(2,1)S(1)}, bf16[8,4096]{1,0:T(8,128)(2,1)S(1)}, u32[]{:S(2)}, u32[]{:S(2)}) collective-permute-start(bf16[8,4096]{1,0:T(8,128)(2,1)S(1)} %get-tuple-element.10), channel_id=1, source_target_pairs={{0,6},{2,4},{4,2},{6,0},{8,14},{10,12},{12,10},{14,8},{16,22},{18,... | collective-permute-start | bytes 196616 | tf_op jit(solution)/shard_map/ppermute | solution.py:33
  30.8 6.3 %collective-permute-start.11 = (bf16[8,4096]{1,0:T(8,128)(2,1)S(1)}, bf16[8,4096]{1,0:T(8,128)(2,1)S(1)}, u32[]{:S(2)}, u32[]{:S(2)}) collective-permute-start(bf16[8,4096]{1,0:T(8,128)(2,1)S(1)} %get-tuple-element.11), channel_id=1, source_target_pairs={{0,4},{2,6},{4,0},{6,2},{8,12},{10,14},{12,8},{14,10},{16,20},{18,... | collective-permute-start | bytes 196616 | tf_op jit(solution)/shard_map/ppermute | solution.py:33
  32.0 5.1 %collective-permute-start.10 = (bf16[8,4096]{1,0:T(8,128)(2,1)S(1)}, bf16[8,4096]{1,0:T(8,128)(2,1)S(1)}, u32[]{:S(2)}, u32[]{:S(2)}) collective-permute-start(bf16[8,4096]{1,0:T(8,128)(2,1)S(1)} %get-tuple-element.9), channel_id=1, source_target_pairs={{0,2},{2,0},{4,6},{6,4},{8,10},{10,8},{12,14},{14,12},{16,18},{18,... | collective-permute-start | bytes 196616 | tf_op jit(solution)/shard_map/ppermute | solution.py:33
  37.2 6.3 %collective-permute-start.15 = (bf16[2,4096]{1,0:T(2,128)(2,1)S(1)}, bf16[2,4096]{1,0:T(2,128)(2,1)S(1)}, u32[]{:S(2)}, u32[]{:S(2)}) collective-permute-start(bf16[2,4096]{1,0:T(2,128)(2,1)S(1)} %get-tuple-element.13), channel_id=1, source_target_pairs={{0,24},{2,26},{4,28},{6,30},{8,16},{10,18},{12,20},{14,22},{16,8},... | collective-permute-start | bytes 49160 | tf_op jit(solution)/shard_map/ppermute | solution.py:33
  39.7 4.6 %collective-permute-start.14 = (bf16[2,4096]{1,0:T(2,128)(2,1)S(1)}, bf16[2,4096]{1,0:T(2,128)(2,1)S(1)}, u32[]{:S(2)}, u32[]{:S(2)}) collective-permute-start(bf16[2,4096]{1,0:T(2,128)(2,1)S(1)} %get-tuple-element.14), channel_id=1, source_target_pairs={{0,16},{2,18},{4,20},{6,22},{8,24},{10,26},{12,28},{14,30},{16,0},... | collective-permute-start | bytes 49160 | tf_op jit(solution)/shard_map/ppermute | solution.py:33
  39.7 4.6 %collective-permute-start.13 = (bf16[2,4096]{1,0:T(2,128)(2,1)S(1)}, bf16[2,4096]{1,0:T(2,128)(2,1)S(1)}, u32[]{:S(2)}, u32[]{:S(2)}) collective-permute-start(bf16[2,4096]{1,0:T(2,128)(2,1)S(1)} %get-tuple-element.12), channel_id=1, source_target_pairs={{0,8},{2,10},{4,12},{6,14},{8,0},{10,2},{12,4},{14,6},{16,24},{18,... | collective-permute-start | bytes 49160 | tf_op jit(solution)/shard_map/ppermute | solution.py:33

commit v3 on v2

v3 whole, which is shorter than its diff:
```python
import functools

import jax
import jax.numpy as jnp
from jax import lax
from jax.experimental import pallas as pl
from jax.experimental.pallas import tpu as pltpu
from jax.sharding import PartitionSpec as P

SLOTS = 4
LANES = 128


def levels_of(size):
    levels, stride = [], 1
    while stride < size:
        rest = size // stride
        radix = next(r for r in (4, 2, 3, 5, 7, rest) if rest % r == 0)
        levels.append((stride, radix))
        stride *= radix
    return levels[::-1]


def partner(index, stride, radix, offset):
    digit = index // stride % radix
    if radix & (radix - 1) == 0:
        other = digit ^ offset
    else:
        other = (digit + offset) % radix
    return index + (other - digit) * stride


def fetch(value, axis, size, level, offset):
    pairs = [(partner(i, *level, offset), i) for i in range(size)]
    return lax.ppermute(value, axis, pairs)


def deliver(value, axis, size, level, offset):
    pairs = [(i, partner(i, *level, offset)) for i in range(size)]
    return lax.ppermute(value, axis, pairs)


def gather_blocks(own, axis, size):
    rest = []
    for level in levels_of(size):
        offsets = range(level[1] - 1, 0, -1)
        held = jnp.concatenate(rest) if rest else None
        mine = {o: [fetch(own, axis, size, level, o)] for o in offsets}
        if rest:
            for o in offsets:
                mine[o].append(fetch(held, axis, size, level, o))
        rest = ([held] if rest else []) + sum((mine[o] for o in offsets[::-1]), [])
    return [own] + rest


def scatter_sum(groups, axis, size):
    for level in levels_of(size)[::-1]:
        if len(groups) == 1:
            groups = jnp.split(groups[0], level[1])
        total = groups[0]
        for o in range(1, level[1]):
            sent = groups[o].astype(jnp.bfloat16)
            total = total + deliver(sent, axis, size, level, o).astype(jnp.float32)
        groups = [total]
    return groups[0]


def fold_kernel(*refs):
    *rows, out = refs
    for k, ref in enumerate(rows):
        tokens, width = ref.shape
        split = ref[...].reshape(tokens, width // (SLOTS * LANES), SLOTS, LANES)
        for s in range(SLOTS):
            at = (k * SLOTS + s) * tokens
            out[0, at : at + tokens] = split[:, :, s].reshape(tokens, width // SLOTS)


def fold(*rows):
    tokens, width = rows[0].shape
    shape = (1, len(rows) * SLOTS * tokens, width // SLOTS)
    vmem = pl.BlockSpec(memory_space=pltpu.VMEM)
    return pl.pallas_call(
        fold_kernel,
        out_shape=jax.ShapeDtypeStruct(shape, rows[0].dtype),
        in_specs=[vmem] * len(rows),
        out_specs=vmem,
    )(*rows)


def unfold(rows):
    tokens = rows.shape[0] // SLOTS
    split = rows.reshape(SLOTS, tokens, rows.shape[1] // LANES, LANES)
    return split.transpose(1, 2, 0, 3).reshape(tokens, rows.shape[1] * SLOTS)


def slot_of(shape, axis):
    return lax.broadcasted_iota(jnp.int32, shape, axis) // 2


def rows_for_slot(weight, slot):
    height, width = weight.shape
    split = weight.reshape(height // (SLOTS * LANES), SLOTS, LANES, width)
    return split[:, slot].reshape(height // SLOTS, width)


def over_slots(x):
    axis = x.ndim - 2
    x = x + pltpu.roll(x, 4, axis)
    return x + pltpu.roll(x, 2, axis)


def pick_slots(parts):
    slot = slot_of(parts[0].shape, parts[0].ndim - 2)
    result = parts[0]
    for s in range(1, SLOTS):
        result = jnp.where(slot == s, parts[s], result)
    return result


def only_slot(x, s):
    return jnp.where(slot_of(x.shape, x.ndim - 2) == s, x, 0.0)


def forward_kernel(n_pieces, *refs):
    pieces, (gate_w, up_w, down_w), (pt_out, c_out, parts_out) = (
        refs[:n_pieces],
        refs[n_pieces : n_pieces + 3],
        refs[n_pieces + 3 :],
    )
    start = 0
    for piece in pieces:
        count = piece.shape[0]
        for i in range(count):
            at = start + i
            pt_out[at * 16 : at * 16 + 16] = piece[i, 0:16]
            c_out[at * 8 : at * 8 + 8] = piece[i, 16:24]
        start += count
    blocks = start
    pt = pt_out[...]
    cot = c_out[...]
    hidden = gate_w.shape[1]
    acts, dacts = [], []
    for s in range(SLOTS):
        weights = jnp.concatenate(
            [rows_for_slot(gate_w[...], s), rows_for_slot(up_w[...], s)], axis=1
        )
        acts.append(
            jnp.dot(pt, weights, preferred_element_type=jnp.float32).reshape(
                2 * blocks, 8, 2 * hidden
            )
        )
        columns = [
            down_w[:, j * LANES : (j + 1) * LANES]
            for j in range(s, down_w.shape[1] // LANES, SLOTS)
        ]
        dacts.append(
            lax.dot_general(
                cot,
                jnp.concatenate(columns, axis=1),
                (((1,), (1,)), ((), ())),
                preferred_element_type=jnp.float32,
            ).reshape(blocks, 8, hidden)
        )
    act = over_slots(pick_slots(acts)).reshape(blocks, 2, 8, 2 * hidden)
    parts_out[0] = pick_slots(
        [
            act[:, 0, :, :hidden],
            act[:, 0, :, hidden:],
            act[:, 1, :, :hidden],
            act[:, 1, :, hidden:],
        ]
    )
    parts_out[1] = over_slots(pick_slots(dacts))


def forward(pieces, gate_w, up_w, down_w):
    blocks = sum(p.shape[0] for p in pieces)
    lanes, hidden = pieces[0].shape[2], gate_w.shape[1]
    vmem = pl.BlockSpec(memory_space=pltpu.VMEM)
    return pl.pallas_call(
        functools.partial(forward_kernel, len(pieces)),
        out_shape=(
            jax.ShapeDtypeStruct((blocks * 16, lanes), jnp.bfloat16),
            jax.ShapeDtypeStruct((blocks * 8, lanes), jnp.bfloat16),
            jax.ShapeDtypeStruct((2, blocks, 8, hidden), jnp.float32),
        ),
        in_specs=[vmem] * (len(pieces) + 3),
        out_specs=(vmem,) * 3,
        compiler_params=pltpu.CompilerParams(vmem_limit_bytes=40 * 2**20),
    )(*pieces, gate_w, up_w, down_w)


def factors(gate, up, tgate, tup, dact):
    sig = 1.0 / (1.0 + jnp.exp(-gate))
    act = gate * sig
    first = sig * (1.0 + gate * (1.0 - sig))
    second = sig * (1.0 - sig) * (2.0 + gate * (1.0 - 2.0 * sig))
    dgate = dact * up * first
    dup = dact * act
    tdgate = dact * (tup * first + up * second * tgate)
    tdup = dact * first * tgate
    tact = tgate * first * up + act * tup
    return (dgate, dup, tdgate, tdup, tact)


def middle_kernel(n_parts, groups, *refs):
    parts, (gate_w, up_w) = refs[:n_parts], refs[n_parts : n_parts + 2]
    factor_out, tact_out = refs[n_parts + 2 : n_parts + 4]
    own_out, others_out = refs[n_parts + 4], refs[n_parts + 5 :]
    packed, dact = (sum(p[k] for p in parts[1:]) + parts[0][k] for k in range(2))
    gate, up, tgate, tup = (over_slots(only_slot(packed, s)) for s in range(SLOTS))
    dgate, dup, tdgate, tdup, tact = factors(gate, up, tgate, tup, dact)
    blocks, _, hidden = gate.shape
    second = jnp.concatenate([tdgate, tdup], axis=2)
    factor_out[...] = (
        jnp.stack([second, jnp.concatenate([dgate, dup], axis=2)], axis=1)
        .reshape(blocks * 16, 2 * hidden)
        .astype(jnp.bfloat16)
    )
    tact_out[...] = tact.reshape(blocks * 8, hidden).astype(jnp.bfloat16)
    left = jnp.concatenate(
        [
            only_slot(second, s).reshape(blocks * 8, 2 * hidden).astype(jnp.bfloat16)
            for s in range(SLOTS)
        ],
        axis=1,
    )
    right = jnp.concatenate(
        [rows_for_slot(w[...], s) for s in range(SLOTS) for w in (gate_w, up_w)], axis=1
    )
    hvp = lax.dot_general(
        left, right, (((1,), (1,)), ((), ())), preferred_element_type=jnp.float32
    )
    hvp = hvp.reshape(groups, blocks // groups, 8, hvp.shape[1])
    own_out[...] = hvp[0]
    for g, out in enumerate(others_out):
        out[...] = hvp[g + 1].astype(out.dtype)


def middle(parts, gate_w, up_w, groups):
    _, blocks, _, hidden = parts[0].shape
    lanes = gate_w.shape[0] // SLOTS
    vmem = pl.BlockSpec(memory_space=pltpu.VMEM)
    group = (blocks // groups, 8, lanes)
    return pl.pallas_call(
        functools.partial(middle_kernel, len(parts), groups),
        out_shape=(
            jax.ShapeDtypeStruct((blocks * 16, 2 * hidden), jnp.bfloat16),
            jax.ShapeDtypeStruct((blocks * 8, hidden), jnp.bfloat16),
            jax.ShapeDtypeStruct(group, jnp.float32),
        )
        + (jax.ShapeDtypeStruct(group, jnp.bfloat16),) * (groups - 1),
        in_specs=[vmem] * (len(parts) + 2),
        out_specs=(vmem,) * (groups + 2),
        compiler_params=pltpu.CompilerParams(vmem_limit_bytes=40 * 2**20),
    )(*parts, gate_w, up_w)


def only_slot_rows(x, s):
    rows = lax.broadcasted_iota(jnp.int32, x.shape, 0)
    return jnp.where(rows % 8 // 2 == s, x.astype(jnp.float32), 0.0).astype(x.dtype)


def contract_first(left, right):
    return lax.dot_general(
        left, right, (((0,), (0,)), ((), ())), preferred_element_type=jnp.float32
    )


def grads_kernel(pt, cot, factor, tact, gate_out, up_out, down_out):
    hidden = tact.shape[1]
    for s in range(SLOTS):
        both = contract_first(pt[...], only_slot_rows(factor[...], s))
        gate_out[s * LANES : (s + 1) * LANES] = both[:, :hidden]
        up_out[s * LANES : (s + 1) * LANES] = both[:, hidden:]
        down_out[:, s * LANES : (s + 1) * LANES] = contract_first(
            only_slot_rows(tact[...], s), cot[...]
        )


def grads(pt, cot, factor, tact):
    hidden = tact.shape[1]
    tiles = pt.shape[1] // LANES
    width = tiles * SLOTS * LANES
    wide = SLOTS * LANES
    up = jax.ShapeDtypeStruct((width, hidden), jnp.float32)
    return pl.pallas_call(
        grads_kernel,
        grid=(tiles,),
        out_shape=(up, up, jax.ShapeDtypeStruct((hidden, width), jnp.float32)),
        in_specs=[
            pl.BlockSpec((pt.shape[0], LANES), lambda m: (0, m)),
            pl.BlockSpec((cot.shape[0], LANES), lambda m: (0, m)),
            pl.BlockSpec(factor.shape, lambda m: (0, 0)),
            pl.BlockSpec(tact.shape, lambda m: (0, 0)),
        ],
        out_specs=(
            pl.BlockSpec((wide, hidden), lambda m: (m, 0)),
            pl.BlockSpec((wide, hidden), lambda m: (m, 0)),
            pl.BlockSpec((hidden, wide), lambda m: (0, m)),
        ),
        compiler_params=pltpu.CompilerParams(vmem_limit_bytes=40 * 2**20),
    )(pt, cot, factor, tact)


def solution(mesh):
    wide, narrow = mesh.shape["wide"], mesh.shape["narrow"]

    def local(primal_in, tangent_in, cotangent, gate_weight, up_weight, down_weight):
        pieces = gather_blocks(fold(primal_in, tangent_in, cotangent), "wide", wide)
        pt, cot, part = forward(pieces, gate_weight, up_weight, down_weight)
        parts = [part]
        for shift in range(1, narrow):
            pairs = [(i, (i + shift) % narrow) for i in range(narrow)]
            parts.append(lax.ppermute(part, "narrow", pairs))
        groups = levels_of(wide)[-1][1]
        factor, tact, *hvp = middle(parts, gate_weight, up_weight, groups)
        total = scatter_sum(hvp, "wide", wide)
        input_hvp = unfold(total[0].astype(jnp.bfloat16))
        return (input_hvp, *grads(pt, cot, factor, tact))

    return jax.shard_map(
        local,
        mesh=mesh,
        in_specs=(
            P("wide", "narrow"),
            P("wide", "narrow"),
            P("wide", "narrow"),
            P("narrow", "wide"),
            P("narrow", "wide"),
            P("wide", "narrow"),
        ),
        out_specs=(
            P("wide", "narrow"),
            P("narrow", "wide"),
            P("narrow", "wide"),
            P("wide", "narrow"),
        ),
        check_vma=False,
    )
```

time: 45.4 us -> 53.3 us (1.17)
  matrix products: 10 us -> 0 us
  waiting for transfers between devices: 9.07 us -> 18.4 us
  Pallas kernels: 0 us -> 8.58 us
  local copies, waits for them, and re-layouts: 1.84 us -> 5.12 us
  other arithmetic: 2.4 us -> 0.05 us
  starting transfers between devices: 20.8 us -> 20.1 us
    dot_general x12 -> x0, matrix products: 10 us -> none  [the longest x5 6.33 us: contract_first(): lax.dot_general(left, right, (((0,), (0,)), ((), ())), preferred_element_...]
    pallas_call x0 -> x4, Pallas kernels: none -> 8.58 us  [the longest x1 5.3 us: grads(): pl.pallas_call(grads_kernel, grid=(tiles,), out_shape=(up, up, jax.ShapeD...]
    ppermute x9, waiting for transfers between devices: 6.84 us -> 13 us  [fetch(): return lax.ppermute(value, axis, pairs)]
    unnamed x11 -> x15, local copies, waits for them, and re-layouts: 0.53 us -> 4.49 us
    ppermute x6, waiting for transfers between devices: 0.96 us -> 4.04 us  [deliver(): return lax.ppermute(value, axis, pairs)]
    broadcast_in_dim x1 -> x0, other arithmetic: 0.92 us -> none  [local(): block = jnp.stack([primal_in, tangent_in, cotangent])[None]]
    ppermute x6, starting transfers between devices: 8.01 us -> 7.11 us  [deliver(): return lax.ppermute(value, axis, pairs)]
    unnamed x1, other arithmetic: 0.8 us -> 0.01 us
  transfers between devices with their start and end apart: 16 -> 16, of which waited for: 5 -> 7; matrix products, arithmetic and copies ran while one was open for 15% -> 0% of each run, Pallas kernels for 0% -> 10%
where the time goes in v3:
time: 53.3 us; the launch traced here: 53 us
  starting transfers between devices  20.1 us (38%)
  waiting for transfers between devices  18.4 us (35%)
  Pallas kernels  8.58 us (16%)
  local copies, waits for them, and re-layouts  5.12 us (10%)
  between operations  0.74 us (1%)
    ppermute x9, waiting for transfers between devices, fetch(): return lax.ppermute(value, axis, pairs)  13 us
    ppermute x9, starting transfers between devices, fetch(): return lax.ppermute(value, axis, pairs)  12.9 us
    ppermute x6, starting transfers between devices, deliver(): return lax.ppermute(value, axis, pairs)  7.11 us
    pallas_call x1, Pallas kernels, grads(): pl.pallas_call(grads_kernel, grid=(tiles,), out_shape=(up, up, jax.ShapeD...  5.3 us
    unnamed x15, local copies, waits for them, and re-layouts  4.49 us
    ppermute x6, waiting for transfers between devices, deliver(): return lax.ppermute(value, axis, pairs)  4.04 us
    pallas_call x1, Pallas kernels, fold(): pl.pallas_call(fold_kernel, out_shape=jax.ShapeDtypeStruct(shape, rows[0]...  1.45 us
    ppermute x1, waiting for transfers between devices, local(): parts.append(lax.ppermute(part, 'narrow', pairs))  1.33 us
  transfers between devices with their start and end apart: 16, of which 7 were waited for; matrix products, arithmetic and copies ran while one was open for 0% of the time, Pallas kernels for 10%

profile of v3, /device:TPU:0, one launch (start us, length us, event | category | flops | bytes accessed | tf_op | source)
XLA Modules:
  0.0 53.0 jit_solution(4481684944567189251)
XLA Ops:
  0.6 1.4 %shard_map.93.refs_0_ = bf16[1,24,1024]{2,1,0:T(8,128)(2,1)} custom-call(bf16[2,4096]{1,0:T(2,128)(2,1)} %refs_0_.1, bf16[2,4096]{1,0:T(2,128)(2,1)} %refs_1_.1, bf16[2,4096]{1,0:T(2,128)(2,1)} %refs_2_.2), custom_call_target="tpu_custom_call" | custom-call | tf_op jit(solution)/shard_map/pallas_call | solution.py:82
  2.1 3.0 %collective-permute-start = (bf16[1,24,1024]{2,1,0:T(8,128)(2,1)}, bf16[1,24,1024]{2,1,0:T(8,128)(2,1)S(1)}, u32[]{:S(2)}, u32[]{:S(2)}) collective-permute-start(bf16[1,24,1024]{2,1,0:T(8,128)(2,1)} %shard_map.93.refs_0_), channel_id=1, source_target_pairs={{8,0},{10,2},{12,4},{14,6},{0,8},{2,10},{4,12},{6,14},{24,16},{26,... | collective-permute-start | bytes 147464 | tf_op jit(solution)/shard_map/ppermute | solution.py:35
  5.1 2.5 %collective-permute-start.2 = (bf16[1,24,1024]{2,1,0:T(8,128)(2,1)}, bf16[1,24,1024]{2,1,0:T(8,128)(2,1)S(1)}, u32[]{:S(2)}, u32[]{:S(2)}) collective-permute-start(bf16[1,24,1024]{2,1,0:T(8,128)(2,1)} %shard_map.93.refs_0_), channel_id=1, source_target_pairs={{24,0},{26,2},{28,4},{30,6},{16,8},{18,10},{20,12},{22,14},{8,16},... | collective-permute-start | bytes 147464 | tf_op jit(solution)/shard_map/ppermute | solution.py:35
  7.6 0.1 collective-permute-start.1
  7.7 0.0 collective-permute-done
  7.7 5.6 %collective-permute-done.1 = bf16[1,24,1024]{2,1,0:T(8,128)(2,1)S(1)} collective-permute-done((bf16[1,24,1024]{2,1,0:T(8,128)(2,1)}, bf16[1,24,1024]{2,1,0:T(8,128)(2,1)S(1)}, u32[]{:S(2)}, u32[]{:S(2)}) %collective-permute-start.1) | collective-permute-done | bytes 49184 | tf_op jit(solution)/shard_map/ppermute | solution.py:35
  13.3 0.0 collective-permute-done.2
  13.3 2.5 %collective-permute-start.8 = (bf16[3,24,1024]{2,1,0:T(8,128)(2,1)S(1)}, bf16[3,24,1024]{2,1,0:T(8,128)(2,1)S(1)}, u32[]{:S(2)}, u32[]{:S(2)}) collective-permute-start(bf16[3,24,1024]{2,1,0:T(8,128)(2,1)S(1)} %constant_dynamic-update-slice_fusion.refs_1_), channel_id=1, source_target_pairs={{6,0},{4,2},{2,4},{0,6},{14,8},{12,10},{10,12},{8,14},{22,16},{20,... | collective-permute-start | bytes 442376 | tf_op jit(solution)/shard_map/ppermute | solution.py:35
  15.8 0.5 collective-permute-start.6
  16.3 0.5 %collective-permute-start.4 = (bf16[3,24,1024]{2,1,0:T(8,128)(2,1)S(1)}, bf16[3,24,1024]{2,1,0:T(8,128)(2,1)S(1)}, u32[]{:S(2)}, u32[]{:S(2)}) collective-permute-start(bf16[3,24,1024]{2,1,0:T(8,128)(2,1)S(1)} %constant_dynamic-update-slice_fusion.refs_1_), channel_id=1, source_target_pairs={{2,0},{0,2},{6,4},{4,6},{10,8},{8,10},{14,12},{12,14},{18,16},{16,... | collective-permute-start | bytes 442376 | tf_op jit(solution)/shard_map/ppermute | solution.py:35
  16.9 2.4 %collective-permute-start.7 = (bf16[1,24,1024]{2,1,0:T(8,128)(2,1)}, bf16[1,24,1024]{2,1,0:T(8,128)(2,1)S(1)}, u32[]{:S(2)}, u32[]{:S(2)}) collective-permute-start(bf16[1,24,1024]{2,1,0:T(8,128)(2,1)} %shard_map.93.refs_0_), channel_id=1, source_target_pairs={{6,0},{4,2},{2,4},{0,6},{14,8},{12,10},{10,12},{8,14},{22,16},{20,... | collective-permute-start | bytes 147464 | tf_op jit(solution)/shard_map/ppermute | solution.py:35
  19.3 0.5 collective-permute-start.5
  19.8 3.9 %collective-permute-done.7.refs_6_ = bf16[1,24,1024]{2,1,0:T(8,128)(2,1)S(1)} collective-permute-done((bf16[1,24,1024]{2,1,0:T(8,128)(2,1)}, bf16[1,24,1024]{2,1,0:T(8,128)(2,1)S(1)}, u32[]{:S(2)}, u32[]{:S(2)}) %collective-permute-start.7) | collective-permute-done | bytes 49184 | tf_op jit(solution)/shard_map/ppermute | solution.py:35
  23.8 0.8 %collective-permute-start.3 = (bf16[1,24,1024]{2,1,0:T(8,128)(2,1)}, bf16[1,24,1024]{2,1,0:T(8,128)(2,1)S(1)}, u32[]{:S(2)}, u32[]{:S(2)}) collective-permute-start(bf16[1,24,1024]{2,1,0:T(8,128)(2,1)} %shard_map.93.refs_0_), channel_id=1, source_target_pairs={{2,0},{0,2},{6,4},{4,6},{10,8},{8,10},{14,12},{12,14},{18,16},{16,... | collective-permute-start | bytes 147464 | tf_op jit(solution)/shard_map/ppermute | solution.py:35
  24.6 0.0 collective-permute-done.5.refs_4_
  24.6 3.5 %collective-permute-done.3.refs_2_ = bf16[1,24,1024]{2,1,0:T(8,128)(2,1)S(1)} collective-permute-done((bf16[1,24,1024]{2,1,0:T(8,128)(2,1)}, bf16[1,24,1024]{2,1,0:T(8,128)(2,1)S(1)}, u32[]{:S(2)}, u32[]{:S(2)}) %collective-permute-start.3) | collective-permute-done | bytes 49184 | tf_op jit(solution)/shard_map/ppermute | solution.py:35
  28.1 0.0 collective-permute-done.8.refs_7_
  28.1 0.0 collective-permute-done.6.refs_5_
  28.1 0.0 collective-permute-done.4.refs_3_
  28.1 0.0 copy-start
  28.1 1.2 %copy-done = bf16[4096,128]{1,0:T(8,128)(2,1)S(1)} copy-done((bf16[4096,128]{1,0:T(8,128)(2,1)S(1)}, bf16[4096,128]{1,0:T(8,128)(2,1)}, u32[]{:S(2)}) %copy-start) | copy-done | bytes 1048600
  29.3 0.0 copy-start.2
  29.3 1.2 %copy-done.2 = bf16[4096,128]{1,0:T(8,128)(2,1)S(1)} copy-done((bf16[4096,128]{1,0:T(8,128)(2,1)S(1)}, bf16[4096,128]{1,0:T(8,128)(2,1)}, u32[]{:S(2)}) %copy-start.2) | copy-done | bytes 1048600
  30.5 0.0 copy-start.4
  30.5 1.2 %copy-done.4 = bf16[128,4096]{1,0:T(8,128)(2,1)S(1)} copy-done((bf16[128,4096]{1,0:T(8,128)(2,1)S(1)}, bf16[128,4096]{1,0:T(8,128)(2,1)}, u32[]{:S(2)}) %copy-start.4) | copy-done | bytes 1048600
  31.8 0.0 copy-start.5
  31.8 0.8 %copy-done.5 = bf16[1,24,1024]{2,1,0:T(8,128)(2,1)S(1)} copy-done((bf16[1,24,1024]{2,1,0:T(8,128)(2,1)S(1)}, bf16[1,24,1024]{2,1,0:T(8,128)(2,1)}, u32[]{:S(2)}) %copy-start.5) | copy-done | bytes 49176
  32.6 0.0 copy-start.1
  32.6 0.0 copy-start.3
  32.6 1.0 %shard_map.94 = (bf16[256,1024]{1,0:T(8,128)(2,1)S(1)}, bf16[128,1024]{1,0:T(8,128)(2,1)S(1)}, f32[2,16,8,128]{3,2,1,0:T(8,128)S(1)}) custom-call(bf16[1,24,1024]{2,1,0:T(8,128)(2,1)S(1)} %copy-done.5, bf16[3,24,1024]{2,1,0:T(8,128)(2,1)S(1)} %constant_dynamic-update-slice_fusion.refs_1_, bf16[1,24,1024]{2,1,0:T(8,128)(2,1)S(1)} %collective-permute-done.3.refs_2_, ...), custom_call_target="tpu_custom_call" | custom-call | tf_op jit(solution)/shard_map/pallas_call | solution.py:180
  33.6 0.1 collective-permute-start.9
  33.6 1.3 %collective-permute-done.9.refs_1_ = f32[2,16,8,128]{3,2,1,0:T(8,128)S(1)} collective-permute-done((f32[2,16,8,128]{3,2,1,0:T(8,128)S(1)}, f32[2,16,8,128]{3,2,1,0:T(8,128)S(1)}, u32[]{:S(2)}, u32[]{:S(2)}) %collective-permute-start.9) | collective-permute-done | bytes 131104 | tf_op jit(solution)/shard_map/ppermute | solution.py:315
  35.0 0.0 copy-done.1
  35.0 0.0 copy-done.3
  35.0 0.8 %shard_map.95 = (bf16[256,256]{1,0:T(8,128)(2,1)S(1)}, bf16[128,128]{1,0:T(8,128)(2,1)S(1)}, f32[4,8,1024]{2,1,0:T(8,128)S(1)}, bf16[4,8,1024]{2,1,0:T(8,128)(2,...) custom-call(f32[2,16,8,128]{3,2,1,0:T(8,128)S(1)} %get-tuple-element.16.refs_0_, ...), custom_call_target="tpu_custom_call" | custom-call | tf_op jit(solution)/shard_map/pallas_call | solution.py:245
  35.8 0.9 %collective-permute-start.10 = (bf16[4,8,1024]{2,1,0:T(8,128)(2,1)S(1)}, bf16[4,8,1024]{2,1,0:T(8,128)(2,1)S(1)}, u32[]{:S(2)}, u32[]{:S(2)}) collective-permute-start(bf16[4,8,1024]{2,1,0:T(8,128)(2,1)S(1)} %get-tuple-element.18), channel_id=1, source_target_pairs={{0,2},{2,0},{4,6},{6,4},{8,10},{10,8},{12,14},{14,12},{16,18},{18,... | collective-permute-start | bytes 196616 | tf_op jit(solution)/shard_map/ppermute | solution.py:40
  36.7 1.6 %collective-permute-start.11 = (bf16[4,8,1024]{2,1,0:T(8,128)(2,1)S(1)}, bf16[4,8,1024]{2,1,0:T(8,128)(2,1)S(1)}, u32[]{:S(2)}, u32[]{:S(2)}) collective-permute-start(bf16[4,8,1024]{2,1,0:T(8,128)(2,1)S(1)} %get-tuple-element.19), channel_id=1, source_target_pairs={{0,4},{2,6},{4,0},{6,2},{8,12},{10,14},{12,8},{14,10},{16,20},{18,... | collective-permute-start | bytes 196616 | tf_op jit(solution)/shard_map/ppermute | solution.py:40
  38.3 1.1 %collective-permute-start.12 = (bf16[4,8,1024]{2,1,0:T(8,128)(2,1)S(1)}, bf16[4,8,1024]{2,1,0:T(8,128)(2,1)S(1)}, u32[]{:S(2)}, u32[]{:S(2)}) collective-permute-start(bf16[4,8,1024]{2,1,0:T(8,128)(2,1)S(1)} %get-tuple-element.20), channel_id=1, source_target_pairs={{0,6},{2,4},{4,2},{6,0},{8,14},{10,12},{12,10},{14,8},{16,22},{18,... | collective-permute-start | bytes 196616 | tf_op jit(solution)/shard_map/ppermute | solution.py:40
  39.4 0.8 %collective-permute-done.10 = bf16[4,8,1024]{2,1,0:T(8,128)(2,1)S(1)} collective-permute-done((bf16[4,8,1024]{2,1,0:T(8,128)(2,1)S(1)}, bf16[4,8,1024]{2,1,0:T(8,128)(2,1)S(1)}, u32[]{:S(2)}, u32[]{:S(2)}) %collective-permute-start.10) | collective-permute-done | bytes 65568 | tf_op jit(solution)/shard_map/ppermute | solution.py:40
  40.2 0.8 %collective-permute-done.11 = bf16[4,8,1024]{2,1,0:T(8,128)(2,1)S(1)} collective-permute-done((bf16[4,8,1024]{2,1,0:T(8,128)(2,1)S(1)}, bf16[4,8,1024]{2,1,0:T(8,128)(2,1)S(1)}, u32[]{:S(2)}, u32[]{:S(2)}) %collective-permute-start.11) | collective-permute-done | bytes 65568 | tf_op jit(solution)/shard_map/ppermute | solution.py:40
  40.9 2.5 %collective-permute-done.12 = bf16[4,8,1024]{2,1,0:T(8,128)(2,1)S(1)} collective-permute-done((bf16[4,8,1024]{2,1,0:T(8,128)(2,1)S(1)}, bf16[4,8,1024]{2,1,0:T(8,128)(2,1)S(1)}, u32[]{:S(2)}, u32[]{:S(2)}) %collective-permute-start.12) | collective-permute-done | bytes 65568 | tf_op jit(solution)/shard_map/ppermute | solution.py:40
  43.5 0.3 collective-permute-start.13
  43.8 2.5 %collective-permute-start.15 = (bf16[1,8,1024]{2,1,0:T(8,128)(2,1)S(1)}, bf16[1,8,1024]{2,1,0:T(8,128)(2,1)S(1)}, u32[]{:S(2)}, u32[]{:S(2)}) collective-permute-start(bf16[1,8,1024]{2,1,0:T(8,128)(2,1)S(1)} %get-tuple-element.31), channel_id=1, source_target_pairs={{0,24},{2,26},{4,28},{6,30},{8,16},{10,18},{12,20},{14,22},{16,8},... | collective-permute-start | bytes 49160 | tf_op jit(solution)/shard_map/ppermute | solution.py:40
  46.3 0.7 %collective-permute-start.14 = (bf16[1,8,1024]{2,1,0:T(8,128)(2,1)S(1)}, bf16[1,8,1024]{2,1,0:T(8,128)(2,1)S(1)}, u32[]{:S(2)}, u32[]{:S(2)}) collective-permute-start(bf16[1,8,1024]{2,1,0:T(8,128)(2,1)S(1)} %get-tuple-element.32), channel_id=1, source_target_pairs={{0,16},{2,18},{4,20},{6,22},{8,24},{10,26},{12,28},{14,30},{16,0},... | collective-permute-start | bytes 49160 | tf_op jit(solution)/shard_map/ppermute | solution.py:40
  47.0 5.3 %shard_map.96 = (f32[4096,128]{1,0:T(8,128)}, f32[4096,128]{1,0:T(8,128)}, f32[128,4096]{1,0:T(8,128)}) custom-call(bf16[256,1024]{1,0:T(8,128)(2,1)S(1)} %get-tuple-element.21.pt, bf16[128,1024]{1,0:T(8,128)(2,1)S(1)} %get-tuple-element.22.cot, bf16[256,256]{1,0:T(8,128)(2,1)S(1)} %get-tuple-element.23.factor, bf16[128,128]{1,0:T(8,128)(2,1)S(1)} %get-tuple-element.24.tact), custom_call_target="tpu_custom_call" | custom-call | tf_op jit(solution)/shard_map/pallas_call | solution.py:287
  52.3 0.0 collective-permute-done.13
  52.3 0.0 collective-permute-done.15
  52.3 0.0 collective-permute-done.14
  52.4 0.6 %reshape.14 = bf16[2,4096]{1,0:T(2,128)(2,1)} reshape(bf16[2,8,4,128]{3,2,1,0:T(4,128)(2,1)S(1)} %copy.10) | data formatting | bytes 32768 | tf_op jit(solution)/shard_map/reshape | solution.py:93
  (8 shorter events, 0.1 us)
Async XLA Ops:
  2.1 5.6 %collective-permute-start = (bf16[1,24,1024]{2,1,0:T(8,128)(2,1)}, bf16[1,24,1024]{2,1,0:T(8,128)(2,1)S(1)}, u32[]{:S(2)}, u32[]{:S(2)}) collective-permute-start(bf16[1,24,1024]{2,1,0:T(8,128)(2,1)} %shard_map.93.refs_0_), channel_id=1, source_target_pairs={{8,0},{10,2},{12,4},{14,6},{0,8},{2,10},{4,12},{6,14},{24,16},{26,... | collective-permute-start | bytes 147464 | tf_op jit(solution)/shard_map/ppermute | solution.py:35
  5.1 8.2 %collective-permute-start.2 = (bf16[1,24,1024]{2,1,0:T(8,128)(2,1)}, bf16[1,24,1024]{2,1,0:T(8,128)(2,1)S(1)}, u32[]{:S(2)}, u32[]{:S(2)}) collective-permute-start(bf16[1,24,1024]{2,1,0:T(8,128)(2,1)} %shard_map.93.refs_0_), channel_id=1, source_target_pairs={{24,0},{26,2},{28,4},{30,6},{16,8},{18,10},{20,12},{22,14},{8,16},... | collective-permute-start | bytes 147464 | tf_op jit(solution)/shard_map/ppermute | solution.py:35
  7.6 5.7 %collective-permute-start.1 = (bf16[1,24,1024]{2,1,0:T(8,128)(2,1)}, bf16[1,24,1024]{2,1,0:T(8,128)(2,1)S(1)}, u32[]{:S(2)}, u32[]{:S(2)}) collective-permute-start(bf16[1,24,1024]{2,1,0:T(8,128)(2,1)} %shard_map.93.refs_0_), channel_id=1, source_target_pairs={{16,0},{18,2},{20,4},{22,6},{24,8},{26,10},{28,12},{30,14},{0,16},... | collective-permute-start | bytes 147464 | tf_op jit(solution)/shard_map/ppermute | solution.py:35
  13.3 14.7 %collective-permute-start.8 = (bf16[3,24,1024]{2,1,0:T(8,128)(2,1)S(1)}, bf16[3,24,1024]{2,1,0:T(8,128)(2,1)S(1)}, u32[]{:S(2)}, u32[]{:S(2)}) collective-permute-start(bf16[3,24,1024]{2,1,0:T(8,128)(2,1)S(1)} %constant_dynamic-update-slice_fusion.refs_1_), channel_id=1, source_target_pairs={{6,0},{4,2},{2,4},{0,6},{14,8},{12,10},{10,12},{8,14},{22,16},{20,... | collective-permute-start | bytes 442376 | tf_op jit(solution)/shard_map/ppermute | solution.py:35
  15.8 12.2 %collective-permute-start.6 = (bf16[3,24,1024]{2,1,0:T(8,128)(2,1)S(1)}, bf16[3,24,1024]{2,1,0:T(8,128)(2,1)S(1)}, u32[]{:S(2)}, u32[]{:S(2)}) collective-permute-start(bf16[3,24,1024]{2,1,0:T(8,128)(2,1)S(1)} %constant_dynamic-update-slice_fusion.refs_1_), channel_id=1, source_target_pairs={{4,0},{6,2},{0,4},{2,6},{12,8},{14,10},{8,12},{10,14},{20,16},{22,... | collective-permute-start | bytes 442376 | tf_op jit(solution)/shard_map/ppermute | solution.py:35
  16.3 11.7 %collective-permute-start.4 = (bf16[3,24,1024]{2,1,0:T(8,128)(2,1)S(1)}, bf16[3,24,1024]{2,1,0:T(8,128)(2,1)S(1)}, u32[]{:S(2)}, u32[]{:S(2)}) collective-permute-start(bf16[3,24,1024]{2,1,0:T(8,128)(2,1)S(1)} %constant_dynamic-update-slice_fusion.refs_1_), channel_id=1, source_target_pairs={{2,0},{0,2},{6,4},{4,6},{10,8},{8,10},{14,12},{12,14},{18,16},{16,... | collective-permute-start | bytes 442376 | tf_op jit(solution)/shard_map/ppermute | solution.py:35
  16.9 6.9 %collective-permute-start.7 = (bf16[1,24,1024]{2,1,0:T(8,128)(2,1)}, bf16[1,24,1024]{2,1,0:T(8,128)(2,1)S(1)}, u32[]{:S(2)}, u32[]{:S(2)}) collective-permute-start(bf16[1,24,1024]{2,1,0:T(8,128)(2,1)} %shard_map.93.refs_0_), channel_id=1, source_target_pairs={{6,0},{4,2},{2,4},{0,6},{14,8},{12,10},{10,12},{8,14},{22,16},{20,... | collective-permute-start | bytes 147464 | tf_op jit(solution)/shard_map/ppermute | solution.py:35
  19.3 5.2 %collective-permute-start.5 = (bf16[1,24,1024]{2,1,0:T(8,128)(2,1)}, bf16[1,24,1024]{2,1,0:T(8,128)(2,1)S(1)}, u32[]{:S(2)}, u32[]{:S(2)}) collective-permute-start(bf16[1,24,1024]{2,1,0:T(8,128)(2,1)} %shard_map.93.refs_0_), channel_id=1, source_target_pairs={{4,0},{6,2},{0,4},{2,6},{12,8},{14,10},{8,12},{10,14},{20,16},{22,... | collective-permute-start | bytes 147464 | tf_op jit(solution)/shard_map/ppermute | solution.py:35
  23.8 4.3 %collective-permute-start.3 = (bf16[1,24,1024]{2,1,0:T(8,128)(2,1)}, bf16[1,24,1024]{2,1,0:T(8,128)(2,1)S(1)}, u32[]{:S(2)}, u32[]{:S(2)}) collective-permute-start(bf16[1,24,1024]{2,1,0:T(8,128)(2,1)} %shard_map.93.refs_0_), channel_id=1, source_target_pairs={{2,0},{0,2},{6,4},{4,6},{10,8},{8,10},{14,12},{12,14},{18,16},{16,... | collective-permute-start | bytes 147464 | tf_op jit(solution)/shard_map/ppermute | solution.py:35
  28.1 1.2 %copy-start = (bf16[4096,128]{1,0:T(8,128)(2,1)S(1)}, bf16[4096,128]{1,0:T(8,128)(2,1)}, u32[]{:S(2)}) copy-start(bf16[4096,128]{1,0:T(8,128)(2,1)} %refs_2_.3) | copy-start | bytes 3145732
  29.3 1.2 %copy-start.2 = (bf16[4096,128]{1,0:T(8,128)(2,1)S(1)}, bf16[4096,128]{1,0:T(8,128)(2,1)}, u32[]{:S(2)}) copy-start(bf16[4096,128]{1,0:T(8,128)(2,1)} %refs_3_.1) | copy-start | bytes 3145732
  30.5 1.2 %copy-start.4 = (bf16[128,4096]{1,0:T(8,128)(2,1)S(1)}, bf16[128,4096]{1,0:T(8,128)(2,1)}, u32[]{:S(2)}) copy-start(bf16[128,4096]{1,0:T(8,128)(2,1)} %refs_10_.1) | copy-start | bytes 3145732
  31.8 0.8 %copy-start.5 = (bf16[1,24,1024]{2,1,0:T(8,128)(2,1)S(1)}, bf16[1,24,1024]{2,1,0:T(8,128)(2,1)}, u32[]{:S(2)}) copy-start(bf16[1,24,1024]{2,1,0:T(8,128)(2,1)} %shard_map.93.refs_0_) | copy-start | bytes 147460
  32.6 2.4 %copy-start.1 = (bf16[4096,128]{1,0:T(8,128)(2,1)S(1)}, bf16[4096,128]{1,0:T(8,128)(2,1)}, u32[]{:S(2)}) copy-start(bf16[4096,128]{1,0:T(8,128)(2,1)} %refs_2_.3) | copy-start | bytes 3145732
  32.6 2.4 %copy-start.3 = (bf16[4096,128]{1,0:T(8,128)(2,1)S(1)}, bf16[4096,128]{1,0:T(8,128)(2,1)}, u32[]{:S(2)}) copy-start(bf16[4096,128]{1,0:T(8,128)(2,1)} %refs_3_.1) | copy-start | bytes 3145732
  33.6 1.4 %collective-permute-start.9 = (f32[2,16,8,128]{3,2,1,0:T(8,128)S(1)}, f32[2,16,8,128]{3,2,1,0:T(8,128)S(1)}, u32[]{:S(2)}, u32[]{:S(2)}) collective-permute-start(f32[2,16,8,128]{3,2,1,0:T(8,128)S(1)} %get-tuple-element.16.refs_0_), channel_id=1, source_target_pairs={{0,1},{1,0},{2,3},{3,2},{4,5},{5,4},{6,7},{7,6},{8,9},{9,8},{10,11... | collective-permute-start | bytes 393224 | tf_op jit(solution)/shard_map/ppermute | solution.py:315
  35.8 4.3 %collective-permute-start.10 = (bf16[4,8,1024]{2,1,0:T(8,128)(2,1)S(1)}, bf16[4,8,1024]{2,1,0:T(8,128)(2,1)S(1)}, u32[]{:S(2)}, u32[]{:S(2)}) collective-permute-start(bf16[4,8,1024]{2,1,0:T(8,128)(2,1)S(1)} %get-tuple-element.18), channel_id=1, source_target_pairs={{0,2},{2,0},{4,6},{6,4},{8,10},{10,8},{12,14},{14,12},{16,18},{18,... | collective-permute-start | bytes 196616 | tf_op jit(solution)/shard_map/ppermute | solution.py:40
  36.7 4.3 %collective-permute-start.11 = (bf16[4,8,1024]{2,1,0:T(8,128)(2,1)S(1)}, bf16[4,8,1024]{2,1,0:T(8,128)(2,1)S(1)}, u32[]{:S(2)}, u32[]{:S(2)}) collective-permute-start(bf16[4,8,1024]{2,1,0:T(8,128)(2,1)S(1)} %get-tuple-element.19), channel_id=1, source_target_pairs={{0,4},{2,6},{4,0},{6,2},{8,12},{10,14},{12,8},{14,10},{16,20},{18,... | collective-permute-start | bytes 196616 | tf_op jit(solution)/shard_map/ppermute | solution.py:40
  38.3 5.2 %collective-permute-start.12 = (bf16[4,8,1024]{2,1,0:T(8,128)(2,1)S(1)}, bf16[4,8,1024]{2,1,0:T(8,128)(2,1)S(1)}, u32[]{:S(2)}, u32[]{:S(2)}) collective-permute-start(bf16[4,8,1024]{2,1,0:T(8,128)(2,1)S(1)} %get-tuple-element.20), channel_id=1, source_target_pairs={{0,6},{2,4},{4,2},{6,0},{8,14},{10,12},{12,10},{14,8},{16,22},{18,... | collective-permute-start | bytes 196616 | tf_op jit(solution)/shard_map/ppermute | solution.py:40
  43.5 8.9 %collective-permute-start.13 = (bf16[1,8,1024]{2,1,0:T(8,128)(2,1)S(1)}, bf16[1,8,1024]{2,1,0:T(8,128)(2,1)S(1)}, u32[]{:S(2)}, u32[]{:S(2)}) collective-permute-start(bf16[1,8,1024]{2,1,0:T(8,128)(2,1)S(1)} %get-tuple-element.30), channel_id=1, source_target_pairs={{0,8},{2,10},{4,12},{6,14},{8,0},{10,2},{12,4},{14,6},{16,24},{18,... | collective-permute-start | bytes 49160 | tf_op jit(solution)/shard_map/ppermute | solution.py:40
  43.8 8.5 %collective-permute-start.15 = (bf16[1,8,1024]{2,1,0:T(8,128)(2,1)S(1)}, bf16[1,8,1024]{2,1,0:T(8,128)(2,1)S(1)}, u32[]{:S(2)}, u32[]{:S(2)}) collective-permute-start(bf16[1,8,1024]{2,1,0:T(8,128)(2,1)S(1)} %get-tuple-element.31), channel_id=1, source_target_pairs={{0,24},{2,26},{4,28},{6,30},{8,16},{10,18},{12,20},{14,22},{16,8},... | collective-permute-start | bytes 49160 | tf_op jit(solution)/shard_map/ppermute | solution.py:40
  46.3 6.0 %collective-permute-start.14 = (bf16[1,8,1024]{2,1,0:T(8,128)(2,1)S(1)}, bf16[1,8,1024]{2,1,0:T(8,128)(2,1)S(1)}, u32[]{:S(2)}, u32[]{:S(2)}) collective-permute-start(bf16[1,8,1024]{2,1,0:T(8,128)(2,1)S(1)} %get-tuple-element.32), channel_id=1, source_target_pairs={{0,16},{2,18},{4,20},{6,22},{8,24},{10,26},{12,28},{14,30},{16,0},... | collective-permute-start | bytes 49160 | tf_op jit(solution)/shard_map/ppermute | solution.py:40

commit v4 on v3

v4 whole, which is shorter than its diff:
```python
import functools

import jax
import jax.numpy as jnp
from jax import lax
from jax.experimental import pallas as pl
from jax.experimental.pallas import tpu as pltpu
from jax.sharding import PartitionSpec as P

SLOTS = 4
LANES = 128
VMEM_LIMIT = 24 * 2**20


def levels_of(size):
    levels, stride = [], 1
    while stride < size:
        rest = size // stride
        radix = next(r for r in (4, 2, 3, 5, 7, rest) if rest % r == 0)
        levels.append((stride, radix))
        stride *= radix
    return levels[::-1]


def partner(index, stride, radix, offset):
    digit = index // stride % radix
    if radix & (radix - 1) == 0:
        other = digit ^ offset
    else:
        other = (digit + offset) % radix
    return index + (other - digit) * stride


def fetch(value, axis, size, level, offset):
    pairs = [(partner(i, *level, offset), i) for i in range(size)]
    return lax.ppermute(value, axis, pairs)


def deliver(value, axis, size, level, offset):
    pairs = [(i, partner(i, *level, offset)) for i in range(size)]
    return lax.ppermute(value, axis, pairs)


def after(value, earlier):
    return lax.optimization_barrier((value, earlier))[0]


def gather_blocks(own, axis, size):
    early, late = [own], []
    for level in levels_of(size):
        early, late = early + late, []
        rest = early[1:]
        offsets = range(level[1] - 1, 0, -1)
        held = jnp.concatenate(rest) if rest else None
        mine = [fetch(own, axis, size, level, o) for o in offsets][::-1]
        if rest:
            late = [
                fetch(after(held, mine[o - 1]), axis, size, level, o) for o in offsets
            ][::-1]
            early = [own, held]
            if level[0] > 1:
                late = [x for pair in zip(mine, late) for x in pair]
                mine = []
        early = early + mine
    return early, late


def scatter_sum(groups, axis, size):
    for level in levels_of(size)[::-1]:
        if len(groups) == 1:
            groups = jnp.split(groups[0], level[1])
        total = groups[0]
        for o in range(1, level[1]):
            sent = groups[o].astype(jnp.bfloat16)
            total = total + deliver(sent, axis, size, level, o).astype(jnp.float32)
        groups = [total]
    return groups[0]


def fold(*rows):
    stacked = lax.optimization_barrier(jnp.stack(rows))
    count, tokens, width = stacked.shape
    split = stacked.reshape(count, tokens, width // (SLOTS * LANES), SLOTS, LANES)
    return split.transpose(0, 3, 1, 2, 4).reshape(1, -1, width // SLOTS)


def unfold(rows):
    tokens = rows.shape[0] // SLOTS
    split = rows.reshape(SLOTS, tokens, rows.shape[1] // LANES, LANES)
    return split.transpose(1, 2, 0, 3).reshape(tokens, rows.shape[1] * SLOTS)


def slot_of(shape, axis):
    return lax.broadcasted_iota(jnp.int32, shape, axis) // 2


def rows_for_slot(weight, slot):
    height, width = weight.shape
    split = weight.reshape(height // (SLOTS * LANES), SLOTS, LANES, width)
    return split[:, slot].reshape(height // SLOTS, width)


def over_slots(x):
    axis = x.ndim - 2
    x = x + pltpu.roll(x, 4, axis)
    return x + pltpu.roll(x, 2, axis)


def pick_slots(parts):
    slot = slot_of(parts[0].shape, parts[0].ndim - 2)
    result = parts[0]
    for s in range(1, SLOTS):
        result = jnp.where(slot == s, parts[s], result)
    return result


def only_slot(x, s):
    return jnp.where(slot_of(x.shape, x.ndim - 2) == s, x, 0.0)


def place(pieces, at, pt_out, c_out):
    for piece in pieces:
        for i in range(piece.shape[0]):
            pt_out[at * 16 : at * 16 + 16] = piece[i, 0:16]
            c_out[at * 8 : at * 8 + 8] = piece[i, 16:24]
            at += 1


def projections(pt, cot, gate_w, up_w, down_w):
    blocks, hidden = cot.shape[0] // 8, gate_w.shape[1]
    acts, dacts = [], []
    for s in range(SLOTS):
        weights = jnp.concatenate(
            [rows_for_slot(gate_w[...], s), rows_for_slot(up_w[...], s)], axis=1
        )
        acts.append(
            jnp.dot(pt, weights, preferred_element_type=jnp.float32).reshape(
                2 * blocks, 8, 2 * hidden
            )
        )
        columns = [
            down_w[:, j * LANES : (j + 1) * LANES]
            for j in range(s, down_w.shape[1] // LANES, SLOTS)
        ]
        dacts.append(
            lax.dot_general(
                cot,
                jnp.concatenate(columns, axis=1),
                (((1,), (1,)), ((), ())),
                preferred_element_type=jnp.float32,
            ).reshape(blocks, 8, hidden)
        )
    act = over_slots(pick_slots(acts)).reshape(blocks, 2, 8, 2 * hidden)
    packed = pick_slots(
        [
            act[:, 0, :, :hidden],
            act[:, 0, :, hidden:],
            act[:, 1, :, :hidden],
            act[:, 1, :, hidden:],
        ]
    )
    return packed, over_slots(pick_slots(dacts))


def begin_kernel(n_pieces, *refs):
    pieces, weights = refs[:n_pieces], refs[n_pieces : n_pieces + 3]
    pt_out, c_out, parts_out, *held, sems = refs[n_pieces + 3 :]
    copies = [
        pltpu.make_async_copy(w, h, sems.at[k])
        for k, (w, h) in enumerate(zip(weights, held))
    ]
    for copy in copies:
        copy.start()
    place(pieces, 0, pt_out, c_out)
    for copy in copies:
        copy.wait()
    parts_out[0], parts_out[1] = projections(pt_out[...], c_out[...], *held)


def begin(pieces, weights):
    blocks = sum(p.shape[0] for p in pieces)
    lanes, hidden = pieces[0].shape[2], weights[0].shape[1]
    vmem = pl.BlockSpec(memory_space=pltpu.VMEM)
    return pl.pallas_call(
        functools.partial(begin_kernel, len(pieces)),
        out_shape=(
            jax.ShapeDtypeStruct((blocks * 16, lanes), jnp.bfloat16),
            jax.ShapeDtypeStruct((blocks * 8, lanes), jnp.bfloat16),
            jax.ShapeDtypeStruct((2, blocks, 8, hidden), jnp.float32),
        )
        + tuple(jax.ShapeDtypeStruct(w.shape, w.dtype) for w in weights),
        in_specs=[vmem] * len(pieces) + [pl.BlockSpec(memory_space=pltpu.HBM)] * 3,
        out_specs=(vmem,) * 6,
        scratch_shapes=[pltpu.SemaphoreType.DMA((3,))],
        compiler_params=pltpu.CompilerParams(vmem_limit_bytes=VMEM_LIMIT),
        cost_estimate=pl.CostEstimate(
            flops=blocks * 8 * 10 * SLOTS * lanes * hidden,
            bytes_accessed=sum(4 * w.size for w in weights),
            transcendentals=0,
        ),
    )(*pieces, *weights)


def finish_kernel(n_pieces, *refs):
    pieces, weights = refs[:n_pieces], refs[n_pieces : n_pieces + 3]
    pt_in, c_in, parts_in, pt_out, c_out, parts_out = refs[n_pieces + 3 :]
    blocks = parts_in.shape[1]
    pt_out[: blocks * 16] = pt_in[...]
    c_out[: blocks * 8] = c_in[...]
    parts_out[:, :blocks] = parts_in[...]
    place(pieces, blocks, pt_out, c_out)
    parts_out[0, blocks:], parts_out[1, blocks:] = projections(
        pt_out[blocks * 16 :], c_out[blocks * 8 :], *weights
    )


def finish(pieces, weights, pt, cot, parts):
    blocks = parts.shape[1] + sum(p.shape[0] for p in pieces)
    lanes, hidden = pieces[0].shape[2], weights[0].shape[1]
    vmem = pl.BlockSpec(memory_space=pltpu.VMEM)
    return pl.pallas_call(
        functools.partial(finish_kernel, len(pieces)),
        out_shape=(
            jax.ShapeDtypeStruct((blocks * 16, lanes), jnp.bfloat16),
            jax.ShapeDtypeStruct((blocks * 8, lanes), jnp.bfloat16),
            jax.ShapeDtypeStruct((2, blocks, 8, hidden), jnp.float32),
        ),
        in_specs=[vmem] * (len(pieces) + 6),
        out_specs=(vmem,) * 3,
        compiler_params=pltpu.CompilerParams(vmem_limit_bytes=VMEM_LIMIT),
    )(*pieces, *weights, pt, cot, parts)


def factors(gate, up, tgate, tup, dact):
    sig = 1.0 / (1.0 + jnp.exp(-gate))
    act = gate * sig
    first = sig * (1.0 + gate * (1.0 - sig))
    second = sig * (1.0 - sig) * (2.0 + gate * (1.0 - 2.0 * sig))
    dgate = dact * up * first
    dup = dact * act
    tdgate = dact * (tup * first + up * second * tgate)
    tdup = dact * first * tgate
    tact = tgate * first * up + act * tup
    return (dgate, dup, tdgate, tdup, tact)


def by_slot(x):
    rows = x.size // x.shape[-1]
    return jnp.concatenate(
        [only_slot(x, s).reshape(rows, x.shape[-1]) for s in range(SLOTS)], axis=1
    ).astype(jnp.bfloat16)


def middle_kernel(n_parts, groups, *refs):
    parts, (gate_w, up_w) = refs[:n_parts], refs[n_parts : n_parts + 2]
    factor_out, tact_out = refs[n_parts + 2 : n_parts + 4]
    own_out, others_out = refs[n_parts + 4], refs[n_parts + 5 :]
    packed, dact = (sum(p[k] for p in parts[1:]) + parts[0][k] for k in range(2))
    gate, up, tgate, tup = (over_slots(only_slot(packed, s)) for s in range(SLOTS))
    dgate, dup, tdgate, tdup, tact = factors(gate, up, tgate, tup, dact)
    blocks, _, hidden = gate.shape
    second = jnp.concatenate([tdgate, tdup], axis=2)
    pair = jnp.stack([second, jnp.concatenate([dgate, dup], axis=2)], axis=1)
    factor_out[...] = by_slot(pair)
    tact_out[...] = by_slot(tact)
    right = jnp.concatenate(
        [rows_for_slot(w[...], s) for s in range(SLOTS) for w in (gate_w, up_w)], axis=1
    )
    hvp = lax.dot_general(
        by_slot(second),
        right,
        (((1,), (1,)), ((), ())),
        preferred_element_type=jnp.float32,
    )
    hvp = hvp.reshape(blocks, 8, hvp.shape[1])
    inner = blocks // groups
    own_out[...] = hvp[:inner]
    early = inner + groups - 1
    for g, out in enumerate(others_out):
        at = early + g * (inner - 1)
        out[0] = hvp[inner + g].astype(out.dtype)
        out[1:] = hvp[at : at + inner - 1].astype(out.dtype)


def middle(parts, gate_w, up_w, groups):
    _, blocks, _, hidden = parts[0].shape
    lanes = gate_w.shape[0] // SLOTS
    vmem = pl.BlockSpec(memory_space=pltpu.VMEM)
    group = (blocks // groups, 8, lanes)
    return pl.pallas_call(
        functools.partial(middle_kernel, len(parts), groups),
        out_shape=(
            jax.ShapeDtypeStruct((blocks * 16, SLOTS * 2 * hidden), jnp.bfloat16),
            jax.ShapeDtypeStruct((blocks * 8, SLOTS * hidden), jnp.bfloat16),
            jax.ShapeDtypeStruct(group, jnp.float32),
        )
        + (jax.ShapeDtypeStruct(group, jnp.bfloat16),) * (groups - 1),
        in_specs=[vmem] * (len(parts) + 2),
        out_specs=(vmem,) * (groups + 2),
        compiler_params=pltpu.CompilerParams(vmem_limit_bytes=VMEM_LIMIT),
    )(*parts, gate_w, up_w)


def contract_first(left, right):
    return lax.dot_general(
        left, right, (((0,), (0,)), ((), ())), preferred_element_type=jnp.float32
    )


def up_grads_kernel(pt, factor, gate_out, up_out):
    hidden = gate_out.shape[1]
    for m in range(pt.shape[1] // LANES):
        both = contract_first(pt[:, m * LANES : (m + 1) * LANES], factor[...])
        for s in range(SLOTS):
            at = (m * SLOTS + s) * LANES
            half = 2 * s * hidden
            gate_out[at : at + LANES] = both[:, half : half + hidden]
            up_out[at : at + LANES] = both[:, half + hidden : half + 2 * hidden]


def up_grads(pt, factor, steps):
    rows, lanes = pt.shape
    hidden = factor.shape[1] // (2 * SLOTS)
    out = jax.ShapeDtypeStruct((SLOTS * lanes, hidden), jnp.float32)
    spec = pl.BlockSpec((SLOTS * lanes // steps, hidden), lambda m: (m, 0))
    return pl.pallas_call(
        up_grads_kernel,
        grid=(steps,),
        out_shape=(out, out),
        in_specs=[
            pl.BlockSpec((rows, lanes // steps), lambda m: (0, m)),
            pl.BlockSpec(memory_space=pltpu.VMEM),
        ],
        out_specs=(spec, spec),
        compiler_params=pltpu.CompilerParams(vmem_limit_bytes=VMEM_LIMIT),
        cost_estimate=pl.CostEstimate(
            flops=2 * pt.size * factor.shape[1],
            bytes_accessed=8 * SLOTS * lanes * hidden,
            transcendentals=0,
        ),
    )(pt, factor)


def down_grad_kernel(cot, tact, down_out):
    hidden = down_out.shape[0]
    for m in range(cot.shape[1] // LANES):
        tiles = contract_first(tact[...], cot[:, m * LANES : (m + 1) * LANES])
        for s in range(SLOTS):
            at = (m * SLOTS + s) * LANES
            down_out[:, at : at + LANES] = tiles[s * hidden : (s + 1) * hidden]


def down_grad(cot, tact, steps):
    rows, lanes = cot.shape
    hidden = tact.shape[1] // SLOTS
    return pl.pallas_call(
        down_grad_kernel,
        grid=(steps,),
        out_shape=jax.ShapeDtypeStruct((hidden, SLOTS * lanes), jnp.float32),
        in_specs=[
            pl.BlockSpec((rows, lanes // steps), lambda m: (0, m)),
            pl.BlockSpec(memory_space=pltpu.VMEM),
        ],
        out_specs=pl.BlockSpec((hidden, SLOTS * lanes // steps), lambda m: (0, m)),
        compiler_params=pltpu.CompilerParams(vmem_limit_bytes=VMEM_LIMIT),
        cost_estimate=pl.CostEstimate(
            flops=2 * cot.size * tact.shape[1],
            bytes_accessed=4 * SLOTS * lanes * hidden,
            transcendentals=0,
        ),
    )(cot, tact)


def solution(mesh):
    wide, narrow = mesh.shape["wide"], mesh.shape["narrow"]

    def local(primal_in, tangent_in, cotangent, gate_weight, up_weight, down_weight):
        weights = (gate_weight, up_weight, down_weight)
        early, late = gather_blocks(
            fold(primal_in, tangent_in, cotangent), "wide", wide
        )
        *first, gate_weight, up_weight, down_weight = begin(early, weights)
        weights = (gate_weight, up_weight, down_weight)
        pt, cot, part = finish(late, weights, *first)
        parts = [part]
        for shift in range(1, narrow):
            pairs = [(i, (i + shift) % narrow) for i in range(narrow)]
            parts.append(lax.ppermute(part, "narrow", pairs))
        groups = levels_of(wide)[-1][1]
        factor, tact, *hvp = middle(parts, gate_weight, up_weight, groups)
        total = scatter_sum(hvp, "wide", wide)
        input_hvp = unfold(total[0].astype(jnp.bfloat16))
        steps = max(1, pt.shape[1] // (2 * LANES))
        gate_grad, up_grad = up_grads(pt, factor, steps)
        return (input_hvp, gate_grad, up_grad, down_grad(cot, tact, steps))

    return jax.shard_map(
        local,
        mesh=mesh,
        in_specs=(
            P("wide", "narrow"),
            P("wide", "narrow"),
            P("wide", "narrow"),
            P("narrow", "wide"),
            P("narrow", "wide"),
            P("wide", "narrow"),
        ),
        out_specs=(
            P("wide", "narrow"),
            P("narrow", "wide"),
            P("narrow", "wide"),
            P("wide", "narrow"),
        ),
        check_vma=False,
    )
```

time: 53.3 us -> 42.9 us (0.80)
  waiting for transfers between devices: 18.4 us -> 7.62 us
  other arithmetic: 0.05 us -> 0.88 us
  local copies, waits for them, and re-layouts: 5.12 us -> 4.41 us
  starting transfers between devices: 20.1 us -> 20.8 us
    ppermute x9, waiting for transfers between devices: 13 us -> 3.32 us  [fetch(): return lax.ppermute(value, axis, pairs)]
    ppermute x6, waiting for transfers between devices: 4.04 us -> 2.97 us  [deliver(): return lax.ppermute(value, axis, pairs)]
    ppermute x6, starting transfers between devices: 7.11 us -> 8.01 us  [deliver(): return lax.ppermute(value, axis, pairs)]
    another operation x1 -> x2, other arithmetic: 0.03 us -> 0.86 us  [the longest x1 0.83 us: fold(): stacked = lax.optimization_barrier(jnp.stack(rows))]
    unnamed x15 -> x9, local copies, waits for them, and re-layouts: 4.49 us -> 3.69 us
    pallas_call x3 -> x4, Pallas kernels: 7.75 us -> 7.32 us  [the longest x1 3.01 us: up_grads(): pl.pallas_call(up_grads_kernel, grid=(steps,), out_shape=(out, out), in_s...]
  transfers between devices with their start and end apart: 16 -> 16, of which waited for: 7 -> 5; matrix products, arithmetic and copies ran while one was open for 0% -> 0% of each run, Pallas kernels for 10% -> 15%
where the time goes in v4:
time: 42.9 us; the launch traced here: 42.6 us
  starting transfers between devices  20.8 us (48%)
  Pallas kernels  8.19 us (19%)
  waiting for transfers between devices  7.62 us (18%)
  local copies, waits for them, and re-layouts  4.41 us (10%)
  other arithmetic  0.88 us (2%)
  between operations  0.75 us (2%)
    ppermute x9, starting transfers between devices, fetch(): return lax.ppermute(value, axis, pairs)  12.7 us
    ppermute x6, starting transfers between devices, deliver(): return lax.ppermute(value, axis, pairs)  8.01 us
    unnamed x9, local copies, waits for them, and re-layouts  3.69 us
    ppermute x9, waiting for transfers between devices, fetch(): return lax.ppermute(value, axis, pairs)  3.32 us
    pallas_call x1, Pallas kernels, up_grads(): pl.pallas_call(up_grads_kernel, grid=(steps,), out_shape=(out, out), in_s...  3.01 us
    ppermute x6, waiting for transfers between devices, deliver(): return lax.ppermute(value, axis, pairs)  2.97 us
    pallas_call x1, Pallas kernels, down_grad(): pl.pallas_call(down_grad_kernel, grid=(steps,), out_shape=jax.ShapeDtypeS...  2.4 us
    ppermute x1, waiting for transfers between devices, local(): parts.append(lax.ppermute(part, 'narrow', pairs))  1.33 us
  transfers between devices with their start and end apart: 16, of which 5 were waited for; matrix products, arithmetic and copies ran while one was open for 0% of the time, Pallas kernels for 15%

profile of v4, /device:TPU:0, one launch (start us, length us, event | category | flops | bytes accessed | tf_op | source)
XLA Modules:
  0.0 42.6 jit_solution(1471931727151535725)
XLA Ops:
  0.6 0.8 %pad_maximum_fusion = bf16[3,2,4096]{2,1,0:T(2,128)(2,1)S(1)} fusion(bf16[1,2,4096]{2,1,0:T(2,128)(2,1)} %bitcast.17, bf16[1,2,4096]{2,1,0:T(2,128)(2,1)} %bitcast.18, bf16[1,2,4096]{2,1,0:T(2,128)(2,1)} %bitcast.19), kind=kLoop, calls=%fused_computation.1 | loop fusion | flops 49152 | bytes 98304 | tf_op jit(solution)/shard_map/stack | solution.py:81
  1.6 3.1 %collective-permute-start = (bf16[1,24,1024]{2,1,0:T(8,128)(2,1)S(1)}, bf16[1,24,1024]{2,1,0:T(8,128)(2,1)S(1)}, u32[]{:S(2)}, u32[]{:S(2)}) collective-permute-start(bf16[1,24,1024]{2,1,0:T(8,128)(2,1)S(1)} %reshape.21.refs_0_), channel_id=1, source_target_pairs={{8,0},{10,2},{12,4},{14,6},{0,8},{2,10},{4,12},{6,14},{24,16},{26,... | collective-permute-start | bytes 147464 | tf_op jit(solution)/shard_map/ppermute | solution.py:36
  4.7 2.6 %collective-permute-start.1 = (bf16[1,24,1024]{2,1,0:T(8,128)(2,1)S(1)}, bf16[1,24,1024]{2,1,0:T(8,128)(2,1)S(1)}, u32[]{:S(2)}, u32[]{:S(2)}) collective-permute-start(bf16[1,24,1024]{2,1,0:T(8,128)(2,1)S(1)} %reshape.21.refs_0_), channel_id=1, source_target_pairs={{16,0},{18,2},{20,4},{22,6},{24,8},{26,10},{28,12},{30,14},{0,16},... | collective-permute-start | bytes 147464 | tf_op jit(solution)/shard_map/ppermute | solution.py:36
  7.2 0.0 collective-permute-start.2
  7.2 1.7 %collective-permute-start.3 = (bf16[1,24,1024]{2,1,0:T(8,128)(2,1)S(1)}, bf16[1,24,1024]{2,1,0:T(8,128)(2,1)S(1)}, u32[]{:S(2)}, u32[]{:S(2)}) collective-permute-start(bf16[1,24,1024]{2,1,0:T(8,128)(2,1)S(1)} %reshape.21.refs_0_), channel_id=1, source_target_pairs={{2,0},{0,2},{6,4},{4,6},{10,8},{8,10},{14,12},{12,14},{18,16},{16,... | collective-permute-start | bytes 147464 | tf_op jit(solution)/shard_map/ppermute | solution.py:36
  9.0 1.5 %collective-permute-start.5 = (bf16[1,24,1024]{2,1,0:T(8,128)(2,1)S(1)}, bf16[1,24,1024]{2,1,0:T(8,128)(2,1)S(1)}, u32[]{:S(2)}, u32[]{:S(2)}) collective-permute-start(bf16[1,24,1024]{2,1,0:T(8,128)(2,1)S(1)} %reshape.21.refs_0_), channel_id=1, source_target_pairs={{4,0},{6,2},{0,4},{2,6},{12,8},{14,10},{8,12},{10,14},{20,16},{22,... | collective-permute-start | bytes 147464 | tf_op jit(solution)/shard_map/ppermute | solution.py:36
  10.5 0.0 collective-permute-done
  10.5 0.3 collective-permute-start.7
  10.7 0.0 collective-permute-done.1
  10.8 2.4 %collective-permute-done.2 = bf16[1,24,1024]{2,1,0:T(8,128)(2,1)S(1)} collective-permute-done((bf16[1,24,1024]{2,1,0:T(8,128)(2,1)S(1)}, bf16[1,24,1024]{2,1,0:T(8,128)(2,1)S(1)}, u32[]{:S(2)}, u32[]{:S(2)}) %collective-permute-start.2) | collective-permute-done | bytes 49184 | tf_op jit(solution)/shard_map/ppermute | solution.py:36
  13.1 0.0 collective-permute-done.3.refs_2_
  13.1 1.6 %collective-permute-start.4 = (bf16[3,24,1024]{2,1,0:T(8,128)(2,1)S(1)}, bf16[3,24,1024]{2,1,0:T(8,128)(2,1)S(1)}, u32[]{:S(2)}, u32[]{:S(2)}) collective-permute-start(bf16[3,24,1024]{2,1,0:T(8,128)(2,1)S(1)} %constant_dynamic-update-slice_fusion.refs_1_), channel_id=1, source_target_pairs={{2,0},{0,2},{6,4},{4,6},{10,8},{8,10},{14,12},{12,14},{18,16},{16,... | collective-permute-start | bytes 442376 | tf_op jit(solution)/shard_map/ppermute | solution.py:36
  14.7 0.0 collective-permute-done.5.refs_3_
  14.7 1.5 %collective-permute-start.6 = (bf16[3,24,1024]{2,1,0:T(8,128)(2,1)S(1)}, bf16[3,24,1024]{2,1,0:T(8,128)(2,1)S(1)}, u32[]{:S(2)}, u32[]{:S(2)}) collective-permute-start(bf16[3,24,1024]{2,1,0:T(8,128)(2,1)S(1)} %constant_dynamic-update-slice_fusion.refs_1_), channel_id=1, source_target_pairs={{4,0},{6,2},{0,4},{2,6},{12,8},{14,10},{8,12},{10,14},{20,16},{22,... | collective-permute-start | bytes 442376 | tf_op jit(solution)/shard_map/ppermute | solution.py:36
  16.2 0.0 collective-permute-done.7.refs_4_
  16.2 0.5 %collective-permute-start.8 = (bf16[3,24,1024]{2,1,0:T(8,128)(2,1)S(1)}, bf16[3,24,1024]{2,1,0:T(8,128)(2,1)S(1)}, u32[]{:S(2)}, u32[]{:S(2)}) collective-permute-start(bf16[3,24,1024]{2,1,0:T(8,128)(2,1)S(1)} %constant_dynamic-update-slice_fusion.refs_1_), channel_id=1, source_target_pairs={{6,0},{4,2},{2,4},{0,6},{14,8},{12,10},{10,12},{8,14},{22,16},{20,... | collective-permute-start | bytes 442376 | tf_op jit(solution)/shard_map/ppermute | solution.py:36
  16.7 0.0 copy-start
  16.7 1.2 %copy-done = bf16[4096,128]{1,0:T(8,128)(2,1)S(1)} copy-done((bf16[4096,128]{1,0:T(8,128)(2,1)S(1)}, bf16[4096,128]{1,0:T(8,128)(2,1)}, u32[]{:S(2)}) %copy-start) | copy-done | bytes 1048600
  17.9 0.0 copy-start.1
  17.9 1.2 %copy-done.1 = bf16[4096,128]{1,0:T(8,128)(2,1)S(1)} copy-done((bf16[4096,128]{1,0:T(8,128)(2,1)S(1)}, bf16[4096,128]{1,0:T(8,128)(2,1)}, u32[]{:S(2)}) %copy-start.1) | copy-done | bytes 1048600
  19.2 0.0 copy-start.2
  19.2 1.2 %copy-done.2 = bf16[128,4096]{1,0:T(8,128)(2,1)S(1)} copy-done((bf16[128,4096]{1,0:T(8,128)(2,1)S(1)}, bf16[128,4096]{1,0:T(8,128)(2,1)}, u32[]{:S(2)}) %copy-start.2) | copy-done | bytes 1048600
  20.4 1.1 %shard_map.93 = (bf16[112,1024]{1,0:T(8,128)(2,1)S(1)}, bf16[56,1024]{1,0:T(8,128)(2,1)S(1)}, f32[2,7,8,128]{3,2,1,0:T(8,128)S(1)}, bf16[4096,128]{1,0:T(8,128)(...) custom-call(bf16[1,24,1024]{2,1,0:T(8,128)(2,1)S(1)} %reshape.21.refs_0_, ...), custom_call_target="tpu_custom_call" | custom-call | flops 293601280 | bytes 6291456 | tf_op jit(solution)/shard_map/pallas_call | solution.py:184
  21.5 0.0 collective-permute-done.4.refs_0_
  21.5 0.9 %collective-permute-done.6.refs_1_ = bf16[3,24,1024]{2,1,0:T(8,128)(2,1)S(1)} collective-permute-done((bf16[3,24,1024]{2,1,0:T(8,128)(2,1)S(1)}, bf16[3,24,1024]{2,1,0:T(8,128)(2,1)S(1)}, u32[]{:S(2)}, u32[]{:S(2)}) %collective-permute-start.6) | collective-permute-done | bytes 147488 | tf_op jit(solution)/shard_map/ppermute | solution.py:36
  22.4 0.0 collective-permute-done.8.refs_2_
  22.4 0.8 %shard_map.94 = (bf16[256,1024]{1,0:T(8,128)(2,1)S(1)}, bf16[128,1024]{1,0:T(8,128)(2,1)S(1)}, f32[2,16,8,128]{3,2,1,0:T(8,128)S(1)}) custom-call(bf16[3,24,1024]{2,1,0:T(8,128)(2,1)S(1)} %collective-permute-done.4.refs_0_, bf16[3,24,1024]{2,1,0:T(8,128)(2,1)S(1)} %collective-permute-done.6.refs_1_, bf16[3,24,1024]{2,1,0:T(8,128)(2,1)S(1)} %collective-permute-done.8.refs_2_, ...), custom_call_target="tpu_custom_call" | custom-call | tf_op jit(solution)/shard_map/pallas_call | solution.py:221
  23.2 0.1 collective-permute-start.9
  23.3 1.3 %collective-permute-done.9.refs_1_ = f32[2,16,8,128]{3,2,1,0:T(8,128)S(1)} collective-permute-done((f32[2,16,8,128]{3,2,1,0:T(8,128)S(1)}, f32[2,16,8,128]{3,2,1,0:T(8,128)S(1)}, u32[]{:S(2)}, u32[]{:S(2)}) %collective-permute-start.9) | collective-permute-done | bytes 131104 | tf_op jit(solution)/shard_map/ppermute | solution.py:388
  24.6 0.9 %shard_map.95 = (bf16[256,1024]{1,0:T(8,128)(2,1)S(1)}, bf16[128,512]{1,0:T(8,128)(2,1)S(1)}, f32[4,8,1024]{2,1,0:T(8,128)S(1)}, bf16[4,8,1024]{2,1,0:T(8,128)(2...) custom-call(f32[2,16,8,128]{3,2,1,0:T(8,128)S(1)} %get-tuple-element.33.refs_0_, ...), custom_call_target="tpu_custom_call" | custom-call | tf_op jit(solution)/shard_map/pallas_call | solution.py:290
  25.5 1.6 %collective-permute-start.12 = (bf16[4,8,1024]{2,1,0:T(8,128)(2,1)S(1)}, bf16[4,8,1024]{2,1,0:T(8,128)(2,1)S(1)}, u32[]{:S(2)}, u32[]{:S(2)}) collective-permute-start(bf16[4,8,1024]{2,1,0:T(8,128)(2,1)S(1)} %get-tuple-element.37), channel_id=1, source_target_pairs={{0,6},{2,4},{4,2},{6,0},{8,14},{10,12},{12,10},{14,8},{16,22},{18,... | collective-permute-start | bytes 196616 | tf_op jit(solution)/shard_map/ppermute | solution.py:41
  27.1 0.5 %collective-permute-start.11 = (bf16[4,8,1024]{2,1,0:T(8,128)(2,1)S(1)}, bf16[4,8,1024]{2,1,0:T(8,128)(2,1)S(1)}, u32[]{:S(2)}, u32[]{:S(2)}) collective-permute-start(bf16[4,8,1024]{2,1,0:T(8,128)(2,1)S(1)} %get-tuple-element.36), channel_id=1, source_target_pairs={{0,4},{2,6},{4,0},{6,2},{8,12},{10,14},{12,8},{14,10},{16,20},{18,... | collective-permute-start | bytes 196616 | tf_op jit(solution)/shard_map/ppermute | solution.py:41
  27.6 1.4 %collective-permute-start.10 = (bf16[4,8,1024]{2,1,0:T(8,128)(2,1)S(1)}, bf16[4,8,1024]{2,1,0:T(8,128)(2,1)S(1)}, u32[]{:S(2)}, u32[]{:S(2)}) collective-permute-start(bf16[4,8,1024]{2,1,0:T(8,128)(2,1)S(1)} %get-tuple-element.35), channel_id=1, source_target_pairs={{0,2},{2,0},{4,6},{6,4},{8,10},{10,8},{12,14},{14,12},{16,18},{18,... | collective-permute-start | bytes 196616 | tf_op jit(solution)/shard_map/ppermute | solution.py:41
  29.1 1.7 %collective-permute-done.12 = bf16[4,8,1024]{2,1,0:T(8,128)(2,1)S(1)} collective-permute-done((bf16[4,8,1024]{2,1,0:T(8,128)(2,1)S(1)}, bf16[4,8,1024]{2,1,0:T(8,128)(2,1)S(1)}, u32[]{:S(2)}, u32[]{:S(2)}) %collective-permute-start.12) | collective-permute-done | bytes 65568 | tf_op jit(solution)/shard_map/ppermute | solution.py:41
  30.8 1.2 %collective-permute-done.11 = bf16[4,8,1024]{2,1,0:T(8,128)(2,1)S(1)} collective-permute-done((bf16[4,8,1024]{2,1,0:T(8,128)(2,1)S(1)}, bf16[4,8,1024]{2,1,0:T(8,128)(2,1)S(1)}, u32[]{:S(2)}, u32[]{:S(2)}) %collective-permute-start.11) | collective-permute-done | bytes 65568 | tf_op jit(solution)/shard_map/ppermute | solution.py:41
  32.0 0.0 collective-permute-done.10
  32.1 3.1 %collective-permute-start.15 = (bf16[1,8,1024]{2,1,0:T(8,128)(2,1)S(1)}, bf16[1,8,1024]{2,1,0:T(8,128)(2,1)S(1)}, u32[]{:S(2)}, u32[]{:S(2)}) collective-permute-start(bf16[1,8,1024]{2,1,0:T(8,128)(2,1)S(1)} %get-tuple-element.47), channel_id=1, source_target_pairs={{0,24},{2,26},{4,28},{6,30},{8,16},{10,18},{12,20},{14,22},{16,8},... | collective-permute-start | bytes 49160 | tf_op jit(solution)/shard_map/ppermute | solution.py:41
  35.2 0.0 collective-permute-start.14
  35.2 1.4 %collective-permute-start.13 = (bf16[1,8,1024]{2,1,0:T(8,128)(2,1)S(1)}, bf16[1,8,1024]{2,1,0:T(8,128)(2,1)S(1)}, u32[]{:S(2)}, u32[]{:S(2)}) collective-permute-start(bf16[1,8,1024]{2,1,0:T(8,128)(2,1)S(1)} %get-tuple-element.46), channel_id=1, source_target_pairs={{0,8},{2,10},{4,12},{6,14},{8,0},{10,2},{12,4},{14,6},{16,24},{18,... | collective-permute-start | bytes 49160 | tf_op jit(solution)/shard_map/ppermute | solution.py:41
  36.5 3.0 %shard_map.96 = (f32[4096,128]{1,0:T(8,128)}, f32[4096,128]{1,0:T(8,128)}) custom-call(bf16[256,1024]{1,0:T(8,128)(2,1)S(1)} %get-tuple-element.38.pt, bf16[256,1024]{1,0:T(8,128)(2,1)S(1)} %get-tuple-element.39.factor), custom_call_target="tpu_custom_call" | custom-call | flops 536870912 | bytes 4194304 | tf_op jit(solution)/shard_map/pallas_call | solution.py:326
  39.6 2.4 %shard_map.97 = f32[128,4096]{1,0:T(8,128)} custom-call(bf16[128,1024]{1,0:T(8,128)(2,1)S(1)} %get-tuple-element.42.cot, bf16[128,512]{1,0:T(8,128)(2,1)S(1)} %get-tuple-element.43.tact), custom_call_target="tpu_custom_call" | custom-call | flops 134217728 | bytes 2097152 | tf_op jit(solution)/shard_map/pallas_call | solution.py:356
  42.0 0.0 collective-permute-done.15
  42.0 0.0 collective-permute-done.14
  42.0 0.0 collective-permute-done.13
  42.0 0.6 %reshape.22 = bf16[2,4096]{1,0:T(2,128)(2,1)} reshape(bf16[2,8,4,128]{3,2,1,0:T(4,128)(2,1)S(1)} %copy.11) | data formatting | bytes 32768 | tf_op jit(solution)/shard_map/reshape | solution.py:90
  (11 shorter events, 0.2 us)
Async XLA Ops:
  1.6 8.9 %collective-permute-start = (bf16[1,24,1024]{2,1,0:T(8,128)(2,1)S(1)}, bf16[1,24,1024]{2,1,0:T(8,128)(2,1)S(1)}, u32[]{:S(2)}, u32[]{:S(2)}) collective-permute-start(bf16[1,24,1024]{2,1,0:T(8,128)(2,1)S(1)} %reshape.21.refs_0_), channel_id=1, source_target_pairs={{8,0},{10,2},{12,4},{14,6},{0,8},{2,10},{4,12},{6,14},{24,16},{26,... | collective-permute-start | bytes 147464 | tf_op jit(solution)/shard_map/ppermute | solution.py:36
  4.7 6.1 %collective-permute-start.1 = (bf16[1,24,1024]{2,1,0:T(8,128)(2,1)S(1)}, bf16[1,24,1024]{2,1,0:T(8,128)(2,1)S(1)}, u32[]{:S(2)}, u32[]{:S(2)}) collective-permute-start(bf16[1,24,1024]{2,1,0:T(8,128)(2,1)S(1)} %reshape.21.refs_0_), channel_id=1, source_target_pairs={{16,0},{18,2},{20,4},{22,6},{24,8},{26,10},{28,12},{30,14},{0,16},... | collective-permute-start | bytes 147464 | tf_op jit(solution)/shard_map/ppermute | solution.py:36
  7.2 5.9 %collective-permute-start.2 = (bf16[1,24,1024]{2,1,0:T(8,128)(2,1)S(1)}, bf16[1,24,1024]{2,1,0:T(8,128)(2,1)S(1)}, u32[]{:S(2)}, u32[]{:S(2)}) collective-permute-start(bf16[1,24,1024]{2,1,0:T(8,128)(2,1)S(1)} %reshape.21.refs_0_), channel_id=1, source_target_pairs={{24,0},{26,2},{28,4},{30,6},{16,8},{18,10},{20,12},{22,14},{8,16},... | collective-permute-start | bytes 147464 | tf_op jit(solution)/shard_map/ppermute | solution.py:36
  7.2 5.9 %collective-permute-start.3 = (bf16[1,24,1024]{2,1,0:T(8,128)(2,1)S(1)}, bf16[1,24,1024]{2,1,0:T(8,128)(2,1)S(1)}, u32[]{:S(2)}, u32[]{:S(2)}) collective-permute-start(bf16[1,24,1024]{2,1,0:T(8,128)(2,1)S(1)} %reshape.21.refs_0_), channel_id=1, source_target_pairs={{2,0},{0,2},{6,4},{4,6},{10,8},{8,10},{14,12},{12,14},{18,16},{16,... | collective-permute-start | bytes 147464 | tf_op jit(solution)/shard_map/ppermute | solution.py:36
  9.0 5.7 %collective-permute-start.5 = (bf16[1,24,1024]{2,1,0:T(8,128)(2,1)S(1)}, bf16[1,24,1024]{2,1,0:T(8,128)(2,1)S(1)}, u32[]{:S(2)}, u32[]{:S(2)}) collective-permute-start(bf16[1,24,1024]{2,1,0:T(8,128)(2,1)S(1)} %reshape.21.refs_0_), channel_id=1, source_target_pairs={{4,0},{6,2},{0,4},{2,6},{12,8},{14,10},{8,12},{10,14},{20,16},{22,... | collective-permute-start | bytes 147464 | tf_op jit(solution)/shard_map/ppermute | solution.py:36
  10.5 5.7 %collective-permute-start.7 = (bf16[1,24,1024]{2,1,0:T(8,128)(2,1)S(1)}, bf16[1,24,1024]{2,1,0:T(8,128)(2,1)S(1)}, u32[]{:S(2)}, u32[]{:S(2)}) collective-permute-start(bf16[1,24,1024]{2,1,0:T(8,128)(2,1)S(1)} %reshape.21.refs_0_), channel_id=1, source_target_pairs={{6,0},{4,2},{2,4},{0,6},{14,8},{12,10},{10,12},{8,14},{22,16},{20,... | collective-permute-start | bytes 147464 | tf_op jit(solution)/shard_map/ppermute | solution.py:36
  13.1 8.3 %collective-permute-start.4 = (bf16[3,24,1024]{2,1,0:T(8,128)(2,1)S(1)}, bf16[3,24,1024]{2,1,0:T(8,128)(2,1)S(1)}, u32[]{:S(2)}, u32[]{:S(2)}) collective-permute-start(bf16[3,24,1024]{2,1,0:T(8,128)(2,1)S(1)} %constant_dynamic-update-slice_fusion.refs_1_), channel_id=1, source_target_pairs={{2,0},{0,2},{6,4},{4,6},{10,8},{8,10},{14,12},{12,14},{18,16},{16,... | collective-permute-start | bytes 442376 | tf_op jit(solution)/shard_map/ppermute | solution.py:36
  14.7 7.7 %collective-permute-start.6 = (bf16[3,24,1024]{2,1,0:T(8,128)(2,1)S(1)}, bf16[3,24,1024]{2,1,0:T(8,128)(2,1)S(1)}, u32[]{:S(2)}, u32[]{:S(2)}) collective-permute-start(bf16[3,24,1024]{2,1,0:T(8,128)(2,1)S(1)} %constant_dynamic-update-slice_fusion.refs_1_), channel_id=1, source_target_pairs={{4,0},{6,2},{0,4},{2,6},{12,8},{14,10},{8,12},{10,14},{20,16},{22,... | collective-permute-start | bytes 442376 | tf_op jit(solution)/shard_map/ppermute | solution.py:36
  16.2 6.2 %collective-permute-start.8 = (bf16[3,24,1024]{2,1,0:T(8,128)(2,1)S(1)}, bf16[3,24,1024]{2,1,0:T(8,128)(2,1)S(1)}, u32[]{:S(2)}, u32[]{:S(2)}) collective-permute-start(bf16[3,24,1024]{2,1,0:T(8,128)(2,1)S(1)} %constant_dynamic-update-slice_fusion.refs_1_), channel_id=1, source_target_pairs={{6,0},{4,2},{2,4},{0,6},{14,8},{12,10},{10,12},{8,14},{22,16},{20,... | collective-permute-start | bytes 442376 | tf_op jit(solution)/shard_map/ppermute | solution.py:36
  16.7 1.2 %copy-start = (bf16[4096,128]{1,0:T(8,128)(2,1)S(1)}, bf16[4096,128]{1,0:T(8,128)(2,1)}, u32[]{:S(2)}) copy-start(bf16[4096,128]{1,0:T(8,128)(2,1)} %refs_5_.1) | copy-start | bytes 3145732
  17.9 1.2 %copy-start.1 = (bf16[4096,128]{1,0:T(8,128)(2,1)S(1)}, bf16[4096,128]{1,0:T(8,128)(2,1)}, u32[]{:S(2)}) copy-start(bf16[4096,128]{1,0:T(8,128)(2,1)} %refs_6_.1) | copy-start | bytes 3145732
  19.2 1.2 %copy-start.2 = (bf16[128,4096]{1,0:T(8,128)(2,1)S(1)}, bf16[128,4096]{1,0:T(8,128)(2,1)}, u32[]{:S(2)}) copy-start(bf16[128,4096]{1,0:T(8,128)(2,1)} %refs_7_.1) | copy-start | bytes 3145732
  23.2 1.4 %collective-permute-start.9 = (f32[2,16,8,128]{3,2,1,0:T(8,128)S(1)}, f32[2,16,8,128]{3,2,1,0:T(8,128)S(1)}, u32[]{:S(2)}, u32[]{:S(2)}) collective-permute-start(f32[2,16,8,128]{3,2,1,0:T(8,128)S(1)} %get-tuple-element.33.refs_0_), channel_id=1, source_target_pairs={{0,1},{1,0},{2,3},{3,2},{4,5},{5,4},{6,7},{7,6},{8,9},{9,8},{10,11... | collective-permute-start | bytes 393224 | tf_op jit(solution)/shard_map/ppermute | solution.py:388
  25.5 5.3 %collective-permute-start.12 = (bf16[4,8,1024]{2,1,0:T(8,128)(2,1)S(1)}, bf16[4,8,1024]{2,1,0:T(8,128)(2,1)S(1)}, u32[]{:S(2)}, u32[]{:S(2)}) collective-permute-start(bf16[4,8,1024]{2,1,0:T(8,128)(2,1)S(1)} %get-tuple-element.37), channel_id=1, source_target_pairs={{0,6},{2,4},{4,2},{6,0},{8,14},{10,12},{12,10},{14,8},{16,22},{18,... | collective-permute-start | bytes 196616 | tf_op jit(solution)/shard_map/ppermute | solution.py:41
  27.1 4.9 %collective-permute-start.11 = (bf16[4,8,1024]{2,1,0:T(8,128)(2,1)S(1)}, bf16[4,8,1024]{2,1,0:T(8,128)(2,1)S(1)}, u32[]{:S(2)}, u32[]{:S(2)}) collective-permute-start(bf16[4,8,1024]{2,1,0:T(8,128)(2,1)S(1)} %get-tuple-element.36), channel_id=1, source_target_pairs={{0,4},{2,6},{4,0},{6,2},{8,12},{10,14},{12,8},{14,10},{16,20},{18,... | collective-permute-start | bytes 196616 | tf_op jit(solution)/shard_map/ppermute | solution.py:41
  27.6 4.4 %collective-permute-start.10 = (bf16[4,8,1024]{2,1,0:T(8,128)(2,1)S(1)}, bf16[4,8,1024]{2,1,0:T(8,128)(2,1)S(1)}, u32[]{:S(2)}, u32[]{:S(2)}) collective-permute-start(bf16[4,8,1024]{2,1,0:T(8,128)(2,1)S(1)} %get-tuple-element.35), channel_id=1, source_target_pairs={{0,2},{2,0},{4,6},{6,4},{8,10},{10,8},{12,14},{14,12},{16,18},{18,... | collective-permute-start | bytes 196616 | tf_op jit(solution)/shard_map/ppermute | solution.py:41
  32.1 9.9 %collective-permute-start.15 = (bf16[1,8,1024]{2,1,0:T(8,128)(2,1)S(1)}, bf16[1,8,1024]{2,1,0:T(8,128)(2,1)S(1)}, u32[]{:S(2)}, u32[]{:S(2)}) collective-permute-start(bf16[1,8,1024]{2,1,0:T(8,128)(2,1)S(1)} %get-tuple-element.47), channel_id=1, source_target_pairs={{0,24},{2,26},{4,28},{6,30},{8,16},{10,18},{12,20},{14,22},{16,8},... | collective-permute-start | bytes 49160 | tf_op jit(solution)/shard_map/ppermute | solution.py:41
  35.2 6.8 %collective-permute-start.14 = (bf16[1,8,1024]{2,1,0:T(8,128)(2,1)S(1)}, bf16[1,8,1024]{2,1,0:T(8,128)(2,1)S(1)}, u32[]{:S(2)}, u32[]{:S(2)}) collective-permute-start(bf16[1,8,1024]{2,1,0:T(8,128)(2,1)S(1)} %get-tuple-element.48), channel_id=1, source_target_pairs={{0,16},{2,18},{4,20},{6,22},{8,24},{10,26},{12,28},{14,30},{16,0},... | collective-permute-start | bytes 49160 | tf_op jit(solution)/shard_map/ppermute | solution.py:41
  35.2 6.8 %collective-permute-start.13 = (bf16[1,8,1024]{2,1,0:T(8,128)(2,1)S(1)}, bf16[1,8,1024]{2,1,0:T(8,128)(2,1)S(1)}, u32[]{:S(2)}, u32[]{:S(2)}) collective-permute-start(bf16[1,8,1024]{2,1,0:T(8,128)(2,1)S(1)} %get-tuple-element.46), channel_id=1, source_target_pairs={{0,8},{2,10},{4,12},{6,14},{8,0},{10,2},{12,4},{14,6},{16,24},{18,... | collective-permute-start | bytes 49160 | tf_op jit(solution)/shard_map/ppermute | solution.py:41

commit v5 on v4

--- a/solution.py
+++ b/solution.py
@@ -45,18 +45,23 @@
     return lax.optimization_barrier((value, earlier))[0]
 
 
+def offsets_of(radix):
+    return range(radix - 1, 0, -1)
+
+
 def gather_blocks(own, axis, size):
     early, late = [own], []
     for level in levels_of(size):
         early, late = early + late, []
         rest = early[1:]
-        offsets = range(level[1] - 1, 0, -1)
+        offsets = offsets_of(level[1])
         held = jnp.concatenate(rest) if rest else None
-        mine = [fetch(own, axis, size, level, o) for o in offsets][::-1]
+        mine = [fetch(own, axis, size, level, o) for o in offsets]
         if rest:
             late = [
-                fetch(after(held, mine[o - 1]), axis, size, level, o) for o in offsets
-            ][::-1]
+                fetch(after(held, came), axis, size, level, o)
+                for o, came in zip(offsets, mine)
+            ]
             early = [own, held]
             if level[0] > 1:
                 late = [x for pair in zip(mine, late) for x in pair]
@@ -65,14 +70,17 @@
     return early, late
 
 
-def scatter_sum(groups, axis, size):
+def scatter_sum(groups, axis, size, beside):
     for level in levels_of(size)[::-1]:
         if len(groups) == 1:
-            groups = jnp.split(groups[0], level[1])
+            groups = jnp.split(after(groups[0], beside), level[1])
+        came = [
+            deliver(group.astype(jnp.bfloat16), axis, size, level, o)
+            for o, group in zip(offsets_of(level[1]), groups[1:])
+        ]
         total = groups[0]
-        for o in range(1, level[1]):
-            sent = groups[o].astype(jnp.bfloat16)
-            total = total + deliver(sent, axis, size, level, o).astype(jnp.float32)
+        for block in came[::-1]:
+            total = total + block.astype(jnp.float32)
         groups = [total]
     return groups[0]
 
@@ -388,10 +396,10 @@
             parts.append(lax.ppermute(part, "narrow", pairs))
         groups = levels_of(wide)[-1][1]
         factor, tact, *hvp = middle(parts, gate_weight, up_weight, groups)
-        total = scatter_sum(hvp, "wide", wide)
-        input_hvp = unfold(total[0].astype(jnp.bfloat16))
         steps = max(1, pt.shape[1] // (2 * LANES))
         gate_grad, up_grad = up_grads(pt, factor, steps)
+        total = scatter_sum(hvp, "wide", wide, gate_grad)
+        input_hvp = unfold(total[0].astype(jnp.bfloat16))
         return (input_hvp, gate_grad, up_grad, down_grad(cot, tact, steps))
 
     return jax.shard_map(

time: 42.9 us -> 40.6 us (0.946)
  waiting for transfers between devices: 7.62 us -> 5.18 us
    ppermute x9, waiting for transfers between devices: 3.32 us -> 1.81 us  [fetch(): return lax.ppermute(value, axis, pairs)]
    ppermute x6, waiting for transfers between devices: 2.97 us -> 2.03 us  [deliver(): return lax.ppermute(value, axis, pairs)]
  transfers between devices with their start and end apart: 16 -> 16, of which waited for: 5 -> 7; matrix products, arithmetic and copies ran while one was open for 0% -> 0% of each run, Pallas kernels for 15% -> 16%
where the time goes in v5:
time: 40.6 us; the launch traced here: 40.3 us
  starting transfers between devices  20.8 us (51%)
  Pallas kernels  8.21 us (20%)
  waiting for transfers between devices  5.18 us (13%)
  local copies, waits for them, and re-layouts  4.41 us (11%)
  other arithmetic  0.88 us (2%)
  between operations  0.76 us (2%)
    ppermute x9, starting transfers between devices, fetch(): return lax.ppermute(value, axis, pairs)  12.7 us
    ppermute x6, starting transfers between devices, deliver(): return lax.ppermute(value, axis, pairs)  8.01 us
    unnamed x9, local copies, waits for them, and re-layouts  3.69 us
    pallas_call x1, Pallas kernels, up_grads(): pl.pallas_call(up_grads_kernel, grid=(steps,), out_shape=(out, out), in_s...  3.03 us
    pallas_call x1, Pallas kernels, down_grad(): pl.pallas_call(down_grad_kernel, grid=(steps,), out_shape=jax.ShapeDtypeS...  2.4 us
    ppermute x6, waiting for transfers between devices, deliver(): return lax.ppermute(value, axis, pairs)  2.03 us
    ppermute x9, waiting for transfers between devices, fetch(): return lax.ppermute(value, axis, pairs)  1.81 us
    ppermute x1, waiting for transfers between devices, local(): parts.append(lax.ppermute(part, 'narrow', pairs))  1.33 us
  transfers between devices with their start and end apart: 16, of which 7 were waited for; matrix products, arithmetic and copies ran while one was open for 0% of the time, Pallas kernels for 16%

profile of v5, /device:TPU:0, one launch (start us, length us, event | category | flops | bytes accessed | tf_op | source)
XLA Modules:
  0.0 40.3 jit_solution(16661176463953331594)
XLA Ops:
  0.6 0.8 %pad_maximum_fusion = bf16[3,2,4096]{2,1,0:T(2,128)(2,1)S(1)} fusion(bf16[1,2,4096]{2,1,0:T(2,128)(2,1)} %bitcast.17, bf16[1,2,4096]{2,1,0:T(2,128)(2,1)} %bitcast.18, bf16[1,2,4096]{2,1,0:T(2,128)(2,1)} %bitcast.19), kind=kLoop, calls=%fused_computation.1 | loop fusion | flops 49152 | bytes 98304 | tf_op jit(solution)/shard_map/stack | solution.py:89
  1.6 5.1 %collective-permute-start = (bf16[1,24,1024]{2,1,0:T(8,128)(2,1)S(1)}, bf16[1,24,1024]{2,1,0:T(8,128)(2,1)S(1)}, u32[]{:S(2)}, u32[]{:S(2)}) collective-permute-start(bf16[1,24,1024]{2,1,0:T(8,128)(2,1)S(1)} %reshape.21.refs_0_), channel_id=1, source_target_pairs={{24,0},{26,2},{28,4},{30,6},{16,8},{18,10},{20,12},{22,14},{8,16},... | collective-permute-start | bytes 147464 | tf_op jit(solution)/shard_map/ppermute | solution.py:36
  6.7 0.0 collective-permute-start.1
  6.7 0.6 %collective-permute-start.2 = (bf16[1,24,1024]{2,1,0:T(8,128)(2,1)S(1)}, bf16[1,24,1024]{2,1,0:T(8,128)(2,1)S(1)}, u32[]{:S(2)}, u32[]{:S(2)}) collective-permute-start(bf16[1,24,1024]{2,1,0:T(8,128)(2,1)S(1)} %reshape.21.refs_0_), channel_id=1, source_target_pairs={{8,0},{10,2},{12,4},{14,6},{0,8},{2,10},{4,12},{6,14},{24,16},{26,... | collective-permute-start | bytes 147464 | tf_op jit(solution)/shard_map/ppermute | solution.py:36
  7.3 2.6 %collective-permute-start.3 = (bf16[1,24,1024]{2,1,0:T(8,128)(2,1)S(1)}, bf16[1,24,1024]{2,1,0:T(8,128)(2,1)S(1)}, u32[]{:S(2)}, u32[]{:S(2)}) collective-permute-start(bf16[1,24,1024]{2,1,0:T(8,128)(2,1)S(1)} %reshape.21.refs_0_), channel_id=1, source_target_pairs={{6,0},{4,2},{2,4},{0,6},{14,8},{12,10},{10,12},{8,14},{22,16},{20,... | collective-permute-start | bytes 147464 | tf_op jit(solution)/shard_map/ppermute | solution.py:36
  9.9 0.5 %collective-permute-start.5 = (bf16[1,24,1024]{2,1,0:T(8,128)(2,1)S(1)}, bf16[1,24,1024]{2,1,0:T(8,128)(2,1)S(1)}, u32[]{:S(2)}, u32[]{:S(2)}) collective-permute-start(bf16[1,24,1024]{2,1,0:T(8,128)(2,1)S(1)} %reshape.21.refs_0_), channel_id=1, source_target_pairs={{4,0},{6,2},{0,4},{2,6},{12,8},{14,10},{8,12},{10,14},{20,16},{22,... | collective-permute-start | bytes 147464 | tf_op jit(solution)/shard_map/ppermute | solution.py:36
  10.4 0.0 collective-permute-done
  10.4 0.4 collective-permute-start.7
  10.8 0.8 %collective-permute-done.1 = bf16[1,24,1024]{2,1,0:T(8,128)(2,1)S(1)} collective-permute-done((bf16[1,24,1024]{2,1,0:T(8,128)(2,1)S(1)}, bf16[1,24,1024]{2,1,0:T(8,128)(2,1)S(1)}, u32[]{:S(2)}, u32[]{:S(2)}) %collective-permute-start.1) | collective-permute-done | bytes 49184 | tf_op jit(solution)/shard_map/ppermute | solution.py:36
  11.7 0.0 collective-permute-done.2
  11.7 0.7 %collective-permute-done.3.refs_2_ = bf16[1,24,1024]{2,1,0:T(8,128)(2,1)S(1)} collective-permute-done((bf16[1,24,1024]{2,1,0:T(8,128)(2,1)S(1)}, bf16[1,24,1024]{2,1,0:T(8,128)(2,1)S(1)}, u32[]{:S(2)}, u32[]{:S(2)}) %collective-permute-start.3) | collective-permute-done | bytes 49184 | tf_op jit(solution)/shard_map/ppermute | solution.py:36
  12.4 2.5 %collective-permute-start.4 = (bf16[3,24,1024]{2,1,0:T(8,128)(2,1)S(1)}, bf16[3,24,1024]{2,1,0:T(8,128)(2,1)S(1)}, u32[]{:S(2)}, u32[]{:S(2)}) collective-permute-start(bf16[3,24,1024]{2,1,0:T(8,128)(2,1)S(1)} %constant_dynamic-update-slice_fusion.refs_1_), channel_id=1, source_target_pairs={{6,0},{4,2},{2,4},{0,6},{14,8},{12,10},{10,12},{8,14},{22,16},{20,... | collective-permute-start | bytes 442376 | tf_op jit(solution)/shard_map/ppermute | solution.py:36
  14.9 0.0 collective-permute-done.5.refs_3_
  14.9 0.7 %collective-permute-start.6 = (bf16[3,24,1024]{2,1,0:T(8,128)(2,1)S(1)}, bf16[3,24,1024]{2,1,0:T(8,128)(2,1)S(1)}, u32[]{:S(2)}, u32[]{:S(2)}) collective-permute-start(bf16[3,24,1024]{2,1,0:T(8,128)(2,1)S(1)} %constant_dynamic-update-slice_fusion.refs_1_), channel_id=1, source_target_pairs={{4,0},{6,2},{0,4},{2,6},{12,8},{14,10},{8,12},{10,14},{20,16},{22,... | collective-permute-start | bytes 442376 | tf_op jit(solution)/shard_map/ppermute | solution.py:36
  15.6 0.0 collective-permute-done.7.refs_4_
  15.6 0.3 collective-permute-start.8
  15.9 0.0 copy-start
  15.9 1.2 %copy-done = bf16[4096,128]{1,0:T(8,128)(2,1)S(1)} copy-done((bf16[4096,128]{1,0:T(8,128)(2,1)S(1)}, bf16[4096,128]{1,0:T(8,128)(2,1)}, u32[]{:S(2)}) %copy-start) | copy-done | bytes 1048600
  17.1 0.0 copy-start.1
  17.1 1.2 %copy-done.1 = bf16[4096,128]{1,0:T(8,128)(2,1)S(1)} copy-done((bf16[4096,128]{1,0:T(8,128)(2,1)S(1)}, bf16[4096,128]{1,0:T(8,128)(2,1)}, u32[]{:S(2)}) %copy-start.1) | copy-done | bytes 1048600
  18.4 0.0 copy-start.2
  18.4 1.2 %copy-done.2 = bf16[128,4096]{1,0:T(8,128)(2,1)S(1)} copy-done((bf16[128,4096]{1,0:T(8,128)(2,1)S(1)}, bf16[128,4096]{1,0:T(8,128)(2,1)}, u32[]{:S(2)}) %copy-start.2) | copy-done | bytes 1048600
  19.6 1.1 %shard_map.93 = (bf16[112,1024]{1,0:T(8,128)(2,1)S(1)}, bf16[56,1024]{1,0:T(8,128)(2,1)S(1)}, f32[2,7,8,128]{3,2,1,0:T(8,128)S(1)}, bf16[4096,128]{1,0:T(8,128)(...) custom-call(bf16[1,24,1024]{2,1,0:T(8,128)(2,1)S(1)} %reshape.21.refs_0_, ...), custom_call_target="tpu_custom_call" | custom-call | flops 293601280 | bytes 6291456 | tf_op jit(solution)/shard_map/pallas_call | solution.py:192
  20.7 0.0 collective-permute-done.4.refs_0_
  20.7 0.1 collective-permute-done.6.refs_1_
  20.8 0.1 collective-permute-done.8.refs_2_
  20.9 0.8 %shard_map.94 = (bf16[256,1024]{1,0:T(8,128)(2,1)S(1)}, bf16[128,1024]{1,0:T(8,128)(2,1)S(1)}, f32[2,16,8,128]{3,2,1,0:T(8,128)S(1)}) custom-call(bf16[3,24,1024]{2,1,0:T(8,128)(2,1)S(1)} %collective-permute-done.4.refs_0_, bf16[3,24,1024]{2,1,0:T(8,128)(2,1)S(1)} %collective-permute-done.6.refs_1_, bf16[3,24,1024]{2,1,0:T(8,128)(2,1)S(1)} %collective-permute-done.8.refs_2_, ...), custom_call_target="tpu_custom_call" | custom-call | tf_op jit(solution)/shard_map/pallas_call | solution.py:229
  21.7 0.1 collective-permute-start.9
  21.8 1.3 %collective-permute-done.9.refs_1_ = f32[2,16,8,128]{3,2,1,0:T(8,128)S(1)} collective-permute-done((f32[2,16,8,128]{3,2,1,0:T(8,128)S(1)}, f32[2,16,8,128]{3,2,1,0:T(8,128)S(1)}, u32[]{:S(2)}, u32[]{:S(2)}) %collective-permute-start.9) | collective-permute-done | bytes 131104 | tf_op jit(solution)/shard_map/ppermute | solution.py:396
  23.2 0.9 %shard_map.95 = (bf16[256,1024]{1,0:T(8,128)(2,1)S(1)}, bf16[128,512]{1,0:T(8,128)(2,1)S(1)}, f32[4,8,1024]{2,1,0:T(8,128)S(1)}, bf16[4,8,1024]{2,1,0:T(8,128)(2...) custom-call(f32[2,16,8,128]{3,2,1,0:T(8,128)S(1)} %get-tuple-element.34.refs_0_, ...), custom_call_target="tpu_custom_call" | custom-call | tf_op jit(solution)/shard_map/pallas_call | solution.py:298
  24.0 2.3 %collective-permute-start.12 = (bf16[4,8,1024]{2,1,0:T(8,128)(2,1)S(1)}, bf16[4,8,1024]{2,1,0:T(8,128)(2,1)S(1)}, u32[]{:S(2)}, u32[]{:S(2)}) collective-permute-start(bf16[4,8,1024]{2,1,0:T(8,128)(2,1)S(1)} %get-tuple-element.38), channel_id=1, source_target_pairs={{0,6},{2,4},{4,2},{6,0},{8,14},{10,12},{12,10},{14,8},{16,22},{18,... | collective-permute-start | bytes 196616 | tf_op jit(solution)/shard_map/ppermute | solution.py:41
  26.4 0.7 %collective-permute-start.11 = (bf16[4,8,1024]{2,1,0:T(8,128)(2,1)S(1)}, bf16[4,8,1024]{2,1,0:T(8,128)(2,1)S(1)}, u32[]{:S(2)}, u32[]{:S(2)}) collective-permute-start(bf16[4,8,1024]{2,1,0:T(8,128)(2,1)S(1)} %get-tuple-element.37), channel_id=1, source_target_pairs={{0,4},{2,6},{4,0},{6,2},{8,12},{10,14},{12,8},{14,10},{16,20},{18,... | collective-permute-start | bytes 196616 | tf_op jit(solution)/shard_map/ppermute | solution.py:41
  27.1 0.5 %collective-permute-start.10 = (bf16[4,8,1024]{2,1,0:T(8,128)(2,1)S(1)}, bf16[4,8,1024]{2,1,0:T(8,128)(2,1)S(1)}, u32[]{:S(2)}, u32[]{:S(2)}) collective-permute-start(bf16[4,8,1024]{2,1,0:T(8,128)(2,1)S(1)} %get-tuple-element.36), channel_id=1, source_target_pairs={{0,2},{2,0},{4,6},{6,4},{8,10},{10,8},{12,14},{14,12},{16,18},{18,... | collective-permute-start | bytes 196616 | tf_op jit(solution)/shard_map/ppermute | solution.py:41
  27.6 3.0 %shard_map.96 = (f32[4096,128]{1,0:T(8,128)}, f32[4096,128]{1,0:T(8,128)}) custom-call(bf16[256,1024]{1,0:T(8,128)(2,1)S(1)} %get-tuple-element.39.pt, bf16[256,1024]{1,0:T(8,128)(2,1)S(1)} %get-tuple-element.40.factor), custom_call_target="tpu_custom_call" | custom-call | flops 536870912 | bytes 4194304 | tf_op jit(solution)/shard_map/pallas_call | solution.py:334
  30.6 0.0 collective-permute-done.12
  30.6 0.0 collective-permute-done.11
  30.7 0.7 %collective-permute-done.10 = bf16[4,8,1024]{2,1,0:T(8,128)(2,1)S(1)} collective-permute-done((bf16[4,8,1024]{2,1,0:T(8,128)(2,1)S(1)}, bf16[4,8,1024]{2,1,0:T(8,128)(2,1)S(1)}, u32[]{:S(2)}, u32[]{:S(2)}) %collective-permute-start.10) | collective-permute-done | bytes 65568 | tf_op jit(solution)/shard_map/ppermute | solution.py:41
  31.4 3.5 %collective-permute-start.15 = (bf16[1,8,1024]{2,1,0:T(8,128)(2,1)S(1)}, bf16[1,8,1024]{2,1,0:T(8,128)(2,1)S(1)}, u32[]{:S(2)}, u32[]{:S(2)}) collective-permute-start(bf16[1,8,1024]{2,1,0:T(8,128)(2,1)S(1)} %get-tuple-element.47), channel_id=1, source_target_pairs={{0,24},{2,26},{4,28},{6,30},{8,16},{10,18},{12,20},{14,22},{16,8},... | collective-permute-start | bytes 49160 | tf_op jit(solution)/shard_map/ppermute | solution.py:41
  34.9 0.0 collective-permute-start.14
  35.0 0.9 %collective-permute-start.13 = (bf16[1,8,1024]{2,1,0:T(8,128)(2,1)S(1)}, bf16[1,8,1024]{2,1,0:T(8,128)(2,1)S(1)}, u32[]{:S(2)}, u32[]{:S(2)}) collective-permute-start(bf16[1,8,1024]{2,1,0:T(8,128)(2,1)S(1)} %get-tuple-element.46), channel_id=1, source_target_pairs={{0,8},{2,10},{4,12},{6,14},{8,0},{10,2},{12,4},{14,6},{16,24},{18,... | collective-permute-start | bytes 49160 | tf_op jit(solution)/shard_map/ppermute | solution.py:41
  35.9 2.4 %shard_map.97 = f32[128,4096]{1,0:T(8,128)} custom-call(bf16[128,1024]{1,0:T(8,128)(2,1)S(1)} %get-tuple-element.44.cot, bf16[128,512]{1,0:T(8,128)(2,1)S(1)} %get-tuple-element.45.tact), custom_call_target="tpu_custom_call" | custom-call | flops 134217728 | bytes 2097152 | tf_op jit(solution)/shard_map/pallas_call | solution.py:364
  38.3 0.0 collective-permute-done.15
  38.3 1.3 %collective-permute-done.14 = bf16[1,8,1024]{2,1,0:T(8,128)(2,1)S(1)} collective-permute-done((bf16[1,8,1024]{2,1,0:T(8,128)(2,1)S(1)}, bf16[1,8,1024]{2,1,0:T(8,128)(2,1)S(1)}, u32[]{:S(2)}, u32[]{:S(2)}) %collective-permute-start.14) | collective-permute-done | bytes 16416 | tf_op jit(solution)/shard_map/ppermute | solution.py:41
  39.6 0.0 collective-permute-done.13
  39.6 0.6 %reshape.22 = bf16[2,4096]{1,0:T(2,128)(2,1)} reshape(bf16[2,8,4,128]{3,2,1,0:T(4,128)(2,1)S(1)} %copy.11) | data formatting | bytes 32768 | tf_op jit(solution)/shard_map/reshape | solution.py:98
  (12 shorter events, 0.2 us)
Async XLA Ops:
  1.6 8.9 %collective-permute-start = (bf16[1,24,1024]{2,1,0:T(8,128)(2,1)S(1)}, bf16[1,24,1024]{2,1,0:T(8,128)(2,1)S(1)}, u32[]{:S(2)}, u32[]{:S(2)}) collective-permute-start(bf16[1,24,1024]{2,1,0:T(8,128)(2,1)S(1)} %reshape.21.refs_0_), channel_id=1, source_target_pairs={{24,0},{26,2},{28,4},{30,6},{16,8},{18,10},{20,12},{22,14},{8,16},... | collective-permute-start | bytes 147464 | tf_op jit(solution)/shard_map/ppermute | solution.py:36
  6.7 5.0 %collective-permute-start.1 = (bf16[1,24,1024]{2,1,0:T(8,128)(2,1)S(1)}, bf16[1,24,1024]{2,1,0:T(8,128)(2,1)S(1)}, u32[]{:S(2)}, u32[]{:S(2)}) collective-permute-start(bf16[1,24,1024]{2,1,0:T(8,128)(2,1)S(1)} %reshape.21.refs_0_), channel_id=1, source_target_pairs={{16,0},{18,2},{20,4},{22,6},{24,8},{26,10},{28,12},{30,14},{0,16},... | collective-permute-start | bytes 147464 | tf_op jit(solution)/shard_map/ppermute | solution.py:36
  6.7 5.0 %collective-permute-start.2 = (bf16[1,24,1024]{2,1,0:T(8,128)(2,1)S(1)}, bf16[1,24,1024]{2,1,0:T(8,128)(2,1)S(1)}, u32[]{:S(2)}, u32[]{:S(2)}) collective-permute-start(bf16[1,24,1024]{2,1,0:T(8,128)(2,1)S(1)} %reshape.21.refs_0_), channel_id=1, source_target_pairs={{8,0},{10,2},{12,4},{14,6},{0,8},{2,10},{4,12},{6,14},{24,16},{26,... | collective-permute-start | bytes 147464 | tf_op jit(solution)/shard_map/ppermute | solution.py:36
  7.3 5.1 %collective-permute-start.3 = (bf16[1,24,1024]{2,1,0:T(8,128)(2,1)S(1)}, bf16[1,24,1024]{2,1,0:T(8,128)(2,1)S(1)}, u32[]{:S(2)}, u32[]{:S(2)}) collective-permute-start(bf16[1,24,1024]{2,1,0:T(8,128)(2,1)S(1)} %reshape.21.refs_0_), channel_id=1, source_target_pairs={{6,0},{4,2},{2,4},{0,6},{14,8},{12,10},{10,12},{8,14},{22,16},{20,... | collective-permute-start | bytes 147464 | tf_op jit(solution)/shard_map/ppermute | solution.py:36
  9.9 5.0 %collective-permute-start.5 = (bf16[1,24,1024]{2,1,0:T(8,128)(2,1)S(1)}, bf16[1,24,1024]{2,1,0:T(8,128)(2,1)S(1)}, u32[]{:S(2)}, u32[]{:S(2)}) collective-permute-start(bf16[1,24,1024]{2,1,0:T(8,128)(2,1)S(1)} %reshape.21.refs_0_), channel_id=1, source_target_pairs={{4,0},{6,2},{0,4},{2,6},{12,8},{14,10},{8,12},{10,14},{20,16},{22,... | collective-permute-start | bytes 147464 | tf_op jit(solution)/shard_map/ppermute | solution.py:36
  10.4 5.2 %collective-permute-start.7 = (bf16[1,24,1024]{2,1,0:T(8,128)(2,1)S(1)}, bf16[1,24,1024]{2,1,0:T(8,128)(2,1)S(1)}, u32[]{:S(2)}, u32[]{:S(2)}) collective-permute-start(bf16[1,24,1024]{2,1,0:T(8,128)(2,1)S(1)} %reshape.21.refs_0_), channel_id=1, source_target_pairs={{2,0},{0,2},{6,4},{4,6},{10,8},{8,10},{14,12},{12,14},{18,16},{16,... | collective-permute-start | bytes 147464 | tf_op jit(solution)/shard_map/ppermute | solution.py:36
  12.4 8.3 %collective-permute-start.4 = (bf16[3,24,1024]{2,1,0:T(8,128)(2,1)S(1)}, bf16[3,24,1024]{2,1,0:T(8,128)(2,1)S(1)}, u32[]{:S(2)}, u32[]{:S(2)}) collective-permute-start(bf16[3,24,1024]{2,1,0:T(8,128)(2,1)S(1)} %constant_dynamic-update-slice_fusion.refs_1_), channel_id=1, source_target_pairs={{6,0},{4,2},{2,4},{0,6},{14,8},{12,10},{10,12},{8,14},{22,16},{20,... | collective-permute-start | bytes 442376 | tf_op jit(solution)/shard_map/ppermute | solution.py:36
  14.9 5.9 %collective-permute-start.6 = (bf16[3,24,1024]{2,1,0:T(8,128)(2,1)S(1)}, bf16[3,24,1024]{2,1,0:T(8,128)(2,1)S(1)}, u32[]{:S(2)}, u32[]{:S(2)}) collective-permute-start(bf16[3,24,1024]{2,1,0:T(8,128)(2,1)S(1)} %constant_dynamic-update-slice_fusion.refs_1_), channel_id=1, source_target_pairs={{4,0},{6,2},{0,4},{2,6},{12,8},{14,10},{8,12},{10,14},{20,16},{22,... | collective-permute-start | bytes 442376 | tf_op jit(solution)/shard_map/ppermute | solution.py:36
  15.6 5.3 %collective-permute-start.8 = (bf16[3,24,1024]{2,1,0:T(8,128)(2,1)S(1)}, bf16[3,24,1024]{2,1,0:T(8,128)(2,1)S(1)}, u32[]{:S(2)}, u32[]{:S(2)}) collective-permute-start(bf16[3,24,1024]{2,1,0:T(8,128)(2,1)S(1)} %constant_dynamic-update-slice_fusion.refs_1_), channel_id=1, source_target_pairs={{2,0},{0,2},{6,4},{4,6},{10,8},{8,10},{14,12},{12,14},{18,16},{16,... | collective-permute-start | bytes 442376 | tf_op jit(solution)/shard_map/ppermute | solution.py:36
  15.9 1.2 %copy-start = (bf16[4096,128]{1,0:T(8,128)(2,1)S(1)}, bf16[4096,128]{1,0:T(8,128)(2,1)}, u32[]{:S(2)}) copy-start(bf16[4096,128]{1,0:T(8,128)(2,1)} %refs_5_.1) | copy-start | bytes 3145732
  17.1 1.2 %copy-start.1 = (bf16[4096,128]{1,0:T(8,128)(2,1)S(1)}, bf16[4096,128]{1,0:T(8,128)(2,1)}, u32[]{:S(2)}) copy-start(bf16[4096,128]{1,0:T(8,128)(2,1)} %refs_6_.1) | copy-start | bytes 3145732
  18.4 1.2 %copy-start.2 = (bf16[128,4096]{1,0:T(8,128)(2,1)S(1)}, bf16[128,4096]{1,0:T(8,128)(2,1)}, u32[]{:S(2)}) copy-start(bf16[128,4096]{1,0:T(8,128)(2,1)} %refs_7_.1) | copy-start | bytes 3145732
  21.7 1.4 %collective-permute-start.9 = (f32[2,16,8,128]{3,2,1,0:T(8,128)S(1)}, f32[2,16,8,128]{3,2,1,0:T(8,128)S(1)}, u32[]{:S(2)}, u32[]{:S(2)}) collective-permute-start(f32[2,16,8,128]{3,2,1,0:T(8,128)S(1)} %get-tuple-element.34.refs_0_), channel_id=1, source_target_pairs={{0,1},{1,0},{2,3},{3,2},{4,5},{5,4},{6,7},{7,6},{8,9},{9,8},{10,11... | collective-permute-start | bytes 393224 | tf_op jit(solution)/shard_map/ppermute | solution.py:396
  24.0 6.6 %collective-permute-start.12 = (bf16[4,8,1024]{2,1,0:T(8,128)(2,1)S(1)}, bf16[4,8,1024]{2,1,0:T(8,128)(2,1)S(1)}, u32[]{:S(2)}, u32[]{:S(2)}) collective-permute-start(bf16[4,8,1024]{2,1,0:T(8,128)(2,1)S(1)} %get-tuple-element.38), channel_id=1, source_target_pairs={{0,6},{2,4},{4,2},{6,0},{8,14},{10,12},{12,10},{14,8},{16,22},{18,... | collective-permute-start | bytes 196616 | tf_op jit(solution)/shard_map/ppermute | solution.py:41
  26.4 4.3 %collective-permute-start.11 = (bf16[4,8,1024]{2,1,0:T(8,128)(2,1)S(1)}, bf16[4,8,1024]{2,1,0:T(8,128)(2,1)S(1)}, u32[]{:S(2)}, u32[]{:S(2)}) collective-permute-start(bf16[4,8,1024]{2,1,0:T(8,128)(2,1)S(1)} %get-tuple-element.37), channel_id=1, source_target_pairs={{0,4},{2,6},{4,0},{6,2},{8,12},{10,14},{12,8},{14,10},{16,20},{18,... | collective-permute-start | bytes 196616 | tf_op jit(solution)/shard_map/ppermute | solution.py:41
  27.1 4.3 %collective-permute-start.10 = (bf16[4,8,1024]{2,1,0:T(8,128)(2,1)S(1)}, bf16[4,8,1024]{2,1,0:T(8,128)(2,1)S(1)}, u32[]{:S(2)}, u32[]{:S(2)}) collective-permute-start(bf16[4,8,1024]{2,1,0:T(8,128)(2,1)S(1)} %get-tuple-element.36), channel_id=1, source_target_pairs={{0,2},{2,0},{4,6},{6,4},{8,10},{10,8},{12,14},{14,12},{16,18},{18,... | collective-permute-start | bytes 196616 | tf_op jit(solution)/shard_map/ppermute | solution.py:41
  31.4 6.9 %collective-permute-start.15 = (bf16[1,8,1024]{2,1,0:T(8,128)(2,1)S(1)}, bf16[1,8,1024]{2,1,0:T(8,128)(2,1)S(1)}, u32[]{:S(2)}, u32[]{:S(2)}) collective-permute-start(bf16[1,8,1024]{2,1,0:T(8,128)(2,1)S(1)} %get-tuple-element.47), channel_id=1, source_target_pairs={{0,24},{2,26},{4,28},{6,30},{8,16},{10,18},{12,20},{14,22},{16,8},... | collective-permute-start | bytes 49160 | tf_op jit(solution)/shard_map/ppermute | solution.py:41
  34.9 4.6 %collective-permute-start.14 = (bf16[1,8,1024]{2,1,0:T(8,128)(2,1)S(1)}, bf16[1,8,1024]{2,1,0:T(8,128)(2,1)S(1)}, u32[]{:S(2)}, u32[]{:S(2)}) collective-permute-start(bf16[1,8,1024]{2,1,0:T(8,128)(2,1)S(1)} %get-tuple-element.48), channel_id=1, source_target_pairs={{0,16},{2,18},{4,20},{6,22},{8,24},{10,26},{12,28},{14,30},{16,0},... | collective-permute-start | bytes 49160 | tf_op jit(solution)/shard_map/ppermute | solution.py:41
  35.0 4.6 %collective-permute-start.13 = (bf16[1,8,1024]{2,1,0:T(8,128)(2,1)S(1)}, bf16[1,8,1024]{2,1,0:T(8,128)(2,1)S(1)}, u32[]{:S(2)}, u32[]{:S(2)}) collective-permute-start(bf16[1,8,1024]{2,1,0:T(8,128)(2,1)S(1)} %get-tuple-element.46), channel_id=1, source_target_pairs={{0,8},{2,10},{4,12},{6,14},{8,0},{10,2},{12,4},{14,6},{16,24},{18,... | collective-permute-start | bytes 49160 | tf_op jit(solution)/shard_map/ppermute | solution.py:41

commit v6 on v5

--- a/solution.py
+++ b/solution.py
@@ -50,24 +50,40 @@
 
 
 def gather_blocks(own, axis, size):
-    early, late = [own], []
+    early, late, count = [(own, [0])], [], 1
+    before = None
     for level in levels_of(size):
-        early, late = early + late, []
-        rest = early[1:]
-        offsets = offsets_of(level[1])
-        held = jnp.concatenate(rest) if rest else None
-        mine = [fetch(own, axis, size, level, o) for o in offsets]
+        rest = early[1:] + late
+        offsets = list(offsets_of(level[1]))
+        slots = {o: count * (k + 1) for k, o in enumerate(offsets)}
+        starts = offsets[::-1] if rest else offsets
+        mine = {o: fetch(own, axis, size, level, o) for o in starts}
+        late = [(mine[o], [slots[o]]) for o in starts]
+        early = [(own, [0])]
         if rest:
-            late = [
-                fetch(after(held, came), axis, size, level, o)
-                for o, came in zip(offsets, mine)
-            ]
-            early = [own, held]
-            if level[0] > 1:
-                late = [x for pair in zip(mine, late) for x in pair]
-                mine = []
-        early = early + mine
-    return early, late
+            held = join(rest)
+            step, near = before
+            far = join([piece for piece in rest if piece[1] != [near]])
+            early, late = early + [held] + late, []
+            for o, first in zip(offsets, starts[:1] * 2 + starts[1:]):
+                part, ids = far if o & (o - 1) else held
+                block = fetch(after(part, mine[first]), axis, size, level, o)
+                late.append((block, [slots[o] + i for i in ids]))
+            for o in offsets:
+                if o & (o - 1):
+                    block = fetch(mine[o], axis, size, step, 1)
+                    late.append((block, [slots[o] + near]))
+        before = level, slots[1]
+        count *= level[1]
+    pieces = early + late
+    ids = sum((ids for _, ids in pieces), [])
+    order = [ids.index(k) for k in range(count)]
+    return [block for block, _ in early], [block for block, _ in late], order
+
+
+def join(pieces):
+    blocks = jnp.concatenate([block for block, _ in pieces])
+    return blocks, sum((ids for _, ids in pieces), [])
 
 
 def scatter_sum(groups, axis, size, beside):
@@ -200,7 +216,7 @@
         in_specs=[vmem] * len(pieces) + [pl.BlockSpec(memory_space=pltpu.HBM)] * 3,
         out_specs=(vmem,) * 6,
         scratch_shapes=[pltpu.SemaphoreType.DMA((3,))],
-        compiler_params=pltpu.CompilerParams(vmem_limit_bytes=VMEM_LIMIT),
+        compiler_params=pltpu.CompilerParams(vmem_limit_bytes=50 * 2**20),
         cost_estimate=pl.CostEstimate(
             flops=blocks * 8 * 10 * SLOTS * lanes * hidden,
             bytes_accessed=sum(4 * w.size for w in weights),
@@ -259,7 +275,7 @@
     ).astype(jnp.bfloat16)
 
 
-def middle_kernel(n_parts, groups, *refs):
+def middle_kernel(n_parts, groups, order, *refs):
     parts, (gate_w, up_w) = refs[:n_parts], refs[n_parts : n_parts + 2]
     factor_out, tact_out = refs[n_parts + 2 : n_parts + 4]
     own_out, others_out = refs[n_parts + 4], refs[n_parts + 5 :]
@@ -282,21 +298,19 @@
     )
     hvp = hvp.reshape(blocks, 8, hvp.shape[1])
     inner = blocks // groups
-    own_out[...] = hvp[:inner]
-    early = inner + groups - 1
-    for g, out in enumerate(others_out):
-        at = early + g * (inner - 1)
-        out[0] = hvp[inner + g].astype(out.dtype)
-        out[1:] = hvp[at : at + inner - 1].astype(out.dtype)
-
-
-def middle(parts, gate_w, up_w, groups):
+    for k, at in enumerate(order):
+        group, place_in = divmod(k, inner)
+        out = others_out[group - 1] if group else own_out
+        out[place_in] = hvp[at].astype(out.dtype)
+
+
+def middle(parts, gate_w, up_w, groups, order):
     _, blocks, _, hidden = parts[0].shape
     lanes = gate_w.shape[0] // SLOTS
     vmem = pl.BlockSpec(memory_space=pltpu.VMEM)
     group = (blocks // groups, 8, lanes)
     return pl.pallas_call(
-        functools.partial(middle_kernel, len(parts), groups),
+        functools.partial(middle_kernel, len(parts), groups, order),
         out_shape=(
             jax.ShapeDtypeStruct((blocks * 16, SLOTS * 2 * hidden), jnp.bfloat16),
             jax.ShapeDtypeStruct((blocks * 8, SLOTS * hidden), jnp.bfloat16),
@@ -315,31 +329,38 @@
     )
 
 
-def up_grads_kernel(pt, factor, gate_out, up_out):
-    hidden = gate_out.shape[1]
-    for m in range(pt.shape[1] // LANES):
+def up_grads_kernel(pt, factor, gate_out, up_out, gate_tiles, up_tiles, sems):
+    tiles, _, hidden = gate_tiles.shape
+    copies = []
+    for m in range(tiles):
         both = contract_first(pt[:, m * LANES : (m + 1) * LANES], factor[...])
         for s in range(SLOTS):
-            at = (m * SLOTS + s) * LANES
-            half = 2 * s * hidden
-            gate_out[at : at + LANES] = both[:, half : half + hidden]
-            up_out[at : at + LANES] = both[:, half + hidden : half + 2 * hidden]
-
-
-def up_grads(pt, factor, steps):
+            at, half = slice(s * LANES, (s + 1) * LANES), 2 * s * hidden
+            gate_tiles[m, at] = both[:, half : half + hidden]
+            up_tiles[m, at] = both[:, half + hidden : half + 2 * hidden]
+        rows = slice(m * SLOTS * LANES, (m + 1) * SLOTS * LANES)
+        for k, (tile, out) in enumerate(((gate_tiles, gate_out), (up_tiles, up_out))):
+            copies.append(pltpu.make_async_copy(tile.at[m], out.at[rows], sems.at[m, k]))
+            copies[-1].start()
+    for copy in copies:
+        copy.wait()
+
+
+def up_grads(pt, factor):
     rows, lanes = pt.shape
-    hidden = factor.shape[1] // (2 * SLOTS)
+    tiles, hidden = lanes // LANES, factor.shape[1] // (2 * SLOTS)
     out = jax.ShapeDtypeStruct((SLOTS * lanes, hidden), jnp.float32)
-    spec = pl.BlockSpec((SLOTS * lanes // steps, hidden), lambda m: (m, 0))
+    vmem = pl.BlockSpec(memory_space=pltpu.VMEM)
     return pl.pallas_call(
         up_grads_kernel,
-        grid=(steps,),
         out_shape=(out, out),
-        in_specs=[
-            pl.BlockSpec((rows, lanes // steps), lambda m: (0, m)),
-            pl.BlockSpec(memory_space=pltpu.VMEM),
+        in_specs=[vmem] * 2,
+        out_specs=(pl.BlockSpec(memory_space=pltpu.HBM),) * 2,
+        scratch_shapes=[
+            pltpu.VMEM((tiles, SLOTS * LANES, hidden), jnp.float32),
+            pltpu.VMEM((tiles, SLOTS * LANES, hidden), jnp.float32),
+            pltpu.SemaphoreType.DMA((tiles, 2)),
         ],
-        out_specs=(spec, spec),
         compiler_params=pltpu.CompilerParams(vmem_limit_bytes=VMEM_LIMIT),
         cost_estimate=pl.CostEstimate(
             flops=2 * pt.size * factor.shape[1],
@@ -349,27 +370,36 @@
     )(pt, factor)
 
 
-def down_grad_kernel(cot, tact, down_out):
-    hidden = down_out.shape[0]
-    for m in range(cot.shape[1] // LANES):
-        tiles = contract_first(tact[...], cot[:, m * LANES : (m + 1) * LANES])
+def down_grad_kernel(cot, tact, down_out, down_tiles, sems):
+    tiles, hidden, _ = down_tiles.shape
+    copies = []
+    for m in range(tiles):
+        down = contract_first(tact[...], cot[:, m * LANES : (m + 1) * LANES])
         for s in range(SLOTS):
-            at = (m * SLOTS + s) * LANES
-            down_out[:, at : at + LANES] = tiles[s * hidden : (s + 1) * hidden]
-
-
-def down_grad(cot, tact, steps):
-    rows, lanes = cot.shape
-    hidden = tact.shape[1] // SLOTS
+            at = slice(s * LANES, (s + 1) * LANES)
+            down_tiles[m, :, at] = down[s * hidden : (s + 1) * hidden]
+        columns = slice(m * SLOTS * LANES, (m + 1) * SLOTS * LANES)
+        copies.append(
+            pltpu.make_async_copy(down_tiles.at[m], down_out.at[:, columns], sems.at[m])
+        )
+        copies[-1].start()
+    for copy in copies:
+        copy.wait()
+
+
+def down_grad(cot, tact):
+    lanes = cot.shape[1]
+    tiles, hidden = lanes // LANES, tact.shape[1] // SLOTS
+    vmem = pl.BlockSpec(memory_space=pltpu.VMEM)
     return pl.pallas_call(
         down_grad_kernel,
-        grid=(steps,),
         out_shape=jax.ShapeDtypeStruct((hidden, SLOTS * lanes), jnp.float32),
-        in_specs=[
-            pl.BlockSpec((rows, lanes // steps), lambda m: (0, m)),
-            pl.BlockSpec(memory_space=pltpu.VMEM),
+        in_specs=[vmem] * 2,
+        out_specs=pl.BlockSpec(memory_space=pltpu.HBM),
+        scratch_shapes=[
+            pltpu.VMEM((tiles, hidden, SLOTS * LANES), jnp.float32),
+            pltpu.SemaphoreType.DMA((tiles,)),
         ],
-        out_specs=pl.BlockSpec((hidden, SLOTS * lanes // steps), lambda m: (0, m)),
         compiler_params=pltpu.CompilerParams(vmem_limit_bytes=VMEM_LIMIT),
         cost_estimate=pl.CostEstimate(
             flops=2 * cot.size * tact.shape[1],
@@ -384,7 +414,7 @@
 
     def local(primal_in, tangent_in, cotangent, gate_weight, up_weight, down_weight):
         weights = (gate_weight, up_weight, down_weight)
-        early, late = gather_blocks(
+        early, late, order = gather_blocks(
             fold(primal_in, tangent_in, cotangent), "wide", wide
         )
         *first, gate_weight, up_weight, down_weight = begin(early, weights)
@@ -395,12 +425,11 @@
             pairs = [(i, (i + shift) % narrow) for i in range(narrow)]
             parts.append(lax.ppermute(part, "narrow", pairs))
         groups = levels_of(wide)[-1][1]
-        factor, tact, *hvp = middle(parts, gate_weight, up_weight, groups)
-        steps = max(1, pt.shape[1] // (2 * LANES))
-        gate_grad, up_grad = up_grads(pt, factor, steps)
+        factor, tact, *hvp = middle(parts, gate_weight, up_weight, groups, order)
+        gate_grad, up_grad = up_grads(pt, factor)
         total = scatter_sum(hvp, "wide", wide, gate_grad)
         input_hvp = unfold(total[0].astype(jnp.bfloat16))
-        return (input_hvp, gate_grad, up_grad, down_grad(cot, tact, steps))
+        return (input_hvp, gate_grad, up_grad, down_grad(cot, tact))
 
     return jax.shard_map(
         local,

time: 40.6 us -> 39.8 us (0.980)
  local copies, waits for them, and re-layouts: 4.41 us -> 0.73 us
  starting transfers between devices: 20.8 us -> 23.2 us
    unnamed x9 -> x3, local copies, waits for them, and re-layouts: 3.69 us -> 0.01 us
    ppermute x9 -> x10, starting transfers between devices: 12.7 us -> 15.1 us  [fetch(): return lax.ppermute(value, axis, pairs)]
    pallas_call x1, Pallas kernels: 1.08 us -> 2.7 us  [begin(): pl.pallas_call(functools.partial(begin_kernel, len(pieces)), out_shape=(j...]
    pallas_call x3, Pallas kernels: 6.31 us -> 4.93 us  [the longest x1 2.42 us: up_grads(): pl.pallas_call(up_grads_kernel, out_shape=(out, out), in_specs=[vmem] * 2...]
    ppermute x6, waiting for transfers between devices: 2.03 us -> 3.08 us  [deliver(): return lax.ppermute(value, axis, pairs)]
    ppermute x9 -> x10, waiting for transfers between devices: 1.81 us -> 1.07 us  [fetch(): return lax.ppermute(value, axis, pairs)]
  transfers between devices with their start and end apart: 16 -> 17, of which waited for: 7 -> 7; matrix products, arithmetic and copies ran while one was open for 0% -> 0% of each run, Pallas kernels for 16% -> 17%
where the time goes in v6:
time: 39.8 us; the launch traced here: 39.5 us
  starting transfers between devices  23.2 us (58%)
  Pallas kernels  8.44 us (21%)
  waiting for transfers between devices  5.48 us (14%)
  other arithmetic  0.89 us (2%)
  between operations  0.78 us (2%)
  local copies, waits for them, and re-layouts  0.73 us (2%)
    ppermute x10, starting transfers between devices, fetch(): return lax.ppermute(value, axis, pairs)  15.1 us
    ppermute x6, starting transfers between devices, deliver(): return lax.ppermute(value, axis, pairs)  8.01 us
    ppermute x6, waiting for transfers between devices, deliver(): return lax.ppermute(value, axis, pairs)  3.08 us
    pallas_call x1, Pallas kernels, begin(): pl.pallas_call(functools.partial(begin_kernel, len(pieces)), out_shape=(j...  2.7 us
    pallas_call x1, Pallas kernels, up_grads(): pl.pallas_call(up_grads_kernel, out_shape=(out, out), in_specs=[vmem] * 2...  2.42 us
    pallas_call x1, Pallas kernels, down_grad(): pl.pallas_call(down_grad_kernel, out_shape=jax.ShapeDtypeStruct((hidden,...  1.64 us
    ppermute x1, waiting for transfers between devices, local(): parts.append(lax.ppermute(part, 'narrow', pairs))  1.33 us
    ppermute x10, waiting for transfers between devices, fetch(): return lax.ppermute(value, axis, pairs)  1.07 us
  transfers between devices with their start and end apart: 17, of which 7 were waited for; matrix products, arithmetic and copies ran while one was open for 0% of the time, Pallas kernels for 17%

profile of v6, /device:TPU:0, one launch (start us, length us, event | category | flops | bytes accessed | tf_op | source)
XLA Modules:
  0.0 39.5 jit_solution(17520412182873114317)
XLA Ops:
  0.6 0.8 %pad_maximum_fusion.1 = bf16[3,2,4096]{2,1,0:T(2,128)(2,1)S(1)} fusion(bf16[1,2,4096]{2,1,0:T(2,128)(2,1)} %bitcast.17, bf16[1,2,4096]{2,1,0:T(2,128)(2,1)} %bitcast.18, bf16[1,2,4096]{2,1,0:T(2,128)(2,1)} %bitcast.19), kind=kLoop, calls=%fused_computation.2 | loop fusion | flops 49152 | bytes 98304 | tf_op jit(solution)/shard_map/stack | solution.py:105
  1.6 5.1 %collective-permute-start = (bf16[1,24,1024]{2,1,0:T(8,128)(2,1)S(1)}, bf16[1,24,1024]{2,1,0:T(8,128)(2,1)S(1)}, u32[]{:S(2)}, u32[]{:S(2)}) collective-permute-start(bf16[1,24,1024]{2,1,0:T(8,128)(2,1)S(1)} %reshape.21.refs_0_), channel_id=1, source_target_pairs={{24,0},{26,2},{28,4},{30,6},{16,8},{18,10},{20,12},{22,14},{8,16},... | collective-permute-start | bytes 147464 | tf_op jit(solution)/shard_map/ppermute | solution.py:36
  6.7 0.0 collective-permute-start.1
  6.7 1.5 %collective-permute-start.2 = (bf16[1,24,1024]{2,1,0:T(8,128)(2,1)S(1)}, bf16[1,24,1024]{2,1,0:T(8,128)(2,1)S(1)}, u32[]{:S(2)}, u32[]{:S(2)}) collective-permute-start(bf16[1,24,1024]{2,1,0:T(8,128)(2,1)S(1)} %reshape.21.refs_0_), channel_id=1, source_target_pairs={{2,0},{0,2},{6,4},{4,6},{10,8},{8,10},{14,12},{12,14},{18,16},{16,... | collective-permute-start | bytes 147464 | tf_op jit(solution)/shard_map/ppermute | solution.py:36
  8.2 0.8 %collective-permute-start.4 = (bf16[1,24,1024]{2,1,0:T(8,128)(2,1)S(1)}, bf16[1,24,1024]{2,1,0:T(8,128)(2,1)S(1)}, u32[]{:S(2)}, u32[]{:S(2)}) collective-permute-start(bf16[1,24,1024]{2,1,0:T(8,128)(2,1)S(1)} %reshape.21.refs_0_), channel_id=1, source_target_pairs={{8,0},{10,2},{12,4},{14,6},{0,8},{2,10},{4,12},{6,14},{24,16},{26,... | collective-permute-start | bytes 147464 | tf_op jit(solution)/shard_map/ppermute | solution.py:36
  9.0 1.5 %collective-permute-start.6 = (bf16[1,24,1024]{2,1,0:T(8,128)(2,1)S(1)}, bf16[1,24,1024]{2,1,0:T(8,128)(2,1)S(1)}, u32[]{:S(2)}, u32[]{:S(2)}) collective-permute-start(bf16[1,24,1024]{2,1,0:T(8,128)(2,1)S(1)} %reshape.21.refs_0_), channel_id=1, source_target_pairs={{4,0},{6,2},{0,4},{2,6},{12,8},{14,10},{8,12},{10,14},{20,16},{22,... | collective-permute-start | bytes 147464 | tf_op jit(solution)/shard_map/ppermute | solution.py:36
  10.5 0.0 collective-permute-done
  10.5 1.2 %collective-permute-start.8 = (bf16[1,24,1024]{2,1,0:T(8,128)(2,1)S(1)}, bf16[1,24,1024]{2,1,0:T(8,128)(2,1)S(1)}, u32[]{:S(2)}, u32[]{:S(2)}) collective-permute-start(bf16[1,24,1024]{2,1,0:T(8,128)(2,1)S(1)} %reshape.21.refs_0_), channel_id=1, source_target_pairs={{6,0},{4,2},{2,4},{0,6},{14,8},{12,10},{10,12},{8,14},{22,16},{20,... | collective-permute-start | bytes 147464 | tf_op jit(solution)/shard_map/ppermute | solution.py:36
  11.7 0.0 collective-permute-done.1
  11.7 0.6 %collective-permute-done.4 = bf16[1,24,1024]{2,1,0:T(8,128)(2,1)S(1)} collective-permute-done((bf16[1,24,1024]{2,1,0:T(8,128)(2,1)S(1)}, bf16[1,24,1024]{2,1,0:T(8,128)(2,1)S(1)}, u32[]{:S(2)}, u32[]{:S(2)}) %collective-permute-start.4) | collective-permute-done | bytes 49184 | tf_op jit(solution)/shard_map/ppermute | solution.py:36
  12.3 0.0 collective-permute-done.2.refs_2_
  12.3 1.6 %collective-permute-start.5 = (bf16[3,24,1024]{2,1,0:T(8,128)(2,1)S(1)}, bf16[3,24,1024]{2,1,0:T(8,128)(2,1)S(1)}, u32[]{:S(2)}, u32[]{:S(2)}) collective-permute-start(bf16[3,24,1024]{2,1,0:T(8,128)(2,1)S(1)} %constant_dynamic-update-slice_fusion.refs_1_), channel_id=1, source_target_pairs={{4,0},{6,2},{0,4},{2,6},{12,8},{14,10},{8,12},{10,14},{20,16},{22,... | collective-permute-start | bytes 442376 | tf_op jit(solution)/shard_map/ppermute | solution.py:36
  13.9 0.0 collective-permute-done.6.refs_3_
  13.9 1.1 %collective-permute-start.7 = (bf16[3,24,1024]{2,1,0:T(8,128)(2,1)S(1)}, bf16[3,24,1024]{2,1,0:T(8,128)(2,1)S(1)}, u32[]{:S(2)}, u32[]{:S(2)}) collective-permute-start(bf16[3,24,1024]{2,1,0:T(8,128)(2,1)S(1)} %constant_dynamic-update-slice_fusion.refs_1_), channel_id=1, source_target_pairs={{2,0},{0,2},{6,4},{4,6},{10,8},{8,10},{14,12},{12,14},{18,16},{16,... | collective-permute-start | bytes 442376 | tf_op jit(solution)/shard_map/ppermute | solution.py:36
  14.9 1.2 %collective-permute-start.3 = (bf16[2,24,1024]{2,1,0:T(8,128)(2,1)S(1)}, bf16[2,24,1024]{2,1,0:T(8,128)(2,1)S(1)}, u32[]{:S(2)}, u32[]{:S(2)}) collective-permute-start(bf16[2,24,1024]{2,1,0:T(8,128)(2,1)S(1)} %pad_maximum_fusion), channel_id=1, source_target_pairs={{6,0},{4,2},{2,4},{0,6},{14,8},{12,10},{10,12},{8,14},{22,16},{20,... | collective-permute-start | bytes 294920 | tf_op jit(solution)/shard_map/ppermute | solution.py:36
  16.1 0.0 collective-permute-done.8.refs_4_
  16.1 1.2 %collective-permute-start.9 = (bf16[1,24,1024]{2,1,0:T(8,128)(2,1)S(1)}, bf16[1,24,1024]{2,1,0:T(8,128)(2,1)S(1)}, u32[]{:S(2)}, u32[]{:S(2)}) collective-permute-start(bf16[1,24,1024]{2,1,0:T(8,128)(2,1)S(1)} %collective-permute-done.8.refs_4_), channel_id=1, source_target_pairs={{8,0},{10,2},{12,4},{14,6},{0,8},{2,10},{4,12},{6,14},{24,16},{26,... | collective-permute-start | bytes 147464 | tf_op jit(solution)/shard_map/ppermute | solution.py:36
  17.4 2.7 %shard_map.93 = (bf16[112,1024]{1,0:T(8,128)(2,1)S(1)}, bf16[56,1024]{1,0:T(8,128)(2,1)S(1)}, f32[2,7,8,128]{3,2,1,0:T(8,128)S(1)}, bf16[4096,128]{1,0:T(8,128)(...) custom-call(bf16[1,24,1024]{2,1,0:T(8,128)(2,1)S(1)} %reshape.21.refs_0_, ...), custom_call_target="tpu_custom_call" | custom-call | flops 293601280 | bytes 6291456 | tf_op jit(solution)/shard_map/pallas_call | solution.py:208
  20.1 0.1 collective-permute-done.9.refs_3_
  20.2 0.3 collective-permute-done.3.refs_0_
  20.5 0.0 collective-permute-done.5.refs_1_
  20.5 0.0 collective-permute-done.7.refs_2_
  20.5 0.8 %shard_map.94 = (bf16[256,1024]{1,0:T(8,128)(2,1)S(1)}, bf16[128,1024]{1,0:T(8,128)(2,1)S(1)}, f32[2,16,8,128]{3,2,1,0:T(8,128)S(1)}) custom-call(bf16[2,24,1024]{2,1,0:T(8,128)(2,1)S(1)} %collective-permute-done.3.refs_0_, bf16[3,24,1024]{2,1,0:T(8,128)(2,1)S(1)} %collective-permute-done.5.refs_1_, bf16[3,24,1024]{2,1,0:T(8,128)(2,1)S(1)} %collective-permute-done.7.refs_2_, ...), custom_call_target="tpu_custom_call" | custom-call | tf_op jit(solution)/shard_map/pallas_call | solution.py:245
  21.3 0.1 collective-permute-start.10
  21.4 1.3 %collective-permute-done.10.refs_1_ = f32[2,16,8,128]{3,2,1,0:T(8,128)S(1)} collective-permute-done((f32[2,16,8,128]{3,2,1,0:T(8,128)S(1)}, f32[2,16,8,128]{3,2,1,0:T(8,128)S(1)}, u32[]{:S(2)}, u32[]{:S(2)}) %collective-permute-start.10) | collective-permute-done | bytes 131104 | tf_op jit(solution)/shard_map/ppermute | solution.py:426
  22.8 0.9 %shard_map.95 = (bf16[256,1024]{1,0:T(8,128)(2,1)S(1)}, bf16[128,512]{1,0:T(8,128)(2,1)S(1)}, f32[4,8,1024]{2,1,0:T(8,128)S(1)}, bf16[4,8,1024]{2,1,0:T(8,128)(2...) custom-call(f32[2,16,8,128]{3,2,1,0:T(8,128)S(1)} %get-tuple-element.34.refs_0_, ...), custom_call_target="tpu_custom_call" | custom-call | tf_op jit(solution)/shard_map/pallas_call | solution.py:312
  23.6 1.8 %collective-permute-start.13 = (bf16[4,8,1024]{2,1,0:T(8,128)(2,1)S(1)}, bf16[4,8,1024]{2,1,0:T(8,128)(2,1)S(1)}, u32[]{:S(2)}, u32[]{:S(2)}) collective-permute-start(bf16[4,8,1024]{2,1,0:T(8,128)(2,1)S(1)} %get-tuple-element.38), channel_id=1, source_target_pairs={{0,6},{2,4},{4,2},{6,0},{8,14},{10,12},{12,10},{14,8},{16,22},{18,... | collective-permute-start | bytes 196616 | tf_op jit(solution)/shard_map/ppermute | solution.py:41
  25.4 0.7 %collective-permute-start.12 = (bf16[4,8,1024]{2,1,0:T(8,128)(2,1)S(1)}, bf16[4,8,1024]{2,1,0:T(8,128)(2,1)S(1)}, u32[]{:S(2)}, u32[]{:S(2)}) collective-permute-start(bf16[4,8,1024]{2,1,0:T(8,128)(2,1)S(1)} %get-tuple-element.37), channel_id=1, source_target_pairs={{0,4},{2,6},{4,0},{6,2},{8,12},{10,14},{12,8},{14,10},{16,20},{18,... | collective-permute-start | bytes 196616 | tf_op jit(solution)/shard_map/ppermute | solution.py:41
  26.1 1.1 %collective-permute-start.11 = (bf16[4,8,1024]{2,1,0:T(8,128)(2,1)S(1)}, bf16[4,8,1024]{2,1,0:T(8,128)(2,1)S(1)}, u32[]{:S(2)}, u32[]{:S(2)}) collective-permute-start(bf16[4,8,1024]{2,1,0:T(8,128)(2,1)S(1)} %get-tuple-element.36), channel_id=1, source_target_pairs={{0,2},{2,0},{4,6},{6,4},{8,10},{10,8},{12,14},{14,12},{16,18},{18,... | collective-permute-start | bytes 196616 | tf_op jit(solution)/shard_map/ppermute | solution.py:41
  27.2 2.4 %shard_map.96 = (f32[4096,128]{1,0:T(8,128)}, f32[4096,128]{1,0:T(8,128)}) custom-call(bf16[256,1024]{1,0:T(8,128)(2,1)S(1)} %get-tuple-element.39.pt, bf16[256,1024]{1,0:T(8,128)(2,1)S(1)} %get-tuple-element.40.factor), custom_call_target="tpu_custom_call" | custom-call | flops 536870912 | bytes 4194304 | tf_op jit(solution)/shard_map/pallas_call | solution.py:354
  29.6 0.0 collective-permute-done.13
  29.6 0.5 %collective-permute-done.12 = bf16[4,8,1024]{2,1,0:T(8,128)(2,1)S(1)} collective-permute-done((bf16[4,8,1024]{2,1,0:T(8,128)(2,1)S(1)}, bf16[4,8,1024]{2,1,0:T(8,128)(2,1)S(1)}, u32[]{:S(2)}, u32[]{:S(2)}) %collective-permute-start.12) | collective-permute-done | bytes 65568 | tf_op jit(solution)/shard_map/ppermute | solution.py:41
  30.2 0.2 collective-permute-done.11
  30.5 3.8 %collective-permute-start.16 = (bf16[1,8,1024]{2,1,0:T(8,128)(2,1)S(1)}, bf16[1,8,1024]{2,1,0:T(8,128)(2,1)S(1)}, u32[]{:S(2)}, u32[]{:S(2)}) collective-permute-start(bf16[1,8,1024]{2,1,0:T(8,128)(2,1)S(1)} %get-tuple-element.47), channel_id=1, source_target_pairs={{0,24},{2,26},{4,28},{6,30},{8,16},{10,18},{12,20},{14,22},{16,8},... | collective-permute-start | bytes 49160 | tf_op jit(solution)/shard_map/ppermute | solution.py:41
  34.2 0.0 collective-permute-start.15
  34.2 0.7 %collective-permute-start.14 = (bf16[1,8,1024]{2,1,0:T(8,128)(2,1)S(1)}, bf16[1,8,1024]{2,1,0:T(8,128)(2,1)S(1)}, u32[]{:S(2)}, u32[]{:S(2)}) collective-permute-start(bf16[1,8,1024]{2,1,0:T(8,128)(2,1)S(1)} %get-tuple-element.46), channel_id=1, source_target_pairs={{0,8},{2,10},{4,12},{6,14},{8,0},{10,2},{12,4},{14,6},{16,24},{18,... | collective-permute-start | bytes 49160 | tf_op jit(solution)/shard_map/ppermute | solution.py:41
  34.9 1.6 %shard_map.97 = f32[128,4096]{1,0:T(8,128)} custom-call(bf16[128,1024]{1,0:T(8,128)(2,1)S(1)} %get-tuple-element.44.cot, bf16[128,512]{1,0:T(8,128)(2,1)S(1)} %get-tuple-element.45.tact), custom_call_target="tpu_custom_call" | custom-call | flops 134217728 | bytes 2097152 | tf_op jit(solution)/shard_map/pallas_call | solution.py:394
  36.6 0.0 collective-permute-done.16
  36.6 2.3 %collective-permute-done.15 = bf16[1,8,1024]{2,1,0:T(8,128)(2,1)S(1)} collective-permute-done((bf16[1,8,1024]{2,1,0:T(8,128)(2,1)S(1)}, bf16[1,8,1024]{2,1,0:T(8,128)(2,1)S(1)}, u32[]{:S(2)}, u32[]{:S(2)}) %collective-permute-start.15) | collective-permute-done | bytes 16416 | tf_op jit(solution)/shard_map/ppermute | solution.py:41
  38.9 0.0 collective-permute-done.14
  38.9 0.6 %reshape.22 = bf16[2,4096]{1,0:T(2,128)(2,1)} reshape(bf16[2,8,4,128]{3,2,1,0:T(4,128)(2,1)S(1)} %copy.11) | data formatting | bytes 32768 | tf_op jit(solution)/shard_map/reshape | solution.py:114
  (13 shorter events, 0.2 us)
Async XLA Ops:
  1.6 8.9 %collective-permute-start = (bf16[1,24,1024]{2,1,0:T(8,128)(2,1)S(1)}, bf16[1,24,1024]{2,1,0:T(8,128)(2,1)S(1)}, u32[]{:S(2)}, u32[]{:S(2)}) collective-permute-start(bf16[1,24,1024]{2,1,0:T(8,128)(2,1)S(1)} %reshape.21.refs_0_), channel_id=1, source_target_pairs={{24,0},{26,2},{28,4},{30,6},{16,8},{18,10},{20,12},{22,14},{8,16},... | collective-permute-start | bytes 147464 | tf_op jit(solution)/shard_map/ppermute | solution.py:36
  6.7 5.0 %collective-permute-start.1 = (bf16[1,24,1024]{2,1,0:T(8,128)(2,1)S(1)}, bf16[1,24,1024]{2,1,0:T(8,128)(2,1)S(1)}, u32[]{:S(2)}, u32[]{:S(2)}) collective-permute-start(bf16[1,24,1024]{2,1,0:T(8,128)(2,1)S(1)} %reshape.21.refs_0_), channel_id=1, source_target_pairs={{16,0},{18,2},{20,4},{22,6},{24,8},{26,10},{28,12},{30,14},{0,16},... | collective-permute-start | bytes 147464 | tf_op jit(solution)/shard_map/ppermute | solution.py:36
  6.7 5.6 %collective-permute-start.2 = (bf16[1,24,1024]{2,1,0:T(8,128)(2,1)S(1)}, bf16[1,24,1024]{2,1,0:T(8,128)(2,1)S(1)}, u32[]{:S(2)}, u32[]{:S(2)}) collective-permute-start(bf16[1,24,1024]{2,1,0:T(8,128)(2,1)S(1)} %reshape.21.refs_0_), channel_id=1, source_target_pairs={{2,0},{0,2},{6,4},{4,6},{10,8},{8,10},{14,12},{12,14},{18,16},{16,... | collective-permute-start | bytes 147464 | tf_op jit(solution)/shard_map/ppermute | solution.py:36
  8.2 4.1 %collective-permute-start.4 = (bf16[1,24,1024]{2,1,0:T(8,128)(2,1)S(1)}, bf16[1,24,1024]{2,1,0:T(8,128)(2,1)S(1)}, u32[]{:S(2)}, u32[]{:S(2)}) collective-permute-start(bf16[1,24,1024]{2,1,0:T(8,128)(2,1)S(1)} %reshape.21.refs_0_), channel_id=1, source_target_pairs={{8,0},{10,2},{12,4},{14,6},{0,8},{2,10},{4,12},{6,14},{24,16},{26,... | collective-permute-start | bytes 147464 | tf_op jit(solution)/shard_map/ppermute | solution.py:36
  9.0 4.9 %collective-permute-start.6 = (bf16[1,24,1024]{2,1,0:T(8,128)(2,1)S(1)}, bf16[1,24,1024]{2,1,0:T(8,128)(2,1)S(1)}, u32[]{:S(2)}, u32[]{:S(2)}) collective-permute-start(bf16[1,24,1024]{2,1,0:T(8,128)(2,1)S(1)} %reshape.21.refs_0_), channel_id=1, source_target_pairs={{4,0},{6,2},{0,4},{2,6},{12,8},{14,10},{8,12},{10,14},{20,16},{22,... | collective-permute-start | bytes 147464 | tf_op jit(solution)/shard_map/ppermute | solution.py:36
  10.5 5.6 %collective-permute-start.8 = (bf16[1,24,1024]{2,1,0:T(8,128)(2,1)S(1)}, bf16[1,24,1024]{2,1,0:T(8,128)(2,1)S(1)}, u32[]{:S(2)}, u32[]{:S(2)}) collective-permute-start(bf16[1,24,1024]{2,1,0:T(8,128)(2,1)S(1)} %reshape.21.refs_0_), channel_id=1, source_target_pairs={{6,0},{4,2},{2,4},{0,6},{14,8},{12,10},{10,12},{8,14},{22,16},{20,... | collective-permute-start | bytes 147464 | tf_op jit(solution)/shard_map/ppermute | solution.py:36
  12.3 8.3 %collective-permute-start.5 = (bf16[3,24,1024]{2,1,0:T(8,128)(2,1)S(1)}, bf16[3,24,1024]{2,1,0:T(8,128)(2,1)S(1)}, u32[]{:S(2)}, u32[]{:S(2)}) collective-permute-start(bf16[3,24,1024]{2,1,0:T(8,128)(2,1)S(1)} %constant_dynamic-update-slice_fusion.refs_1_), channel_id=1, source_target_pairs={{4,0},{6,2},{0,4},{2,6},{12,8},{14,10},{8,12},{10,14},{20,16},{22,... | collective-permute-start | bytes 442376 | tf_op jit(solution)/shard_map/ppermute | solution.py:36
  13.9 6.7 %collective-permute-start.7 = (bf16[3,24,1024]{2,1,0:T(8,128)(2,1)S(1)}, bf16[3,24,1024]{2,1,0:T(8,128)(2,1)S(1)}, u32[]{:S(2)}, u32[]{:S(2)}) collective-permute-start(bf16[3,24,1024]{2,1,0:T(8,128)(2,1)S(1)} %constant_dynamic-update-slice_fusion.refs_1_), channel_id=1, source_target_pairs={{2,0},{0,2},{6,4},{4,6},{10,8},{8,10},{14,12},{12,14},{18,16},{16,... | collective-permute-start | bytes 442376 | tf_op jit(solution)/shard_map/ppermute | solution.py:36
  14.9 5.6 %collective-permute-start.3 = (bf16[2,24,1024]{2,1,0:T(8,128)(2,1)S(1)}, bf16[2,24,1024]{2,1,0:T(8,128)(2,1)S(1)}, u32[]{:S(2)}, u32[]{:S(2)}) collective-permute-start(bf16[2,24,1024]{2,1,0:T(8,128)(2,1)S(1)} %pad_maximum_fusion), channel_id=1, source_target_pairs={{6,0},{4,2},{2,4},{0,6},{14,8},{12,10},{10,12},{8,14},{22,16},{20,... | collective-permute-start | bytes 294920 | tf_op jit(solution)/shard_map/ppermute | solution.py:36
  16.1 4.1 %collective-permute-start.9 = (bf16[1,24,1024]{2,1,0:T(8,128)(2,1)S(1)}, bf16[1,24,1024]{2,1,0:T(8,128)(2,1)S(1)}, u32[]{:S(2)}, u32[]{:S(2)}) collective-permute-start(bf16[1,24,1024]{2,1,0:T(8,128)(2,1)S(1)} %collective-permute-done.8.refs_4_), channel_id=1, source_target_pairs={{8,0},{10,2},{12,4},{14,6},{0,8},{2,10},{4,12},{6,14},{24,16},{26,... | collective-permute-start | bytes 147464 | tf_op jit(solution)/shard_map/ppermute | solution.py:36
  21.3 1.4 %collective-permute-start.10 = (f32[2,16,8,128]{3,2,1,0:T(8,128)S(1)}, f32[2,16,8,128]{3,2,1,0:T(8,128)S(1)}, u32[]{:S(2)}, u32[]{:S(2)}) collective-permute-start(f32[2,16,8,128]{3,2,1,0:T(8,128)S(1)} %get-tuple-element.34.refs_0_), channel_id=1, source_target_pairs={{0,1},{1,0},{2,3},{3,2},{4,5},{5,4},{6,7},{7,6},{8,9},{9,8},{10,11... | collective-permute-start | bytes 393224 | tf_op jit(solution)/shard_map/ppermute | solution.py:426
  23.6 6.0 %collective-permute-start.13 = (bf16[4,8,1024]{2,1,0:T(8,128)(2,1)S(1)}, bf16[4,8,1024]{2,1,0:T(8,128)(2,1)S(1)}, u32[]{:S(2)}, u32[]{:S(2)}) collective-permute-start(bf16[4,8,1024]{2,1,0:T(8,128)(2,1)S(1)} %get-tuple-element.38), channel_id=1, source_target_pairs={{0,6},{2,4},{4,2},{6,0},{8,14},{10,12},{12,10},{14,8},{16,22},{18,... | collective-permute-start | bytes 196616 | tf_op jit(solution)/shard_map/ppermute | solution.py:41
  25.4 4.8 %collective-permute-start.12 = (bf16[4,8,1024]{2,1,0:T(8,128)(2,1)S(1)}, bf16[4,8,1024]{2,1,0:T(8,128)(2,1)S(1)}, u32[]{:S(2)}, u32[]{:S(2)}) collective-permute-start(bf16[4,8,1024]{2,1,0:T(8,128)(2,1)S(1)} %get-tuple-element.37), channel_id=1, source_target_pairs={{0,4},{2,6},{4,0},{6,2},{8,12},{10,14},{12,8},{14,10},{16,20},{18,... | collective-permute-start | bytes 196616 | tf_op jit(solution)/shard_map/ppermute | solution.py:41
  26.1 4.3 %collective-permute-start.11 = (bf16[4,8,1024]{2,1,0:T(8,128)(2,1)S(1)}, bf16[4,8,1024]{2,1,0:T(8,128)(2,1)S(1)}, u32[]{:S(2)}, u32[]{:S(2)}) collective-permute-start(bf16[4,8,1024]{2,1,0:T(8,128)(2,1)S(1)} %get-tuple-element.36), channel_id=1, source_target_pairs={{0,2},{2,0},{4,6},{6,4},{8,10},{10,8},{12,14},{14,12},{16,18},{18,... | collective-permute-start | bytes 196616 | tf_op jit(solution)/shard_map/ppermute | solution.py:41
  30.5 6.1 %collective-permute-start.16 = (bf16[1,8,1024]{2,1,0:T(8,128)(2,1)S(1)}, bf16[1,8,1024]{2,1,0:T(8,128)(2,1)S(1)}, u32[]{:S(2)}, u32[]{:S(2)}) collective-permute-start(bf16[1,8,1024]{2,1,0:T(8,128)(2,1)S(1)} %get-tuple-element.47), channel_id=1, source_target_pairs={{0,24},{2,26},{4,28},{6,30},{8,16},{10,18},{12,20},{14,22},{16,8},... | collective-permute-start | bytes 49160 | tf_op jit(solution)/shard_map/ppermute | solution.py:41
  34.2 4.6 %collective-permute-start.15 = (bf16[1,8,1024]{2,1,0:T(8,128)(2,1)S(1)}, bf16[1,8,1024]{2,1,0:T(8,128)(2,1)S(1)}, u32[]{:S(2)}, u32[]{:S(2)}) collective-permute-start(bf16[1,8,1024]{2,1,0:T(8,128)(2,1)S(1)} %get-tuple-element.48), channel_id=1, source_target_pairs={{0,16},{2,18},{4,20},{6,22},{8,24},{10,26},{12,28},{14,30},{16,0},... | collective-permute-start | bytes 49160 | tf_op jit(solution)/shard_map/ppermute | solution.py:41
  34.2 4.6 %collective-permute-start.14 = (bf16[1,8,1024]{2,1,0:T(8,128)(2,1)S(1)}, bf16[1,8,1024]{2,1,0:T(8,128)(2,1)S(1)}, u32[]{:S(2)}, u32[]{:S(2)}) collective-permute-start(bf16[1,8,1024]{2,1,0:T(8,128)(2,1)S(1)} %get-tuple-element.46), channel_id=1, source_target_pairs={{0,8},{2,10},{4,12},{6,14},{8,0},{10,2},{12,4},{14,6},{16,24},{18,... | collective-permute-start | bytes 49160 | tf_op jit(solution)/shard_map/ppermute | solution.py:41

commit v7 on v6

--- a/solution.py
+++ b/solution.py
@@ -31,14 +31,29 @@
     return index + (other - digit) * stride
 
 
-def fetch(value, axis, size, level, offset):
-    pairs = [(partner(i, *level, offset), i) for i in range(size)]
-    return lax.ppermute(value, axis, pairs)
-
-
-def deliver(value, axis, size, level, offset):
-    pairs = [(i, partner(i, *level, offset)) for i in range(size)]
-    return lax.ppermute(value, axis, pairs)
+def turned(offset, level, core):
+    stride, radix = level
+    if stride == 1 and radix == 4 and core % 2 and offset in (1, 2):
+        return 3 - offset
+    return offset
+
+
+def pairs_of(sizes, level, offset):
+    wide, narrow = sizes
+    return [
+        (i * narrow + c, partner(i, *level, turned(offset, level, c)) * narrow + c)
+        for i in range(wide)
+        for c in range(narrow)
+    ]
+
+
+def fetch(value, sizes, level, offset):
+    pairs = [(there, here) for here, there in pairs_of(sizes, level, offset)]
+    return lax.ppermute(value, ("wide", "narrow"), pairs)
+
+
+def deliver(value, sizes, level, offset):
+    return lax.ppermute(value, ("wide", "narrow"), pairs_of(sizes, level, offset))
 
 
 def after(value, earlier):
@@ -49,15 +64,26 @@
     return range(radix - 1, 0, -1)
 
 
-def gather_blocks(own, axis, size):
+def aligned(order, level):
+    inner = len(order) // level[1]
+    slots = {o: k + 1 for k, o in enumerate(offsets_of(level[1]))} | {0: 0}
+    places = [0] * len(order)
+    for offset, slot in slots.items():
+        other = slots[turned(offset, level, 1)]
+        for k in range(inner):
+            places[order[slot * inner + k]] = order[other * inner + k]
+    return places
+
+
+def gather_blocks(own, sizes):
     early, late, count = [(own, [0])], [], 1
     before = None
-    for level in levels_of(size):
+    for level in levels_of(sizes[0]):
         rest = early[1:] + late
         offsets = list(offsets_of(level[1]))
         slots = {o: count * (k + 1) for k, o in enumerate(offsets)}
         starts = offsets[::-1] if rest else offsets
-        mine = {o: fetch(own, axis, size, level, o) for o in starts}
+        mine = {o: fetch(own, sizes, level, o) for o in starts}
         late = [(mine[o], [slots[o]]) for o in starts]
         early = [(own, [0])]
         if rest:
@@ -67,11 +93,11 @@
             early, late = early + [held] + late, []
             for o, first in zip(offsets, starts[:1] * 2 + starts[1:]):
                 part, ids = far if o & (o - 1) else held
-                block = fetch(after(part, mine[first]), axis, size, level, o)
+                block = fetch(after(part, mine[first]), sizes, level, o)
                 late.append((block, [slots[o] + i for i in ids]))
             for o in offsets:
                 if o & (o - 1):
-                    block = fetch(mine[o], axis, size, step, 1)
+                    block = fetch(mine[o], sizes, step, 1)
                     late.append((block, [slots[o] + near]))
         before = level, slots[1]
         count *= level[1]
@@ -86,12 +112,12 @@
     return blocks, sum((ids for _, ids in pieces), [])
 
 
-def scatter_sum(groups, axis, size, beside):
-    for level in levels_of(size)[::-1]:
+def scatter_sum(groups, sizes, beside):
+    for level in levels_of(sizes[0])[::-1]:
         if len(groups) == 1:
             groups = jnp.split(after(groups[0], beside), level[1])
         came = [
-            deliver(group.astype(jnp.bfloat16), axis, size, level, o)
+            deliver(group.astype(jnp.bfloat16), sizes, level, o)
             for o, group in zip(offsets_of(level[1]), groups[1:])
         ]
         total = groups[0]
@@ -275,11 +301,20 @@
     ).astype(jnp.bfloat16)
 
 
-def middle_kernel(n_parts, groups, order, *refs):
+def middle_kernel(n_parts, groups, order, places, *refs):
     parts, (gate_w, up_w) = refs[:n_parts], refs[n_parts : n_parts + 2]
     factor_out, tact_out = refs[n_parts + 2 : n_parts + 4]
     own_out, others_out = refs[n_parts + 4], refs[n_parts + 5 :]
-    packed, dact = (sum(p[k] for p in parts[1:]) + parts[0][k] for k in range(2))
+    packed, dact = (
+        sum(
+            (
+                jnp.stack([p[k, at] for at in places]) if shift % 2 else p[k]
+                for shift, p in enumerate(parts)
+            ),
+            0.0,
+        )
+        for k in range(2)
+    )
     gate, up, tgate, tup = (over_slots(only_slot(packed, s)) for s in range(SLOTS))
     dgate, dup, tdgate, tdup, tact = factors(gate, up, tgate, tup, dact)
     blocks, _, hidden = gate.shape
@@ -304,13 +339,13 @@
         out[place_in] = hvp[at].astype(out.dtype)
 
 
-def middle(parts, gate_w, up_w, groups, order):
+def middle(parts, gate_w, up_w, groups, order, places):
     _, blocks, _, hidden = parts[0].shape
     lanes = gate_w.shape[0] // SLOTS
     vmem = pl.BlockSpec(memory_space=pltpu.VMEM)
     group = (blocks // groups, 8, lanes)
     return pl.pallas_call(
-        functools.partial(middle_kernel, len(parts), groups, order),
+        functools.partial(middle_kernel, len(parts), groups, order, places),
         out_shape=(
             jax.ShapeDtypeStruct((blocks * 16, SLOTS * 2 * hidden), jnp.bfloat16),
             jax.ShapeDtypeStruct((blocks * 8, SLOTS * hidden), jnp.bfloat16),
@@ -415,7 +450,7 @@
     def local(primal_in, tangent_in, cotangent, gate_weight, up_weight, down_weight):
         weights = (gate_weight, up_weight, down_weight)
         early, late, order = gather_blocks(
-            fold(primal_in, tangent_in, cotangent), "wide", wide
+            fold(primal_in, tangent_in, cotangent), (wide, narrow)
         )
         *first, gate_weight, up_weight, down_weight = begin(early, weights)
         weights = (gate_weight, up_weight, down_weight)
@@ -424,10 +459,13 @@
         for shift in range(1, narrow):
             pairs = [(i, (i + shift) % narrow) for i in range(narrow)]
             parts.append(lax.ppermute(part, "narrow", pairs))
-        groups = levels_of(wide)[-1][1]
-        factor, tact, *hvp = middle(parts, gate_weight, up_weight, groups, order)
+        finest = levels_of(wide)[-1]
+        groups, places = finest[1], aligned(order, finest)
+        factor, tact, *hvp = middle(
+            parts, gate_weight, up_weight, groups, order, places
+        )
         gate_grad, up_grad = up_grads(pt, factor)
-        total = scatter_sum(hvp, "wide", wide, gate_grad)
+        total = scatter_sum(hvp, (wide, narrow), gate_grad)
         input_hvp = unfold(total[0].astype(jnp.bfloat16))
         return (input_hvp, gate_grad, up_grad, down_grad(cot, tact))
 

time: 39.8 us -> 39.3 us (0.987)
  waiting for transfers between devices: 5.48 us -> 4.98 us
    ppermute x16, waiting for transfers between devices: 4.14 us -> 3.64 us  [the longest x6 2.55 us: deliver(): lax.ppermute(value, ('wide', 'narrow'), pairs_of(sizes, level, offset))]
  transfers between devices with their start and end apart: 17 -> 17, of which waited for: 7 -> 6; matrix products, arithmetic and copies ran while one was open for 0% -> 0% of each run, Pallas kernels for 17% -> 17%
where the time goes in v7:
time: 39.3 us; the launch traced here: 39 us
  starting transfers between devices  23.2 us (59%)
  Pallas kernels  8.43 us (21%)
  waiting for transfers between devices  4.98 us (13%)
  other arithmetic  0.89 us (2%)
  between operations  0.78 us (2%)
  local copies, waits for them, and re-layouts  0.73 us (2%)
    ppermute x10, starting transfers between devices, fetch(): return lax.ppermute(value, ('wide', 'narrow'), pairs)  15.1 us
    ppermute x6, starting transfers between devices, deliver(): lax.ppermute(value, ('wide', 'narrow'), pairs_of(sizes, level, offset))  8.01 us
    pallas_call x1, Pallas kernels, begin(): pl.pallas_call(functools.partial(begin_kernel, len(pieces)), out_shape=(j...  2.7 us
    ppermute x6, waiting for transfers between devices, deliver(): lax.ppermute(value, ('wide', 'narrow'), pairs_of(sizes, level, offset))  2.55 us
    pallas_call x1, Pallas kernels, up_grads(): pl.pallas_call(up_grads_kernel, out_shape=(out, out), in_specs=[vmem] * 2...  2.41 us
    pallas_call x1, Pallas kernels, down_grad(): pl.pallas_call(down_grad_kernel, out_shape=jax.ShapeDtypeStruct((hidden,...  1.64 us
    ppermute x1, waiting for transfers between devices, local(): parts.append(lax.ppermute(part, 'narrow', pairs))  1.33 us
    ppermute x10, waiting for transfers between devices, fetch(): return lax.ppermute(value, ('wide', 'narrow'), pairs)  1.1 us
  transfers between devices with their start and end apart: 17, of which 6 were waited for; matrix products, arithmetic and copies ran while one was open for 0% of the time, Pallas kernels for 17%

profile of v7, /device:TPU:0, one launch (start us, length us, event | category | flops | bytes accessed | tf_op | source)
XLA Modules:
  0.0 39.0 jit_solution(4184131116289718138)
XLA Ops:
  0.6 0.8 %pad_maximum_fusion.1 = bf16[3,2,4096]{2,1,0:T(2,128)(2,1)S(1)} fusion(bf16[1,2,4096]{2,1,0:T(2,128)(2,1)} %bitcast.17, bf16[1,2,4096]{2,1,0:T(2,128)(2,1)} %bitcast.18, bf16[1,2,4096]{2,1,0:T(2,128)(2,1)} %bitcast.19), kind=kLoop, calls=%fused_computation.2 | loop fusion | flops 49152 | bytes 98304 | tf_op jit(solution)/shard_map/stack | solution.py:131
  1.6 5.1 %collective-permute-start = (bf16[1,24,1024]{2,1,0:T(8,128)(2,1)S(1)}, bf16[1,24,1024]{2,1,0:T(8,128)(2,1)S(1)}, u32[]{:S(2)}, u32[]{:S(2)}) collective-permute-start(bf16[1,24,1024]{2,1,0:T(8,128)(2,1)S(1)} %reshape.21.refs_0_), channel_id=1, source_target_pairs={{24,0},{25,1},{26,2},{27,3},{28,4},{29,5},{30,6},{31,7},{16,8},{17... | collective-permute-start | bytes 147464 | tf_op jit(solution)/shard_map/ppermute | solution.py:52
  6.7 0.0 collective-permute-start.1
  6.7 1.5 %collective-permute-start.2 = (bf16[1,24,1024]{2,1,0:T(8,128)(2,1)S(1)}, bf16[1,24,1024]{2,1,0:T(8,128)(2,1)S(1)}, u32[]{:S(2)}, u32[]{:S(2)}) collective-permute-start(bf16[1,24,1024]{2,1,0:T(8,128)(2,1)S(1)} %reshape.21.refs_0_), channel_id=1, source_target_pairs={{2,0},{5,1},{0,2},{7,3},{6,4},{1,5},{4,6},{3,7},{10,8},{13,9},{8,1... | collective-permute-start | bytes 147464 | tf_op jit(solution)/shard_map/ppermute | solution.py:52
  8.2 0.8 %collective-permute-start.4 = (bf16[1,24,1024]{2,1,0:T(8,128)(2,1)S(1)}, bf16[1,24,1024]{2,1,0:T(8,128)(2,1)S(1)}, u32[]{:S(2)}, u32[]{:S(2)}) collective-permute-start(bf16[1,24,1024]{2,1,0:T(8,128)(2,1)S(1)} %reshape.21.refs_0_), channel_id=1, source_target_pairs={{8,0},{9,1},{10,2},{11,3},{12,4},{13,5},{14,6},{15,7},{0,8},{1,9},... | collective-permute-start | bytes 147464 | tf_op jit(solution)/shard_map/ppermute | solution.py:52
  9.0 1.5 %collective-permute-start.6 = (bf16[1,24,1024]{2,1,0:T(8,128)(2,1)S(1)}, bf16[1,24,1024]{2,1,0:T(8,128)(2,1)S(1)}, u32[]{:S(2)}, u32[]{:S(2)}) collective-permute-start(bf16[1,24,1024]{2,1,0:T(8,128)(2,1)S(1)} %reshape.21.refs_0_), channel_id=1, source_target_pairs={{4,0},{3,1},{6,2},{1,3},{0,4},{7,5},{2,6},{5,7},{12,8},{11,9},{14,... | collective-permute-start | bytes 147464 | tf_op jit(solution)/shard_map/ppermute | solution.py:52
  10.5 0.0 collective-permute-done
  10.5 1.2 %collective-permute-start.8 = (bf16[1,24,1024]{2,1,0:T(8,128)(2,1)S(1)}, bf16[1,24,1024]{2,1,0:T(8,128)(2,1)S(1)}, u32[]{:S(2)}, u32[]{:S(2)}) collective-permute-start(bf16[1,24,1024]{2,1,0:T(8,128)(2,1)S(1)} %reshape.21.refs_0_), channel_id=1, source_target_pairs={{6,0},{7,1},{4,2},{5,3},{2,4},{3,5},{0,6},{1,7},{14,8},{15,9},{12,... | collective-permute-start | bytes 147464 | tf_op jit(solution)/shard_map/ppermute | solution.py:52
  11.7 0.0 collective-permute-done.1
  11.7 0.6 %collective-permute-done.4 = bf16[1,24,1024]{2,1,0:T(8,128)(2,1)S(1)} collective-permute-done((bf16[1,24,1024]{2,1,0:T(8,128)(2,1)S(1)}, bf16[1,24,1024]{2,1,0:T(8,128)(2,1)S(1)}, u32[]{:S(2)}, u32[]{:S(2)}) %collective-permute-start.4) | collective-permute-done | bytes 49184 | tf_op jit(solution)/shard_map/ppermute | solution.py:52
  12.3 0.0 collective-permute-done.2.refs_2_
  12.3 1.6 %collective-permute-start.5 = (bf16[3,24,1024]{2,1,0:T(8,128)(2,1)S(1)}, bf16[3,24,1024]{2,1,0:T(8,128)(2,1)S(1)}, u32[]{:S(2)}, u32[]{:S(2)}) collective-permute-start(bf16[3,24,1024]{2,1,0:T(8,128)(2,1)S(1)} %constant_dynamic-update-slice_fusion.refs_1_), channel_id=1, source_target_pairs={{4,0},{3,1},{6,2},{1,3},{0,4},{7,5},{2,6},{5,7},{12,8},{11,9},{14,... | collective-permute-start | bytes 442376 | tf_op jit(solution)/shard_map/ppermute | solution.py:52
  13.9 0.0 collective-permute-done.6.refs_3_
  13.9 1.1 %collective-permute-start.7 = (bf16[3,24,1024]{2,1,0:T(8,128)(2,1)S(1)}, bf16[3,24,1024]{2,1,0:T(8,128)(2,1)S(1)}, u32[]{:S(2)}, u32[]{:S(2)}) collective-permute-start(bf16[3,24,1024]{2,1,0:T(8,128)(2,1)S(1)} %constant_dynamic-update-slice_fusion.refs_1_), channel_id=1, source_target_pairs={{2,0},{5,1},{0,2},{7,3},{6,4},{1,5},{4,6},{3,7},{10,8},{13,9},{8,1... | collective-permute-start | bytes 442376 | tf_op jit(solution)/shard_map/ppermute | solution.py:52
  14.9 1.2 %collective-permute-start.3 = (bf16[2,24,1024]{2,1,0:T(8,128)(2,1)S(1)}, bf16[2,24,1024]{2,1,0:T(8,128)(2,1)S(1)}, u32[]{:S(2)}, u32[]{:S(2)}) collective-permute-start(bf16[2,24,1024]{2,1,0:T(8,128)(2,1)S(1)} %pad_maximum_fusion), channel_id=1, source_target_pairs={{6,0},{7,1},{4,2},{5,3},{2,4},{3,5},{0,6},{1,7},{14,8},{15,9},{12,... | collective-permute-start | bytes 294920 | tf_op jit(solution)/shard_map/ppermute | solution.py:52
  16.1 0.0 collective-permute-done.8.refs_4_
  16.1 1.2 %collective-permute-start.9 = (bf16[1,24,1024]{2,1,0:T(8,128)(2,1)S(1)}, bf16[1,24,1024]{2,1,0:T(8,128)(2,1)S(1)}, u32[]{:S(2)}, u32[]{:S(2)}) collective-permute-start(bf16[1,24,1024]{2,1,0:T(8,128)(2,1)S(1)} %collective-permute-done.8.refs_4_), channel_id=1, source_target_pairs={{8,0},{9,1},{10,2},{11,3},{12,4},{13,5},{14,6},{15,7},{0,8},{1,9},... | collective-permute-start | bytes 147464 | tf_op jit(solution)/shard_map/ppermute | solution.py:52
  17.4 2.7 %shard_map.93 = (bf16[112,1024]{1,0:T(8,128)(2,1)S(1)}, bf16[56,1024]{1,0:T(8,128)(2,1)S(1)}, f32[2,7,8,128]{3,2,1,0:T(8,128)S(1)}, bf16[4096,128]{1,0:T(8,128)(...) custom-call(bf16[1,24,1024]{2,1,0:T(8,128)(2,1)S(1)} %reshape.21.refs_0_, ...), custom_call_target="tpu_custom_call" | custom-call | flops 293601280 | bytes 6291456 | tf_op jit(solution)/shard_map/pallas_call | solution.py:234
  20.1 0.1 collective-permute-done.9.refs_3_
  20.2 0.3 collective-permute-done.3.refs_0_
  20.6 0.0 collective-permute-done.5.refs_1_
  20.6 0.0 collective-permute-done.7.refs_2_
  20.6 0.8 %shard_map.94 = (bf16[256,1024]{1,0:T(8,128)(2,1)S(1)}, bf16[128,1024]{1,0:T(8,128)(2,1)S(1)}, f32[2,16,8,128]{3,2,1,0:T(8,128)S(1)}) custom-call(bf16[2,24,1024]{2,1,0:T(8,128)(2,1)S(1)} %collective-permute-done.3.refs_0_, bf16[3,24,1024]{2,1,0:T(8,128)(2,1)S(1)} %collective-permute-done.5.refs_1_, bf16[3,24,1024]{2,1,0:T(8,128)(2,1)S(1)} %collective-permute-done.7.refs_2_, ...), custom_call_target="tpu_custom_call" | custom-call | tf_op jit(solution)/shard_map/pallas_call | solution.py:271
  21.4 0.1 collective-permute-start.10
  21.4 1.3 %collective-permute-done.10.refs_1_ = f32[2,16,8,128]{3,2,1,0:T(8,128)S(1)} collective-permute-done((f32[2,16,8,128]{3,2,1,0:T(8,128)S(1)}, f32[2,16,8,128]{3,2,1,0:T(8,128)S(1)}, u32[]{:S(2)}, u32[]{:S(2)}) %collective-permute-start.10) | collective-permute-done | bytes 131104 | tf_op jit(solution)/shard_map/ppermute | solution.py:461
  22.8 0.9 %shard_map.95 = (bf16[256,1024]{1,0:T(8,128)(2,1)S(1)}, bf16[128,512]{1,0:T(8,128)(2,1)S(1)}, f32[4,8,1024]{2,1,0:T(8,128)S(1)}, bf16[4,8,1024]{2,1,0:T(8,128)(2...) custom-call(f32[2,16,8,128]{3,2,1,0:T(8,128)S(1)} %get-tuple-element.34.refs_0_, ...), custom_call_target="tpu_custom_call" | custom-call | tf_op jit(solution)/shard_map/pallas_call | solution.py:347
  23.7 1.6 %collective-permute-start.13 = (bf16[4,8,1024]{2,1,0:T(8,128)(2,1)S(1)}, bf16[4,8,1024]{2,1,0:T(8,128)(2,1)S(1)}, u32[]{:S(2)}, u32[]{:S(2)}) collective-permute-start(bf16[4,8,1024]{2,1,0:T(8,128)(2,1)S(1)} %get-tuple-element.38), channel_id=1, source_target_pairs={{0,6},{1,7},{2,4},{3,5},{4,2},{5,3},{6,0},{7,1},{8,14},{9,15},{10,... | collective-permute-start | bytes 196616 | tf_op jit(solution)/shard_map/ppermute | solution.py:56
  25.2 0.9 %collective-permute-start.12 = (bf16[4,8,1024]{2,1,0:T(8,128)(2,1)S(1)}, bf16[4,8,1024]{2,1,0:T(8,128)(2,1)S(1)}, u32[]{:S(2)}, u32[]{:S(2)}) collective-permute-start(bf16[4,8,1024]{2,1,0:T(8,128)(2,1)S(1)} %get-tuple-element.37), channel_id=1, source_target_pairs={{0,4},{1,3},{2,6},{3,1},{4,0},{5,7},{6,2},{7,5},{8,12},{9,11},{10,... | collective-permute-start | bytes 196616 | tf_op jit(solution)/shard_map/ppermute | solution.py:56
  26.1 1.1 %collective-permute-start.11 = (bf16[4,8,1024]{2,1,0:T(8,128)(2,1)S(1)}, bf16[4,8,1024]{2,1,0:T(8,128)(2,1)S(1)}, u32[]{:S(2)}, u32[]{:S(2)}) collective-permute-start(bf16[4,8,1024]{2,1,0:T(8,128)(2,1)S(1)} %get-tuple-element.36), channel_id=1, source_target_pairs={{0,2},{1,5},{2,0},{3,7},{4,6},{5,1},{6,4},{7,3},{8,10},{9,13},{10,... | collective-permute-start | bytes 196616 | tf_op jit(solution)/shard_map/ppermute | solution.py:56
  27.2 2.4 %shard_map.96 = (f32[4096,128]{1,0:T(8,128)}, f32[4096,128]{1,0:T(8,128)}) custom-call(bf16[256,1024]{1,0:T(8,128)(2,1)S(1)} %get-tuple-element.39.pt, bf16[256,1024]{1,0:T(8,128)(2,1)S(1)} %get-tuple-element.40.factor), custom_call_target="tpu_custom_call" | custom-call | flops 536870912 | bytes 4194304 | tf_op jit(solution)/shard_map/pallas_call | solution.py:389
  29.6 0.0 collective-permute-done.13
  29.7 0.7 %collective-permute-done.12 = bf16[4,8,1024]{2,1,0:T(8,128)(2,1)S(1)} collective-permute-done((bf16[4,8,1024]{2,1,0:T(8,128)(2,1)S(1)}, bf16[4,8,1024]{2,1,0:T(8,128)(2,1)S(1)}, u32[]{:S(2)}, u32[]{:S(2)}) %collective-permute-start.12) | collective-permute-done | bytes 65568 | tf_op jit(solution)/shard_map/ppermute | solution.py:56
  30.4 0.0 collective-permute-done.11
  30.5 3.3 %collective-permute-start.16 = (bf16[1,8,1024]{2,1,0:T(8,128)(2,1)S(1)}, bf16[1,8,1024]{2,1,0:T(8,128)(2,1)S(1)}, u32[]{:S(2)}, u32[]{:S(2)}) collective-permute-start(bf16[1,8,1024]{2,1,0:T(8,128)(2,1)S(1)} %get-tuple-element.47), channel_id=1, source_target_pairs={{0,24},{1,25},{2,26},{3,27},{4,28},{5,29},{6,30},{7,31},{8,16},{9,... | collective-permute-start | bytes 49160 | tf_op jit(solution)/shard_map/ppermute | solution.py:56
  33.7 0.0 collective-permute-start.15
  33.7 1.2 %collective-permute-start.14 = (bf16[1,8,1024]{2,1,0:T(8,128)(2,1)S(1)}, bf16[1,8,1024]{2,1,0:T(8,128)(2,1)S(1)}, u32[]{:S(2)}, u32[]{:S(2)}) collective-permute-start(bf16[1,8,1024]{2,1,0:T(8,128)(2,1)S(1)} %get-tuple-element.46), channel_id=1, source_target_pairs={{0,8},{1,9},{2,10},{3,11},{4,12},{5,13},{6,14},{7,15},{8,0},{9,1},... | collective-permute-start | bytes 49160 | tf_op jit(solution)/shard_map/ppermute | solution.py:56
  34.9 1.6 %shard_map.97 = f32[128,4096]{1,0:T(8,128)} custom-call(bf16[128,1024]{1,0:T(8,128)(2,1)S(1)} %get-tuple-element.44.cot, bf16[128,512]{1,0:T(8,128)(2,1)S(1)} %get-tuple-element.45.tact), custom_call_target="tpu_custom_call" | custom-call | flops 134217728 | bytes 2097152 | tf_op jit(solution)/shard_map/pallas_call | solution.py:429
  36.6 0.0 collective-permute-done.16
  36.6 1.8 %collective-permute-done.15 = bf16[1,8,1024]{2,1,0:T(8,128)(2,1)S(1)} collective-permute-done((bf16[1,8,1024]{2,1,0:T(8,128)(2,1)S(1)}, bf16[1,8,1024]{2,1,0:T(8,128)(2,1)S(1)}, u32[]{:S(2)}, u32[]{:S(2)}) %collective-permute-start.15) | collective-permute-done | bytes 16416 | tf_op jit(solution)/shard_map/ppermute | solution.py:56
  38.4 0.0 collective-permute-done.14
  38.4 0.6 %reshape.22 = bf16[2,4096]{1,0:T(2,128)(2,1)} reshape(bf16[2,8,4,128]{3,2,1,0:T(4,128)(2,1)S(1)} %copy.11) | data formatting | bytes 32768 | tf_op jit(solution)/shard_map/reshape | solution.py:140
  (13 shorter events, 0.2 us)
Async XLA Ops:
  1.6 8.9 %collective-permute-start = (bf16[1,24,1024]{2,1,0:T(8,128)(2,1)S(1)}, bf16[1,24,1024]{2,1,0:T(8,128)(2,1)S(1)}, u32[]{:S(2)}, u32[]{:S(2)}) collective-permute-start(bf16[1,24,1024]{2,1,0:T(8,128)(2,1)S(1)} %reshape.21.refs_0_), channel_id=1, source_target_pairs={{24,0},{25,1},{26,2},{27,3},{28,4},{29,5},{30,6},{31,7},{16,8},{17... | collective-permute-start | bytes 147464 | tf_op jit(solution)/shard_map/ppermute | solution.py:52
  6.7 5.0 %collective-permute-start.1 = (bf16[1,24,1024]{2,1,0:T(8,128)(2,1)S(1)}, bf16[1,24,1024]{2,1,0:T(8,128)(2,1)S(1)}, u32[]{:S(2)}, u32[]{:S(2)}) collective-permute-start(bf16[1,24,1024]{2,1,0:T(8,128)(2,1)S(1)} %reshape.21.refs_0_), channel_id=1, source_target_pairs={{16,0},{17,1},{18,2},{19,3},{20,4},{21,5},{22,6},{23,7},{24,8},{25... | collective-permute-start | bytes 147464 | tf_op jit(solution)/shard_map/ppermute | solution.py:52
  6.7 5.6 %collective-permute-start.2 = (bf16[1,24,1024]{2,1,0:T(8,128)(2,1)S(1)}, bf16[1,24,1024]{2,1,0:T(8,128)(2,1)S(1)}, u32[]{:S(2)}, u32[]{:S(2)}) collective-permute-start(bf16[1,24,1024]{2,1,0:T(8,128)(2,1)S(1)} %reshape.21.refs_0_), channel_id=1, source_target_pairs={{2,0},{5,1},{0,2},{7,3},{6,4},{1,5},{4,6},{3,7},{10,8},{13,9},{8,1... | collective-permute-start | bytes 147464 | tf_op jit(solution)/shard_map/ppermute | solution.py:52
  8.2 4.1 %collective-permute-start.4 = (bf16[1,24,1024]{2,1,0:T(8,128)(2,1)S(1)}, bf16[1,24,1024]{2,1,0:T(8,128)(2,1)S(1)}, u32[]{:S(2)}, u32[]{:S(2)}) collective-permute-start(bf16[1,24,1024]{2,1,0:T(8,128)(2,1)S(1)} %reshape.21.refs_0_), channel_id=1, source_target_pairs={{8,0},{9,1},{10,2},{11,3},{12,4},{13,5},{14,6},{15,7},{0,8},{1,9},... | collective-permute-start | bytes 147464 | tf_op jit(solution)/shard_map/ppermute | solution.py:52
  9.0 4.9 %collective-permute-start.6 = (bf16[1,24,1024]{2,1,0:T(8,128)(2,1)S(1)}, bf16[1,24,1024]{2,1,0:T(8,128)(2,1)S(1)}, u32[]{:S(2)}, u32[]{:S(2)}) collective-permute-start(bf16[1,24,1024]{2,1,0:T(8,128)(2,1)S(1)} %reshape.21.refs_0_), channel_id=1, source_target_pairs={{4,0},{3,1},{6,2},{1,3},{0,4},{7,5},{2,6},{5,7},{12,8},{11,9},{14,... | collective-permute-start | bytes 147464 | tf_op jit(solution)/shard_map/ppermute | solution.py:52
  10.5 5.6 %collective-permute-start.8 = (bf16[1,24,1024]{2,1,0:T(8,128)(2,1)S(1)}, bf16[1,24,1024]{2,1,0:T(8,128)(2,1)S(1)}, u32[]{:S(2)}, u32[]{:S(2)}) collective-permute-start(bf16[1,24,1024]{2,1,0:T(8,128)(2,1)S(1)} %reshape.21.refs_0_), channel_id=1, source_target_pairs={{6,0},{7,1},{4,2},{5,3},{2,4},{3,5},{0,6},{1,7},{14,8},{15,9},{12,... | collective-permute-start | bytes 147464 | tf_op jit(solution)/shard_map/ppermute | solution.py:52
  12.3 8.3 %collective-permute-start.5 = (bf16[3,24,1024]{2,1,0:T(8,128)(2,1)S(1)}, bf16[3,24,1024]{2,1,0:T(8,128)(2,1)S(1)}, u32[]{:S(2)}, u32[]{:S(2)}) collective-permute-start(bf16[3,24,1024]{2,1,0:T(8,128)(2,1)S(1)} %constant_dynamic-update-slice_fusion.refs_1_), channel_id=1, source_target_pairs={{4,0},{3,1},{6,2},{1,3},{0,4},{7,5},{2,6},{5,7},{12,8},{11,9},{14,... | collective-permute-start | bytes 442376 | tf_op jit(solution)/shard_map/ppermute | solution.py:52
  13.9 6.7 %collective-permute-start.7 = (bf16[3,24,1024]{2,1,0:T(8,128)(2,1)S(1)}, bf16[3,24,1024]{2,1,0:T(8,128)(2,1)S(1)}, u32[]{:S(2)}, u32[]{:S(2)}) collective-permute-start(bf16[3,24,1024]{2,1,0:T(8,128)(2,1)S(1)} %constant_dynamic-update-slice_fusion.refs_1_), channel_id=1, source_target_pairs={{2,0},{5,1},{0,2},{7,3},{6,4},{1,5},{4,6},{3,7},{10,8},{13,9},{8,1... | collective-permute-start | bytes 442376 | tf_op jit(solution)/shard_map/ppermute | solution.py:52
  14.9 5.6 %collective-permute-start.3 = (bf16[2,24,1024]{2,1,0:T(8,128)(2,1)S(1)}, bf16[2,24,1024]{2,1,0:T(8,128)(2,1)S(1)}, u32[]{:S(2)}, u32[]{:S(2)}) collective-permute-start(bf16[2,24,1024]{2,1,0:T(8,128)(2,1)S(1)} %pad_maximum_fusion), channel_id=1, source_target_pairs={{6,0},{7,1},{4,2},{5,3},{2,4},{3,5},{0,6},{1,7},{14,8},{15,9},{12,... | collective-permute-start | bytes 294920 | tf_op jit(solution)/shard_map/ppermute | solution.py:52
  16.1 4.1 %collective-permute-start.9 = (bf16[1,24,1024]{2,1,0:T(8,128)(2,1)S(1)}, bf16[1,24,1024]{2,1,0:T(8,128)(2,1)S(1)}, u32[]{:S(2)}, u32[]{:S(2)}) collective-permute-start(bf16[1,24,1024]{2,1,0:T(8,128)(2,1)S(1)} %collective-permute-done.8.refs_4_), channel_id=1, source_target_pairs={{8,0},{9,1},{10,2},{11,3},{12,4},{13,5},{14,6},{15,7},{0,8},{1,9},... | collective-permute-start | bytes 147464 | tf_op jit(solution)/shard_map/ppermute | solution.py:52
  21.4 1.4 %collective-permute-start.10 = (f32[2,16,8,128]{3,2,1,0:T(8,128)S(1)}, f32[2,16,8,128]{3,2,1,0:T(8,128)S(1)}, u32[]{:S(2)}, u32[]{:S(2)}) collective-permute-start(f32[2,16,8,128]{3,2,1,0:T(8,128)S(1)} %get-tuple-element.34.refs_0_), channel_id=1, source_target_pairs={{0,1},{1,0},{2,3},{3,2},{4,5},{5,4},{6,7},{7,6},{8,9},{9,8},{10,11... | collective-permute-start | bytes 393224 | tf_op jit(solution)/shard_map/ppermute | solution.py:461
  23.7 6.0 %collective-permute-start.13 = (bf16[4,8,1024]{2,1,0:T(8,128)(2,1)S(1)}, bf16[4,8,1024]{2,1,0:T(8,128)(2,1)S(1)}, u32[]{:S(2)}, u32[]{:S(2)}) collective-permute-start(bf16[4,8,1024]{2,1,0:T(8,128)(2,1)S(1)} %get-tuple-element.38), channel_id=1, source_target_pairs={{0,6},{1,7},{2,4},{3,5},{4,2},{5,3},{6,0},{7,1},{8,14},{9,15},{10,... | collective-permute-start | bytes 196616 | tf_op jit(solution)/shard_map/ppermute | solution.py:56
  25.2 5.2 %collective-permute-start.12 = (bf16[4,8,1024]{2,1,0:T(8,128)(2,1)S(1)}, bf16[4,8,1024]{2,1,0:T(8,128)(2,1)S(1)}, u32[]{:S(2)}, u32[]{:S(2)}) collective-permute-start(bf16[4,8,1024]{2,1,0:T(8,128)(2,1)S(1)} %get-tuple-element.37), channel_id=1, source_target_pairs={{0,4},{1,3},{2,6},{3,1},{4,0},{5,7},{6,2},{7,5},{8,12},{9,11},{10,... | collective-permute-start | bytes 196616 | tf_op jit(solution)/shard_map/ppermute | solution.py:56
  26.1 4.3 %collective-permute-start.11 = (bf16[4,8,1024]{2,1,0:T(8,128)(2,1)S(1)}, bf16[4,8,1024]{2,1,0:T(8,128)(2,1)S(1)}, u32[]{:S(2)}, u32[]{:S(2)}) collective-permute-start(bf16[4,8,1024]{2,1,0:T(8,128)(2,1)S(1)} %get-tuple-element.36), channel_id=1, source_target_pairs={{0,2},{1,5},{2,0},{3,7},{4,6},{5,1},{6,4},{7,3},{8,10},{9,13},{10,... | collective-permute-start | bytes 196616 | tf_op jit(solution)/shard_map/ppermute | solution.py:56
  30.5 6.1 %collective-permute-start.16 = (bf16[1,8,1024]{2,1,0:T(8,128)(2,1)S(1)}, bf16[1,8,1024]{2,1,0:T(8,128)(2,1)S(1)}, u32[]{:S(2)}, u32[]{:S(2)}) collective-permute-start(bf16[1,8,1024]{2,1,0:T(8,128)(2,1)S(1)} %get-tuple-element.47), channel_id=1, source_target_pairs={{0,24},{1,25},{2,26},{3,27},{4,28},{5,29},{6,30},{7,31},{8,16},{9,... | collective-permute-start | bytes 49160 | tf_op jit(solution)/shard_map/ppermute | solution.py:56
  33.7 4.6 %collective-permute-start.15 = (bf16[1,8,1024]{2,1,0:T(8,128)(2,1)S(1)}, bf16[1,8,1024]{2,1,0:T(8,128)(2,1)S(1)}, u32[]{:S(2)}, u32[]{:S(2)}) collective-permute-start(bf16[1,8,1024]{2,1,0:T(8,128)(2,1)S(1)} %get-tuple-element.48), channel_id=1, source_target_pairs={{0,16},{1,17},{2,18},{3,19},{4,20},{5,21},{6,22},{7,23},{8,24},{9,... | collective-permute-start | bytes 49160 | tf_op jit(solution)/shard_map/ppermute | solution.py:56
  33.7 4.6 %collective-permute-start.14 = (bf16[1,8,1024]{2,1,0:T(8,128)(2,1)S(1)}, bf16[1,8,1024]{2,1,0:T(8,128)(2,1)S(1)}, u32[]{:S(2)}, u32[]{:S(2)}) collective-permute-start(bf16[1,8,1024]{2,1,0:T(8,128)(2,1)S(1)} %get-tuple-element.46), channel_id=1, source_target_pairs={{0,8},{1,9},{2,10},{3,11},{4,12},{5,13},{6,14},{7,15},{8,0},{9,1},... | collective-permute-start | bytes 49160 | tf_op jit(solution)/shard_map/ppermute | solution.py:56

commit v8 on v7

--- a/solution.py
+++ b/solution.py
@@ -91,14 +91,16 @@
             step, near = before
             far = join([piece for piece in rest if piece[1] != [near]])
             early, late = early + [held] + late, []
+            came = []
             for o, first in zip(offsets, starts[:1] * 2 + starts[1:]):
                 part, ids = far if o & (o - 1) else held
                 block = fetch(after(part, mine[first]), sizes, level, o)
-                late.append((block, [slots[o] + i for i in ids]))
+                came.append((block, [slots[o] + i for i in ids]))
             for o in offsets:
                 if o & (o - 1):
                     block = fetch(mine[o], sizes, step, 1)
-                    late.append((block, [slots[o] + near]))
+                    came.append((block, [slots[o] + near]))
+            late += [came[k] for k in (1, 2, 0, 3) if k < len(came)]
         before = level, slots[1]
         count *= level[1]
     pieces = early + late

time: 39.3 us -> 39.4 us (level)
    ppermute x10, waiting for transfers between devices: 1.1 us -> 0.68 us  [fetch(): return lax.ppermute(value, ('wide', 'narrow'), pairs)]
where the time goes in v8:
time: 39.4 us; the launch traced here: 39.1 us
  starting transfers between devices  23.5 us (60%)
  Pallas kernels  8.45 us (21%)
  waiting for transfers between devices  4.72 us (12%)
  other arithmetic  0.89 us (2%)
  between operations  0.8 us (2%)
  local copies, waits for them, and re-layouts  0.73 us (2%)
    ppermute x10, starting transfers between devices, fetch(): return lax.ppermute(value, ('wide', 'narrow'), pairs)  15.4 us
    ppermute x6, starting transfers between devices, deliver(): lax.ppermute(value, ('wide', 'narrow'), pairs_of(sizes, level, offset))  8.01 us
    ppermute x6, waiting for transfers between devices, deliver(): lax.ppermute(value, ('wide', 'narrow'), pairs_of(sizes, level, offset))  2.7 us
    pallas_call x1, Pallas kernels, begin(): pl.pallas_call(functools.partial(begin_kernel, len(pieces)), out_shape=(j...  2.7 us
    pallas_call x1, Pallas kernels, up_grads(): pl.pallas_call(up_grads_kernel, out_shape=(out, out), in_specs=[vmem] * 2...  2.41 us
    pallas_call x1, Pallas kernels, down_grad(): pl.pallas_call(down_grad_kernel, out_shape=jax.ShapeDtypeStruct((hidden,...  1.64 us
    ppermute x1, waiting for transfers between devices, local(): parts.append(lax.ppermute(part, 'narrow', pairs))  1.33 us
    pallas_call x1, Pallas kernels, middle(): pl.pallas_call(functools.partial(middle_kernel, len(parts), groups, order...  0.88 us
  transfers between devices with their start and end apart: 17, of which 6 were waited for; matrix products, arithmetic and copies ran while one was open for 0% of the time, Pallas kernels for 17%

profile of v8, /device:TPU:0, one launch (start us, length us, event | category | flops | bytes accessed | tf_op | source)
XLA Modules:
  0.0 39.1 jit_solution(12229328061378191908)
XLA Ops:
  0.6 0.8 %pad_maximum_fusion.1 = bf16[3,2,4096]{2,1,0:T(2,128)(2,1)S(1)} fusion(bf16[1,2,4096]{2,1,0:T(2,128)(2,1)} %bitcast.17, bf16[1,2,4096]{2,1,0:T(2,128)(2,1)} %bitcast.18, bf16[1,2,4096]{2,1,0:T(2,128)(2,1)} %bitcast.19), kind=kLoop, calls=%fused_computation.2 | loop fusion | flops 49152 | bytes 98304 | tf_op jit(solution)/shard_map/stack | solution.py:133
  1.6 5.1 %collective-permute-start = (bf16[1,24,1024]{2,1,0:T(8,128)(2,1)S(1)}, bf16[1,24,1024]{2,1,0:T(8,128)(2,1)S(1)}, u32[]{:S(2)}, u32[]{:S(2)}) collective-permute-start(bf16[1,24,1024]{2,1,0:T(8,128)(2,1)S(1)} %reshape.21.refs_0_), channel_id=1, source_target_pairs={{24,0},{25,1},{26,2},{27,3},{28,4},{29,5},{30,6},{31,7},{16,8},{17... | collective-permute-start | bytes 147464 | tf_op jit(solution)/shard_map/ppermute | solution.py:52
  6.7 0.0 collective-permute-start.1
  6.7 0.6 %collective-permute-start.2 = (bf16[1,24,1024]{2,1,0:T(8,128)(2,1)S(1)}, bf16[1,24,1024]{2,1,0:T(8,128)(2,1)S(1)}, u32[]{:S(2)}, u32[]{:S(2)}) collective-permute-start(bf16[1,24,1024]{2,1,0:T(8,128)(2,1)S(1)} %reshape.21.refs_0_), channel_id=1, source_target_pairs={{8,0},{9,1},{10,2},{11,3},{12,4},{13,5},{14,6},{15,7},{0,8},{1,9},... | collective-permute-start | bytes 147464 | tf_op jit(solution)/shard_map/ppermute | solution.py:52
  7.3 1.6 %collective-permute-start.3 = (bf16[1,24,1024]{2,1,0:T(8,128)(2,1)S(1)}, bf16[1,24,1024]{2,1,0:T(8,128)(2,1)S(1)}, u32[]{:S(2)}, u32[]{:S(2)}) collective-permute-start(bf16[1,24,1024]{2,1,0:T(8,128)(2,1)S(1)} %reshape.21.refs_0_), channel_id=1, source_target_pairs={{2,0},{5,1},{0,2},{7,3},{6,4},{1,5},{4,6},{3,7},{10,8},{13,9},{8,1... | collective-permute-start | bytes 147464 | tf_op jit(solution)/shard_map/ppermute | solution.py:52
  9.0 1.5 %collective-permute-start.5 = (bf16[1,24,1024]{2,1,0:T(8,128)(2,1)S(1)}, bf16[1,24,1024]{2,1,0:T(8,128)(2,1)S(1)}, u32[]{:S(2)}, u32[]{:S(2)}) collective-permute-start(bf16[1,24,1024]{2,1,0:T(8,128)(2,1)S(1)} %reshape.21.refs_0_), channel_id=1, source_target_pairs={{4,0},{3,1},{6,2},{1,3},{0,4},{7,5},{2,6},{5,7},{12,8},{11,9},{14,... | collective-permute-start | bytes 147464 | tf_op jit(solution)/shard_map/ppermute | solution.py:52
  10.5 0.0 collective-permute-done
  10.5 1.2 %collective-permute-start.8 = (bf16[1,24,1024]{2,1,0:T(8,128)(2,1)S(1)}, bf16[1,24,1024]{2,1,0:T(8,128)(2,1)S(1)}, u32[]{:S(2)}, u32[]{:S(2)}) collective-permute-start(bf16[1,24,1024]{2,1,0:T(8,128)(2,1)S(1)} %reshape.21.refs_0_), channel_id=1, source_target_pairs={{6,0},{7,1},{4,2},{5,3},{2,4},{3,5},{0,6},{1,7},{14,8},{15,9},{12,... | collective-permute-start | bytes 147464 | tf_op jit(solution)/shard_map/ppermute | solution.py:52
  11.7 0.0 collective-permute-done.1
  11.7 0.0 collective-permute-done.2
  11.7 0.0 collective-permute-done.3.refs_2_
  11.7 1.6 %collective-permute-start.4 = (bf16[3,24,1024]{2,1,0:T(8,128)(2,1)S(1)}, bf16[3,24,1024]{2,1,0:T(8,128)(2,1)S(1)}, u32[]{:S(2)}, u32[]{:S(2)}) collective-permute-start(bf16[3,24,1024]{2,1,0:T(8,128)(2,1)S(1)} %constant_dynamic-update-slice_fusion.refs_1_), channel_id=1, source_target_pairs={{4,0},{3,1},{6,2},{1,3},{0,4},{7,5},{2,6},{5,7},{12,8},{11,9},{14,... | collective-permute-start | bytes 442376 | tf_op jit(solution)/shard_map/ppermute | solution.py:52
  13.3 0.3 collective-permute-done.5.refs_3_
  13.6 1.2 %collective-permute-start.6 = (bf16[3,24,1024]{2,1,0:T(8,128)(2,1)S(1)}, bf16[3,24,1024]{2,1,0:T(8,128)(2,1)S(1)}, u32[]{:S(2)}, u32[]{:S(2)}) collective-permute-start(bf16[3,24,1024]{2,1,0:T(8,128)(2,1)S(1)} %constant_dynamic-update-slice_fusion.refs_1_), channel_id=1, source_target_pairs={{2,0},{5,1},{0,2},{7,3},{6,4},{1,5},{4,6},{3,7},{10,8},{13,9},{8,1... | collective-permute-start | bytes 442376 | tf_op jit(solution)/shard_map/ppermute | solution.py:52
  14.8 1.3 %collective-permute-start.7 = (bf16[2,24,1024]{2,1,0:T(8,128)(2,1)S(1)}, bf16[2,24,1024]{2,1,0:T(8,128)(2,1)S(1)}, u32[]{:S(2)}, u32[]{:S(2)}) collective-permute-start(bf16[2,24,1024]{2,1,0:T(8,128)(2,1)S(1)} %pad_maximum_fusion), channel_id=1, source_target_pairs={{6,0},{7,1},{4,2},{5,3},{2,4},{3,5},{0,6},{1,7},{14,8},{15,9},{12,... | collective-permute-start | bytes 294920 | tf_op jit(solution)/shard_map/ppermute | solution.py:52
  16.1 0.0 collective-permute-done.8.refs_4_
  16.1 1.2 %collective-permute-start.9 = (bf16[1,24,1024]{2,1,0:T(8,128)(2,1)S(1)}, bf16[1,24,1024]{2,1,0:T(8,128)(2,1)S(1)}, u32[]{:S(2)}, u32[]{:S(2)}) collective-permute-start(bf16[1,24,1024]{2,1,0:T(8,128)(2,1)S(1)} %collective-permute-done.8.refs_4_), channel_id=1, source_target_pairs={{8,0},{9,1},{10,2},{11,3},{12,4},{13,5},{14,6},{15,7},{0,8},{1,9},... | collective-permute-start | bytes 147464 | tf_op jit(solution)/shard_map/ppermute | solution.py:52
  17.4 2.7 %shard_map.93 = (bf16[112,1024]{1,0:T(8,128)(2,1)S(1)}, bf16[56,1024]{1,0:T(8,128)(2,1)S(1)}, f32[2,7,8,128]{3,2,1,0:T(8,128)S(1)}, bf16[4096,128]{1,0:T(8,128)(...) custom-call(bf16[1,24,1024]{2,1,0:T(8,128)(2,1)S(1)} %reshape.21.refs_0_, ...), custom_call_target="tpu_custom_call" | custom-call | flops 293601280 | bytes 6291456 | tf_op jit(solution)/shard_map/pallas_call | solution.py:236
  20.1 0.1 collective-permute-done.9.refs_3_
  20.2 0.2 collective-permute-done.7.refs_2_
  20.4 0.0 collective-permute-done.4.refs_0_
  20.4 0.0 collective-permute-done.6.refs_1_
  20.4 0.8 %shard_map.94 = (bf16[256,1024]{1,0:T(8,128)(2,1)S(1)}, bf16[128,1024]{1,0:T(8,128)(2,1)S(1)}, f32[2,16,8,128]{3,2,1,0:T(8,128)S(1)}) custom-call(bf16[3,24,1024]{2,1,0:T(8,128)(2,1)S(1)} %collective-permute-done.4.refs_0_, bf16[3,24,1024]{2,1,0:T(8,128)(2,1)S(1)} %collective-permute-done.6.refs_1_, bf16[2,24,1024]{2,1,0:T(8,128)(2,1)S(1)} %collective-permute-done.7.refs_2_, ...), custom_call_target="tpu_custom_call" | custom-call | tf_op jit(solution)/shard_map/pallas_call | solution.py:273
  21.3 0.1 collective-permute-start.10
  21.3 1.3 %collective-permute-done.10.refs_1_ = f32[2,16,8,128]{3,2,1,0:T(8,128)S(1)} collective-permute-done((f32[2,16,8,128]{3,2,1,0:T(8,128)S(1)}, f32[2,16,8,128]{3,2,1,0:T(8,128)S(1)}, u32[]{:S(2)}, u32[]{:S(2)}) %collective-permute-start.10) | collective-permute-done | bytes 131104 | tf_op jit(solution)/shard_map/ppermute | solution.py:463
  22.7 0.9 %shard_map.95 = (bf16[256,1024]{1,0:T(8,128)(2,1)S(1)}, bf16[128,512]{1,0:T(8,128)(2,1)S(1)}, f32[4,8,1024]{2,1,0:T(8,128)S(1)}, bf16[4,8,1024]{2,1,0:T(8,128)(2...) custom-call(f32[2,16,8,128]{3,2,1,0:T(8,128)S(1)} %get-tuple-element.34.refs_0_, ...), custom_call_target="tpu_custom_call" | custom-call | tf_op jit(solution)/shard_map/pallas_call | solution.py:349
  23.6 1.5 %collective-permute-start.13 = (bf16[4,8,1024]{2,1,0:T(8,128)(2,1)S(1)}, bf16[4,8,1024]{2,1,0:T(8,128)(2,1)S(1)}, u32[]{:S(2)}, u32[]{:S(2)}) collective-permute-start(bf16[4,8,1024]{2,1,0:T(8,128)(2,1)S(1)} %get-tuple-element.38), channel_id=1, source_target_pairs={{0,6},{1,7},{2,4},{3,5},{4,2},{5,3},{6,0},{7,1},{8,14},{9,15},{10,... | collective-permute-start | bytes 196616 | tf_op jit(solution)/shard_map/ppermute | solution.py:56
  25.1 0.9 %collective-permute-start.12 = (bf16[4,8,1024]{2,1,0:T(8,128)(2,1)S(1)}, bf16[4,8,1024]{2,1,0:T(8,128)(2,1)S(1)}, u32[]{:S(2)}, u32[]{:S(2)}) collective-permute-start(bf16[4,8,1024]{2,1,0:T(8,128)(2,1)S(1)} %get-tuple-element.37), channel_id=1, source_target_pairs={{0,4},{1,3},{2,6},{3,1},{4,0},{5,7},{6,2},{7,5},{8,12},{9,11},{10,... | collective-permute-start | bytes 196616 | tf_op jit(solution)/shard_map/ppermute | solution.py:56
  26.0 1.2 %collective-permute-start.11 = (bf16[4,8,1024]{2,1,0:T(8,128)(2,1)S(1)}, bf16[4,8,1024]{2,1,0:T(8,128)(2,1)S(1)}, u32[]{:S(2)}, u32[]{:S(2)}) collective-permute-start(bf16[4,8,1024]{2,1,0:T(8,128)(2,1)S(1)} %get-tuple-element.36), channel_id=1, source_target_pairs={{0,2},{1,5},{2,0},{3,7},{4,6},{5,1},{6,4},{7,3},{8,10},{9,13},{10,... | collective-permute-start | bytes 196616 | tf_op jit(solution)/shard_map/ppermute | solution.py:56
  27.1 2.4 %shard_map.96 = (f32[4096,128]{1,0:T(8,128)}, f32[4096,128]{1,0:T(8,128)}) custom-call(bf16[256,1024]{1,0:T(8,128)(2,1)S(1)} %get-tuple-element.39.pt, bf16[256,1024]{1,0:T(8,128)(2,1)S(1)} %get-tuple-element.40.factor), custom_call_target="tpu_custom_call" | custom-call | flops 536870912 | bytes 4194304 | tf_op jit(solution)/shard_map/pallas_call | solution.py:391
  29.5 0.0 collective-permute-done.13
  29.6 0.8 %collective-permute-done.12 = bf16[4,8,1024]{2,1,0:T(8,128)(2,1)S(1)} collective-permute-done((bf16[4,8,1024]{2,1,0:T(8,128)(2,1)S(1)}, bf16[4,8,1024]{2,1,0:T(8,128)(2,1)S(1)}, u32[]{:S(2)}, u32[]{:S(2)}) %collective-permute-start.12) | collective-permute-done | bytes 65568 | tf_op jit(solution)/shard_map/ppermute | solution.py:56
  30.3 0.0 collective-permute-done.11
  30.4 3.4 %collective-permute-start.16 = (bf16[1,8,1024]{2,1,0:T(8,128)(2,1)S(1)}, bf16[1,8,1024]{2,1,0:T(8,128)(2,1)S(1)}, u32[]{:S(2)}, u32[]{:S(2)}) collective-permute-start(bf16[1,8,1024]{2,1,0:T(8,128)(2,1)S(1)} %get-tuple-element.47), channel_id=1, source_target_pairs={{0,24},{1,25},{2,26},{3,27},{4,28},{5,29},{6,30},{7,31},{8,16},{9,... | collective-permute-start | bytes 49160 | tf_op jit(solution)/shard_map/ppermute | solution.py:56
  33.8 0.0 collective-permute-start.15
  33.8 1.1 %collective-permute-start.14 = (bf16[1,8,1024]{2,1,0:T(8,128)(2,1)S(1)}, bf16[1,8,1024]{2,1,0:T(8,128)(2,1)S(1)}, u32[]{:S(2)}, u32[]{:S(2)}) collective-permute-start(bf16[1,8,1024]{2,1,0:T(8,128)(2,1)S(1)} %get-tuple-element.46), channel_id=1, source_target_pairs={{0,8},{1,9},{2,10},{3,11},{4,12},{5,13},{6,14},{7,15},{8,0},{9,1},... | collective-permute-start | bytes 49160 | tf_op jit(solution)/shard_map/ppermute | solution.py:56
  34.8 1.6 %shard_map.97 = f32[128,4096]{1,0:T(8,128)} custom-call(bf16[128,1024]{1,0:T(8,128)(2,1)S(1)} %get-tuple-element.44.cot, bf16[128,512]{1,0:T(8,128)(2,1)S(1)} %get-tuple-element.45.tact), custom_call_target="tpu_custom_call" | custom-call | flops 134217728 | bytes 2097152 | tf_op jit(solution)/shard_map/pallas_call | solution.py:431
  36.5 0.0 collective-permute-done.16
  36.5 1.9 %collective-permute-done.15 = bf16[1,8,1024]{2,1,0:T(8,128)(2,1)S(1)} collective-permute-done((bf16[1,8,1024]{2,1,0:T(8,128)(2,1)S(1)}, bf16[1,8,1024]{2,1,0:T(8,128)(2,1)S(1)}, u32[]{:S(2)}, u32[]{:S(2)}) %collective-permute-start.15) | collective-permute-done | bytes 16416 | tf_op jit(solution)/shard_map/ppermute | solution.py:56
  38.4 0.0 collective-permute-done.14
  38.5 0.6 %reshape.22 = bf16[2,4096]{1,0:T(2,128)(2,1)} reshape(bf16[2,8,4,128]{3,2,1,0:T(4,128)(2,1)S(1)} %copy.11) | data formatting | bytes 32768 | tf_op jit(solution)/shard_map/reshape | solution.py:142
  (13 shorter events, 0.2 us)
Async XLA Ops:
  1.6 8.9 %collective-permute-start = (bf16[1,24,1024]{2,1,0:T(8,128)(2,1)S(1)}, bf16[1,24,1024]{2,1,0:T(8,128)(2,1)S(1)}, u32[]{:S(2)}, u32[]{:S(2)}) collective-permute-start(bf16[1,24,1024]{2,1,0:T(8,128)(2,1)S(1)} %reshape.21.refs_0_), channel_id=1, source_target_pairs={{24,0},{25,1},{26,2},{27,3},{28,4},{29,5},{30,6},{31,7},{16,8},{17... | collective-permute-start | bytes 147464 | tf_op jit(solution)/shard_map/ppermute | solution.py:52
  6.7 5.0 %collective-permute-start.1 = (bf16[1,24,1024]{2,1,0:T(8,128)(2,1)S(1)}, bf16[1,24,1024]{2,1,0:T(8,128)(2,1)S(1)}, u32[]{:S(2)}, u32[]{:S(2)}) collective-permute-start(bf16[1,24,1024]{2,1,0:T(8,128)(2,1)S(1)} %reshape.21.refs_0_), channel_id=1, source_target_pairs={{16,0},{17,1},{18,2},{19,3},{20,4},{21,5},{22,6},{23,7},{24,8},{25... | collective-permute-start | bytes 147464 | tf_op jit(solution)/shard_map/ppermute | solution.py:52
  6.7 5.0 %collective-permute-start.2 = (bf16[1,24,1024]{2,1,0:T(8,128)(2,1)S(1)}, bf16[1,24,1024]{2,1,0:T(8,128)(2,1)S(1)}, u32[]{:S(2)}, u32[]{:S(2)}) collective-permute-start(bf16[1,24,1024]{2,1,0:T(8,128)(2,1)S(1)} %reshape.21.refs_0_), channel_id=1, source_target_pairs={{8,0},{9,1},{10,2},{11,3},{12,4},{13,5},{14,6},{15,7},{0,8},{1,9},... | collective-permute-start | bytes 147464 | tf_op jit(solution)/shard_map/ppermute | solution.py:52
  7.3 4.4 %collective-permute-start.3 = (bf16[1,24,1024]{2,1,0:T(8,128)(2,1)S(1)}, bf16[1,24,1024]{2,1,0:T(8,128)(2,1)S(1)}, u32[]{:S(2)}, u32[]{:S(2)}) collective-permute-start(bf16[1,24,1024]{2,1,0:T(8,128)(2,1)S(1)} %reshape.21.refs_0_), channel_id=1, source_target_pairs={{2,0},{5,1},{0,2},{7,3},{6,4},{1,5},{4,6},{3,7},{10,8},{13,9},{8,1... | collective-permute-start | bytes 147464 | tf_op jit(solution)/shard_map/ppermute | solution.py:52
  9.0 4.6 %collective-permute-start.5 = (bf16[1,24,1024]{2,1,0:T(8,128)(2,1)S(1)}, bf16[1,24,1024]{2,1,0:T(8,128)(2,1)S(1)}, u32[]{:S(2)}, u32[]{:S(2)}) collective-permute-start(bf16[1,24,1024]{2,1,0:T(8,128)(2,1)S(1)} %reshape.21.refs_0_), channel_id=1, source_target_pairs={{4,0},{3,1},{6,2},{1,3},{0,4},{7,5},{2,6},{5,7},{12,8},{11,9},{14,... | collective-permute-start | bytes 147464 | tf_op jit(solution)/shard_map/ppermute | solution.py:52
  10.5 5.6 %collective-permute-start.8 = (bf16[1,24,1024]{2,1,0:T(8,128)(2,1)S(1)}, bf16[1,24,1024]{2,1,0:T(8,128)(2,1)S(1)}, u32[]{:S(2)}, u32[]{:S(2)}) collective-permute-start(bf16[1,24,1024]{2,1,0:T(8,128)(2,1)S(1)} %reshape.21.refs_0_), channel_id=1, source_target_pairs={{6,0},{7,1},{4,2},{5,3},{2,4},{3,5},{0,6},{1,7},{14,8},{15,9},{12,... | collective-permute-start | bytes 147464 | tf_op jit(solution)/shard_map/ppermute | solution.py:52
  11.7 8.7 %collective-permute-start.4 = (bf16[3,24,1024]{2,1,0:T(8,128)(2,1)S(1)}, bf16[3,24,1024]{2,1,0:T(8,128)(2,1)S(1)}, u32[]{:S(2)}, u32[]{:S(2)}) collective-permute-start(bf16[3,24,1024]{2,1,0:T(8,128)(2,1)S(1)} %constant_dynamic-update-slice_fusion.refs_1_), channel_id=1, source_target_pairs={{4,0},{3,1},{6,2},{1,3},{0,4},{7,5},{2,6},{5,7},{12,8},{11,9},{14,... | collective-permute-start | bytes 442376 | tf_op jit(solution)/shard_map/ppermute | solution.py:52
  13.6 6.8 %collective-permute-start.6 = (bf16[3,24,1024]{2,1,0:T(8,128)(2,1)S(1)}, bf16[3,24,1024]{2,1,0:T(8,128)(2,1)S(1)}, u32[]{:S(2)}, u32[]{:S(2)}) collective-permute-start(bf16[3,24,1024]{2,1,0:T(8,128)(2,1)S(1)} %constant_dynamic-update-slice_fusion.refs_1_), channel_id=1, source_target_pairs={{2,0},{5,1},{0,2},{7,3},{6,4},{1,5},{4,6},{3,7},{10,8},{13,9},{8,1... | collective-permute-start | bytes 442376 | tf_op jit(solution)/shard_map/ppermute | solution.py:52
  14.8 5.6 %collective-permute-start.7 = (bf16[2,24,1024]{2,1,0:T(8,128)(2,1)S(1)}, bf16[2,24,1024]{2,1,0:T(8,128)(2,1)S(1)}, u32[]{:S(2)}, u32[]{:S(2)}) collective-permute-start(bf16[2,24,1024]{2,1,0:T(8,128)(2,1)S(1)} %pad_maximum_fusion), channel_id=1, source_target_pairs={{6,0},{7,1},{4,2},{5,3},{2,4},{3,5},{0,6},{1,7},{14,8},{15,9},{12,... | collective-permute-start | bytes 294920 | tf_op jit(solution)/shard_map/ppermute | solution.py:52
  16.1 4.1 %collective-permute-start.9 = (bf16[1,24,1024]{2,1,0:T(8,128)(2,1)S(1)}, bf16[1,24,1024]{2,1,0:T(8,128)(2,1)S(1)}, u32[]{:S(2)}, u32[]{:S(2)}) collective-permute-start(bf16[1,24,1024]{2,1,0:T(8,128)(2,1)S(1)} %collective-permute-done.8.refs_4_), channel_id=1, source_target_pairs={{8,0},{9,1},{10,2},{11,3},{12,4},{13,5},{14,6},{15,7},{0,8},{1,9},... | collective-permute-start | bytes 147464 | tf_op jit(solution)/shard_map/ppermute | solution.py:52
  21.3 1.4 %collective-permute-start.10 = (f32[2,16,8,128]{3,2,1,0:T(8,128)S(1)}, f32[2,16,8,128]{3,2,1,0:T(8,128)S(1)}, u32[]{:S(2)}, u32[]{:S(2)}) collective-permute-start(f32[2,16,8,128]{3,2,1,0:T(8,128)S(1)} %get-tuple-element.34.refs_0_), channel_id=1, source_target_pairs={{0,1},{1,0},{2,3},{3,2},{4,5},{5,4},{6,7},{7,6},{8,9},{9,8},{10,11... | collective-permute-start | bytes 393224 | tf_op jit(solution)/shard_map/ppermute | solution.py:463
  23.6 6.0 %collective-permute-start.13 = (bf16[4,8,1024]{2,1,0:T(8,128)(2,1)S(1)}, bf16[4,8,1024]{2,1,0:T(8,128)(2,1)S(1)}, u32[]{:S(2)}, u32[]{:S(2)}) collective-permute-start(bf16[4,8,1024]{2,1,0:T(8,128)(2,1)S(1)} %get-tuple-element.38), channel_id=1, source_target_pairs={{0,6},{1,7},{2,4},{3,5},{4,2},{5,3},{6,0},{7,1},{8,14},{9,15},{10,... | collective-permute-start | bytes 196616 | tf_op jit(solution)/shard_map/ppermute | solution.py:56
  25.1 5.2 %collective-permute-start.12 = (bf16[4,8,1024]{2,1,0:T(8,128)(2,1)S(1)}, bf16[4,8,1024]{2,1,0:T(8,128)(2,1)S(1)}, u32[]{:S(2)}, u32[]{:S(2)}) collective-permute-start(bf16[4,8,1024]{2,1,0:T(8,128)(2,1)S(1)} %get-tuple-element.37), channel_id=1, source_target_pairs={{0,4},{1,3},{2,6},{3,1},{4,0},{5,7},{6,2},{7,5},{8,12},{9,11},{10,... | collective-permute-start | bytes 196616 | tf_op jit(solution)/shard_map/ppermute | solution.py:56
  26.0 4.4 %collective-permute-start.11 = (bf16[4,8,1024]{2,1,0:T(8,128)(2,1)S(1)}, bf16[4,8,1024]{2,1,0:T(8,128)(2,1)S(1)}, u32[]{:S(2)}, u32[]{:S(2)}) collective-permute-start(bf16[4,8,1024]{2,1,0:T(8,128)(2,1)S(1)} %get-tuple-element.36), channel_id=1, source_target_pairs={{0,2},{1,5},{2,0},{3,7},{4,6},{5,1},{6,4},{7,3},{8,10},{9,13},{10,... | collective-permute-start | bytes 196616 | tf_op jit(solution)/shard_map/ppermute | solution.py:56
  30.4 6.1 %collective-permute-start.16 = (bf16[1,8,1024]{2,1,0:T(8,128)(2,1)S(1)}, bf16[1,8,1024]{2,1,0:T(8,128)(2,1)S(1)}, u32[]{:S(2)}, u32[]{:S(2)}) collective-permute-start(bf16[1,8,1024]{2,1,0:T(8,128)(2,1)S(1)} %get-tuple-element.47), channel_id=1, source_target_pairs={{0,24},{1,25},{2,26},{3,27},{4,28},{5,29},{6,30},{7,31},{8,16},{9,... | collective-permute-start | bytes 49160 | tf_op jit(solution)/shard_map/ppermute | solution.py:56
  33.8 4.6 %collective-permute-start.15 = (bf16[1,8,1024]{2,1,0:T(8,128)(2,1)S(1)}, bf16[1,8,1024]{2,1,0:T(8,128)(2,1)S(1)}, u32[]{:S(2)}, u32[]{:S(2)}) collective-permute-start(bf16[1,8,1024]{2,1,0:T(8,128)(2,1)S(1)} %get-tuple-element.48), channel_id=1, source_target_pairs={{0,16},{1,17},{2,18},{3,19},{4,20},{5,21},{6,22},{7,23},{8,24},{9,... | collective-permute-start | bytes 49160 | tf_op jit(solution)/shard_map/ppermute | solution.py:56
  33.8 4.6 %collective-permute-start.14 = (bf16[1,8,1024]{2,1,0:T(8,128)(2,1)S(1)}, bf16[1,8,1024]{2,1,0:T(8,128)(2,1)S(1)}, u32[]{:S(2)}, u32[]{:S(2)}) collective-permute-start(bf16[1,8,1024]{2,1,0:T(8,128)(2,1)S(1)} %get-tuple-element.46), channel_id=1, source_target_pairs={{0,8},{1,9},{2,10},{3,11},{4,12},{5,13},{6,14},{7,15},{8,0},{9,1},... | collective-permute-start | bytes 49160 | tf_op jit(solution)/shard_map/ppermute | solution.py:56
